TPU v7x, 32 devices: a whole 2x2x4 slice. The times are simulated.
32 devices in a mesh: dp: 4 (over y, x), tensor: 8 (over z, core).
Axes of the slice: x: 2, y: 2, z: 4, core: 2. Of those that a mesh axis runs over, the one named last changes fastest.
Arguments:
- inputs: bfloat16 [512, 6144], P('dp'), may hold values from -6 to 6
- targets: bfloat16 [512, 6144], P('dp'), may hold values from -6 to 6
- lengths: int32 [4], P('dp'), may hold values from 1 to 128, 384 in all
- ln_gain: float32 [6144], replicated, may hold values from 0.5 to 1.5
- ln_bias: float32 [6144], replicated, may hold values from -0.8 to 0.8
- query_weight: bfloat16 [6144, 3072], P(None, 'tensor'), may hold values from -0.078125 to 0.078125
- w_key: bfloat16 [6144, 3072], P(None, 'tensor'), may hold values from -0.078125 to 0.078125
- value_weight: bfloat16 [6144, 3072], P(None, 'tensor'), may hold values from -0.078125 to 0.078125
- w_out: bfloat16 [3072, 6144], P('tensor'), may hold values from -0.109375 to 0.109375
- down_query: bfloat16 [6144, 16], replicated, may hold values from -0.078125 to 0.078125
- down_value: bfloat16 [6144, 16], replicated, may hold values from -0.078125 to 0.078125
- query_up_factor: float32 [16, 3072], P(None, 'tensor'), may hold values from -0.6 to 0.6
- value_up_factor: float32 [16, 3072], P(None, 'tensor'), may hold values from -0.6 to 0.6
Outputs:
- step_query: float32 [16, 3072], P(None, 'tensor')
- step_value: float32 [16, 3072], P(None, 'tensor')
- remain_query: float32 [16, 3072], P(None, 'tensor')
- remain_value: float32 [16, 3072], P(None, 'tensor')
Inputs may be any that keep to these rules, and one draw needn't show every extreme that they name: `lengths`: live tokens of each sequence; one sequence has exactly 128.
All inputs are finite; a program needn't handle non-finite values. No bound on the sum of `lengths` on one device may be relied on, other than what follows from the above.
Results may differ from a plain program's by a relative error of at most 0.035.
Values sent between devices are 32-bit elements; how exact they have to be, the bound alone decides.
No kernel may reach another device: no remote copies, remote signals or barrier semaphores. Data moves between devices by JAX's collectives and lax.ppermute only.
A program may use at most 128 MiB of HBM per device.

v0:
```python
import jax
import jax.numpy as jnp
from jax import lax
from jax.sharding import PartitionSpec as P

HEAD_DIM = 128
CG_STEPS = 3


EPS = 1e-05
ADAPTER_SCALE = 2.0
DAMP = 0.05
NEG = -1e30


def layer_norm(rows, gain, bias):
    rows = rows.astype(jnp.float32)
    centred = rows - jnp.mean(rows, axis=-1, keepdims=True)
    spread = jnp.mean(centred * centred, axis=-1, keepdims=True)
    return (centred * lax.rsqrt(spread + EPS) * gain + bias).astype(jnp.bfloat16)


def attend(
    ups, normalized_input, query_weight, w_key, value_weight, w_out, down_query, down_value, live
):
    query_up_factor, value_up_factor = ups
    length = normalized_input.shape[0]
    heads = query_weight.shape[1] // HEAD_DIM
    query_down_factor = jnp.dot(normalized_input, down_query, preferred_element_type=jnp.float32)
    value_down_factor = jnp.dot(normalized_input, down_value, preferred_element_type=jnp.float32)
    query_rows = jnp.dot(
        normalized_input, query_weight, preferred_element_type=jnp.float32
    ) + ADAPTER_SCALE * jnp.dot(query_down_factor, query_up_factor, precision=lax.Precision.HIGHEST)
    value_rows = jnp.dot(
        normalized_input, value_weight, preferred_element_type=jnp.float32
    ) + ADAPTER_SCALE * jnp.dot(value_down_factor, value_up_factor, precision=lax.Precision.HIGHEST)
    keys = jnp.dot(normalized_input, w_key, preferred_element_type=jnp.float32)
    query_rows = query_rows.astype(jnp.bfloat16).reshape(length, heads, HEAD_DIM)
    value_rows = value_rows.astype(jnp.bfloat16).reshape(length, heads, HEAD_DIM)
    keys = keys.astype(jnp.bfloat16).reshape(length, heads, HEAD_DIM)
    scores = jnp.einsum(
        "qhd,khd->hqk", query_rows, keys, preferred_element_type=jnp.float32
    ) * HEAD_DIM ** (-0.5)
    scores = jnp.where(live[None], scores, NEG)
    top = lax.stop_gradient(jnp.max(scores, axis=-1, keepdims=True))
    weights = jnp.exp(scores - top)
    probs = (weights / jnp.sum(weights, axis=-1, keepdims=True)).astype(jnp.bfloat16)
    mixed = jnp.einsum("hqk,khd->qhd", probs, value_rows, preferred_element_type=jnp.float32)
    mixed = mixed.astype(jnp.bfloat16).reshape(length, heads * HEAD_DIM)
    return jnp.dot(mixed, w_out, preferred_element_type=jnp.float32)


def linear_parts(apply, ups):
    output, pullback = jax.vjp(apply, ups)

    def backward(cotan):
        return pullback(cotan)[0]

    def forward(vector):
        _, undo = jax.vjp(backward, jnp.zeros_like(output))
        return undo(vector)[0]

    return (output, forward, backward)


def local_dot(first, second):
    return jnp.sum(first[0] * second[0]) + jnp.sum(first[1] * second[1])


def head_total(partial_value, offset, row_live):
    position = lax.axis_index("tensor")
    share = lax.psum_scatter(partial_value, "tensor", scatter_dimension=0, tiled=True)
    rows = share.shape[0]
    live_share = lax.dynamic_slice_in_dim(row_live, position * rows, rows, 0)
    if offset is not None:
        share = share + lax.dynamic_slice_in_dim(offset, position * rows, rows, 0)
    sent = live_share[:, None] * share
    return lax.all_gather(sent, "tensor", axis=0, tiled=True)


def on_device(
    inputs,
    targets,
    lengths,
    ln_gain,
    ln_bias,
    query_weight,
    w_key,
    value_weight,
    w_out,
    down_query,
    down_value,
    query_up_factor,
    value_up_factor,
):
    length = inputs.shape[0]
    places = jnp.arange(length, dtype=jnp.int32)
    limit = lengths[0]
    live = (places[None, :] <= places[:, None]) & (places[None, :] < limit)
    row_live = (places < limit).astype(jnp.float32)
    normalized_input = layer_norm(inputs, ln_gain, ln_bias)
    ups = (query_up_factor, value_up_factor)

    def apply(weights):
        return attend(
            weights,
            normalized_input,
            query_weight,
            w_key,
            value_weight,
            w_out,
            down_query,
            down_value,
            live,
        )

    output, linear, backward = linear_parts(apply, ups)
    token_count = length * lax.axis_size("dp")
    gap = inputs.astype(jnp.float32) - targets.astype(jnp.float32)

    def pulled(shared):
        return backward(shared / token_count)

    def data_sum(part):
        return lax.psum((part[0], part[1]), "dp")

    def squared(vector):
        return lax.psum(local_dot(vector, vector), "tensor")

    grads = data_sum(pulled(head_total(output, gap, row_live)))
    newton = (jnp.zeros_like(query_up_factor), jnp.zeros_like(value_up_factor))
    remain = (-grads[0], -grads[1])
    direction = remain
    norm_now = squared(remain)
    for index in range(CG_STEPS):
        part = pulled(head_total(linear(direction), None, row_live))
        summed = data_sum(part)
        image = (summed[0] + DAMP * direction[0], summed[1] + DAMP * direction[1])
        curv = lax.psum(local_dot(direction, image), "tensor")
        alpha = norm_now / curv
        newton = (newton[0] + alpha * direction[0], newton[1] + alpha * direction[1])
        remain = (remain[0] - alpha * image[0], remain[1] - alpha * image[1])
        norm_next = squared(remain)
        ratio = norm_next / norm_now
        direction = (remain[0] + ratio * direction[0], remain[1] + ratio * direction[1])
        norm_now = norm_next
    return (newton[0], newton[1], remain[0], remain[1])


def solution(mesh):
    in_specs = (
        P("dp", None),
        P("dp", None),
        P("dp"),
        P(),
        P(),
        P(None, "tensor"),
        P(None, "tensor"),
        P(None, "tensor"),
        P("tensor", None),
        P(),
        P(),
        P(None, "tensor"),
        P(None, "tensor"),
    )
    out_specs = (P(None, "tensor"), P(None, "tensor"), P(None, "tensor"), P(None, "tensor"))
    return jax.shard_map(
        on_device, mesh=mesh, in_specs=in_specs, out_specs=out_specs, check_vma=False
    )
```

profile of v0, /device:TPU:0, one launch (start us, length us, event | category | flops | bytes accessed | tf_op | source)
XLA Modules:
  0.0 563.6 jit_solution(6570640541697365108)
XLA Ops:
  7.3 1.8 convert_reduce_fusion
  9.1 2.1 multiply_reduce_fusion
  11.3 0.7 add_convert_fusion
  12.5 1.1 fusion.152
  13.9 0.7 copy.64
  14.7 3.3 convolution_convert_fusion
  19.5 1.1 fusion.20
  21.3 0.7 fusion.145
  22.0 1.4 fusion.151
  23.5 3.3 fusion.150
  27.3 0.7 divide_convert_fusion
  28.2 5.1 fusion.153
  33.4 2.0 convert_element_type.200
  35.4 41.1 %reduce-scatter.5.cloned.1.call-done = f32[16,6144]{1,0:T(8,128)} async-done(((f32[128,6144]{1,0:T(8,128)}), f32[16,6144]{1,0:T(8,128)}) %reduce-scatter.5.cloned.1.call-update) | async-done | bytes 393232 | tf_op jit(solution)/shard_map/reduce_scatter | solution.py:72
  76.5 2.0 fusion.72
  78.6 37.4 %all-gather.5.cloned.1.call-done = f32[128,6144]{1,0:T(8,128)} async-done(((f32[16,6144]{1,0:T(8,128)}), f32[128,6144]{1,0:T(8,128)}) %all-gather.5.cloned.1.call-update) | async-done | bytes 3145744 | tf_op jit(solution)/shard_map/all_gather | solution.py:78
  116.0 4.8 fusion.29
  121.9 1.2 fusion.69
  123.4 16.7 %all-reduce.4 = (f32[16,384]{1,0:T(8,128)S(1)}, f32[16,384]{1,0:T(8,128)S(1)}) all-reduce(f32[16,384]{1,0:T(8,128)S(1)} %fusion.154, f32[16,384]{1,0:T(8,128)S(1)} %fusion.155), channel_id=1, replica_groups=mesh['dp'=4,'tensor'=8] {'dp'}, use_global_device_ids=true, to_apply=%region_6.7 | all-reduce | flops 12288 | bytes 98304 | tf_op jit(solution)/shard_map/psum | solution.py:125
  141.5 1.3 fusion.26
  142.8 5.0 fusion.157
  147.9 37.5 %reduce-scatter.7.cloned.1.call-done = f32[16,6144]{1,0:T(8,128)} async-done(((f32[128,6144]{1,0:T(8,128)}), f32[16,6144]{1,0:T(8,128)}) %reduce-scatter.7.cloned.1.call-update) | async-done | bytes 393232 | tf_op jit(solution)/shard_map/reduce_scatter | solution.py:72
  185.4 1.8 broadcast_multiply_fusion.2
  187.5 37.3 %all-gather.7.cloned.1.call-done = f32[128,6144]{1,0:T(8,128)} async-done(((f32[16,6144]{1,0:T(8,128)}), f32[128,6144]{1,0:T(8,128)}) %all-gather.7.cloned.1.call-update) | async-done | bytes 3145744 | tf_op jit(solution)/shard_map/all_gather | solution.py:78
  224.8 4.8 fusion.32
  230.6 1.3 fusion.63
  232.2 16.7 %all-reduce.3 = (f32[16,384]{1,0:T(8,128)S(1)}, f32[16,384]{1,0:T(8,128)S(1)}) all-reduce(f32[16,384]{1,0:T(8,128)S(1)} %fusion.158, f32[16,384]{1,0:T(8,128)S(1)} %fusion.159), channel_id=1, replica_groups=mesh['dp'=4,'tensor'=8] {'dp'}, use_global_device_ids=true, to_apply=%region_14.15 | all-reduce | flops 12288 | bytes 98304 | tf_op jit(solution)/shard_map/psum | solution.py:125
  252.7 14.1 %all-reduce = (f32[]{:T(128)}, f32[]{:T(128)}) all-reduce(f32[]{:T(128)S(6)} %add.139, f32[]{:T(128)S(6)} %add.142), channel_id=1, replica_groups=mesh['dp'=4,'tensor'=8] {'tensor'}, use_global_device_ids=true, to_apply=%region_10.11 | all-reduce | flops 2 | bytes 16 | tf_op jit(solution)/shard_map/psum | solution.py:128
  270.6 14.1 %psum.104 = f32[]{:T(128)} all-reduce(f32[]{:T(128)S(6)} %add.143), channel_id=1, replica_groups=mesh['dp'=4,'tensor'=8] {'tensor'}, use_global_device_ids=true, to_apply=%region_21.22 | all-reduce | flops 1 | bytes 8 | tf_op jit(solution)/shard_map/psum | solution.py:128
  287.5 1.3 fusion.27
  288.8 5.0 fusion.161
  293.9 36.8 %reduce-scatter.9.cloned.1.call-done = f32[16,6144]{1,0:T(8,128)} async-done(((f32[128,6144]{1,0:T(8,128)}), f32[16,6144]{1,0:T(8,128)}) %reduce-scatter.9.cloned.1.call-update) | async-done | bytes 393232 | tf_op jit(solution)/shard_map/reduce_scatter | solution.py:72
  330.7 1.8 broadcast_multiply_fusion.1
  332.6 37.5 %all-gather.9.cloned.1.call-done = f32[128,6144]{1,0:T(8,128)} async-done(((f32[16,6144]{1,0:T(8,128)}), f32[128,6144]{1,0:T(8,128)}) %all-gather.9.cloned.1.call-update) | async-done | bytes 3145744 | tf_op jit(solution)/shard_map/all_gather | solution.py:78
  370.1 4.8 fusion.35
  375.9 1.3 fusion.57
  377.5 16.7 %all-reduce.2 = (f32[16,384]{1,0:T(8,128)S(1)}, f32[16,384]{1,0:T(8,128)S(1)}) all-reduce(f32[16,384]{1,0:T(8,128)S(1)} %fusion.162, f32[16,384]{1,0:T(8,128)S(1)} %fusion.163), channel_id=1, replica_groups=mesh['dp'=4,'tensor'=8] {'dp'}, use_global_device_ids=true, to_apply=%region_25.26 | all-reduce | flops 12288 | bytes 98304 | tf_op jit(solution)/shard_map/psum | solution.py:125
  396.7 14.1 %psum.107 = f32[]{:T(128)} all-reduce(f32[]{:T(128)S(6)} %add.148), channel_id=1, replica_groups=mesh['dp'=4,'tensor'=8] {'tensor'}, use_global_device_ids=true, to_apply=%region_29.30 | all-reduce | flops 1 | bytes 8 | tf_op jit(solution)/shard_map/psum | solution.py:139
  414.6 14.1 %psum.108 = f32[]{:T(128)} all-reduce(f32[]{:T(128)S(6)} %add.150), channel_id=1, replica_groups=mesh['dp'=4,'tensor'=8] {'tensor'}, use_global_device_ids=true, to_apply=%region_32.33 | all-reduce | flops 1 | bytes 8 | tf_op jit(solution)/shard_map/psum | solution.py:128
  431.5 1.3 fusion.28
  432.8 5.0 fusion.165
  437.9 36.8 %reduce-scatter.11.cloned.1.call-done = f32[16,6144]{1,0:T(8,128)} async-done(((f32[128,6144]{1,0:T(8,128)}), f32[16,6144]{1,0:T(8,128)}) %reduce-scatter.11.cloned.1.call-update) | async-done | bytes 393232 | tf_op jit(solution)/shard_map/reduce_scatter | solution.py:72
  474.7 1.8 broadcast_multiply_fusion
  476.5 37.5 %all-gather.11.cloned.1.call-done = f32[128,6144]{1,0:T(8,128)} async-done(((f32[16,6144]{1,0:T(8,128)}), f32[128,6144]{1,0:T(8,128)}) %all-gather.11.cloned.1.call-update) | async-done | bytes 3145744 | tf_op jit(solution)/shard_map/all_gather | solution.py:78
  514.1 4.8 fusion.38
  519.9 1.3 fusion.51
  521.5 16.7 %all-reduce.1 = (f32[16,384]{1,0:T(8,128)S(1)}, f32[16,384]{1,0:T(8,128)S(1)}) all-reduce(f32[16,384]{1,0:T(8,128)S(1)} %fusion.166, f32[16,384]{1,0:T(8,128)S(1)} %fusion.167), channel_id=1, replica_groups=mesh['dp'=4,'tensor'=8] {'dp'}, use_global_device_ids=true, to_apply=%region_36.37 | all-reduce | flops 12288 | bytes 98304 | tf_op jit(solution)/shard_map/psum | solution.py:125
  540.7 14.1 %psum.111 = f32[]{:T(128)} all-reduce(f32[]{:T(128)S(6)} %add.155), channel_id=1, replica_groups=mesh['dp'=4,'tensor'=8] {'tensor'}, use_global_device_ids=true, to_apply=%region_40.41 | all-reduce | flops 1 | bytes 8 | tf_op jit(solution)/shard_map/psum | solution.py:139
  (117 shorter events, 20.0 us)
Async XLA Ops:
  7.2 4.8 copy-start
  7.2 4.1 copy-start.1
  7.2 4.0 copy-start.9
  7.2 4.0 copy-start.8
  7.2 69.3 %reduce-scatter.5.cloned.1.call-start = ((), (), s32[]{:S(2)}) async-start(), calls=%async_computation.4 | async-start | bytes 3538944 | tf_op jit(solution)/shard_map/reduce_scatter | solution.py:72
  9.1 3.4 copy-start.2
  12.5 1.1 copy-start.10
  18.1 0.8 copy-start.3
  18.9 0.6 copy-start.6
  20.6 0.7 copy-start.5
  23.5 3.4 copy-start.11
  33.3 82.7 %all-gather.5.cloned.1.call-start = ((), (), s32[]{:S(2)}) async-start(), calls=%async_computation.5 | async-start | bytes 3538944 | tf_op jit(solution)/shard_map/all_gather | solution.py:78
  33.3 45.2 %copy-start.12 = (f32[3,128]{1,0:T(4,128)S(1)}, f32[3,128]{1,0:T(4,128)}, u32[]{:S(2)}) copy-start(f32[3,128]{1,0:T(4,128)} %get-tuple-element.26) | copy-start | bytes 4612
  78.5 106.9 %reduce-scatter.7.cloned.1.call-start = ((), (), s32[]{:S(2)}) async-start(), calls=%async_computation.6 | async-start | bytes 3538944 | tf_op jit(solution)/shard_map/reduce_scatter | solution.py:72
  78.6 43.2 %copy-start.4 = (bf16[128,384]{0,1:T(8,128)(2,1)S(1)}, bf16[128,384]{0,1:T(8,128)(2,1)}, u32[]{:S(2)}) copy-start(bf16[128,384]{0,1:T(8,128)(2,1)} %copy-done.3) | copy-start | bytes 294916
  78.6 43.2 %copy-start.7 = (pred[128,128]{0,1:T(8,128)(4,1)S(1)}, pred[128,128]{0,1:T(8,128)(4,1)}, u32[]{:S(2)}) copy-start(pred[128,128]{0,1:T(8,128)(4,1)} %copy-done.6) | copy-start | bytes 49156
  147.8 76.9 %all-gather.7.cloned.1.call-start = ((), (), s32[]{:S(2)}) async-start(), calls=%async_computation.7 | async-start | bytes 3538944 | tf_op jit(solution)/shard_map/all_gather | solution.py:78
  187.2 143.5 %reduce-scatter.9.cloned.1.call-start = ((), (), s32[]{:S(2)}) async-start(), calls=%async_computation.8 | async-start | bytes 3538944 | tf_op jit(solution)/shard_map/reduce_scatter | solution.py:72
  293.8 76.2 %all-gather.9.cloned.1.call-start = ((), (), s32[]{:S(2)}) async-start(), calls=%async_computation.9 | async-start | bytes 3538944 | tf_op jit(solution)/shard_map/all_gather | solution.py:78
  332.6 142.1 %reduce-scatter.11.cloned.1.call-start = ((), (), s32[]{:S(2)}) async-start(), calls=%async_computation.10 | async-start | bytes 3538944 | tf_op jit(solution)/shard_map/reduce_scatter | solution.py:72
  437.8 76.2 %all-gather.11.cloned.1.call-start = ((), (), s32[]{:S(2)}) async-start(), calls=%async_computation.11 | async-start | bytes 3538944 | tf_op jit(solution)/shard_map/all_gather | solution.py:78
Sparse Core Ops, SparseCore 0:
  33.4 43.0 reduce-scatter.4
  78.6 37.2 all-gather.4
  148.0 37.3 reduce-scatter.6
  187.4 37.3 all-gather.6
  294.0 36.6 reduce-scatter.8
  332.7 37.3 all-gather.8
  437.9 36.6 reduce-scatter.10
  476.7 37.3 all-gather.10
where the time goes:
time: 565 us; the launch traced here: 564 us
  waiting for transfers between devices  302 us (53%)
  blocking collectives  137 us (24%)
  matrix products  67.5 us (12%)
  between operations  29.8 us (5%)
  other arithmetic  22.4 us (4%)
    reduce_scatter x4, waiting for transfers between devices, head_total(): lax.psum_scatter(partial_value, 'tensor', scatter_dimension=0, tiled=True)  152 us
    all_gather x4, waiting for transfers between devices, head_total(): return lax.all_gather(sent, 'tensor', axis=0, tiled=True)  150 us
    psum x4, blocking collectives, data_sum(): return lax.psum((part[0], part[1]), 'dp')  66.7 us
    psum x3, blocking collectives, squared(): return lax.psum(local_dot(vector, vector), 'tensor')  42.3 us
    dot_general x8, matrix products, attend(): return jnp.dot(mixed, w_out, preferred_element_type=jnp.float32)  39.3 us
    psum x2, blocking collectives, on_device(): curv = lax.psum(local_dot(direction, image), 'tensor')  28.2 us
  transfers between devices with their start and end apart: 8, of which 8 were waited for; matrix products, arithmetic and copies ran while one was open for 0% of the time, Pallas kernels for 0%

commit v1 on v0

v1 whole, which is shorter than its diff:
```python
import functools

import jax
import jax.numpy as jnp
from jax import lax
from jax.experimental import pallas as pl
from jax.experimental.pallas import tpu as pltpu
from jax.sharding import Mesh
from jax.sharding import PartitionSpec as P

HEAD_DIM = 128
CG_STEPS = 3
COLUMNS = 512
DEPTH = 512

EPS = 1e-05
ADAPTER_SCALE = 2.0
DAMP = 0.05
NEG = -1e30
F32 = jnp.float32
BF16 = jnp.bfloat16
HIGH = lax.Precision.HIGHEST
SCALE = HEAD_DIM ** (-0.5)
VMEM = pl.BlockSpec(memory_space=pltpu.VMEM)
SMEM = pl.BlockSpec(memory_space=pltpu.SMEM)
LIMIT = 32 * 1024 * 1024


def dot32(first, second):
    return jnp.dot(first, second, preferred_element_type=F32)


def dot_nt(first, second):
    return lax.dot_general(
        first, second, (((1,), (1,)), ((), ())), preferred_element_type=F32
    )


def dot_tn(first, second):
    return lax.dot_general(
        first, second, (((0,), (0,)), ((), ())), preferred_element_type=F32
    )


def high(first, second):
    return jnp.dot(first, second, precision=HIGH, preferred_element_type=F32)


def head(index):
    return slice(index * HEAD_DIM, (index + 1) * HEAD_DIM)


def rows_below(limit, length, width):
    return lax.broadcasted_iota(jnp.int32, (length, width), 0) < limit


def live_pairs(limit, length):
    row = lax.broadcasted_iota(jnp.int32, (length, length), 0)
    column = lax.broadcasted_iota(jnp.int32, (length, length), 1)
    return (column <= row) & (column < limit)


def project_kernel(
    limit_ref, x_ref, gain_ref, bias_ref, wq_ref, wk_ref, wv_ref, aq_ref, av_ref, bq_ref, bv_ref,
    soft_ref, key_ref, value_ref, down_q_ref, down_v_ref, mixed_ref,
    normed, query_sum, key_sum, value_sum,
):
    step = pl.program_id(0)
    length, width = x_ref.shape
    depth = wq_ref.shape[0]

    @pl.when(step == 0)
    def _():
        rows = x_ref[...].astype(F32)
        centred = rows - jnp.sum(rows, axis=-1, keepdims=True) / width
        spread = jnp.sum(centred * centred, axis=-1, keepdims=True) / width
        full = centred * lax.rsqrt(spread + EPS) * gain_ref[...] + bias_ref[...]
        normed[...] = full.astype(BF16)
        query_sum[...] = jnp.zeros_like(query_sum)
        key_sum[...] = jnp.zeros_like(key_sum)
        value_sum[...] = jnp.zeros_like(value_sum)
        down_q_ref[...] = jnp.zeros_like(down_q_ref)
        down_v_ref[...] = jnp.zeros_like(down_v_ref)

    part = normed[:, pl.ds(pl.multiple_of(step * depth, depth), depth)]
    query_sum[...] += dot32(part, wq_ref[...])
    key_sum[...] += dot32(part, wk_ref[...])
    value_sum[...] += dot32(part, wv_ref[...])
    down_q_ref[...] += dot32(part, aq_ref[...])
    down_v_ref[...] += dot32(part, av_ref[...])

    @pl.when(step == pl.num_programs(0) - 1)
    def _():
        limit = limit_ref[0]
        live = live_pairs(limit, length)
        kept = rows_below(limit, length, HEAD_DIM)
        query = query_sum[...] + ADAPTER_SCALE * high(down_q_ref[...], bq_ref[...])
        value = value_sum[...] + ADAPTER_SCALE * high(down_v_ref[...], bv_ref[...])
        query = query.astype(BF16)
        value = value.astype(BF16)
        key = key_sum[...].astype(BF16)
        key_ref[...] = key
        value_ref[...] = value
        for h in range(key.shape[1] // HEAD_DIM):
            scores = dot_nt(query[:, head(h)], key[:, head(h)]) * SCALE
            scores = jnp.where(live, scores, NEG)
            weights = jnp.exp(scores - jnp.max(scores, axis=-1, keepdims=True))
            soft = weights / jnp.sum(weights, axis=-1, keepdims=True)
            soft_ref[h] = soft
            mixed = dot32(soft.astype(BF16), value[:, head(h)]).astype(BF16)
            mixed_ref[:, head(h)] = jnp.where(kept, mixed.astype(F32), 0.0)


def project(limit, x, gain, bias, wq, wk, wv, aq, av, bq, bv):
    length, width = x.shape
    inner = wq.shape[1]
    rank = aq.shape[1]
    heads = inner // HEAD_DIM
    whole = lambda i: (0, 0)
    deep = lambda i: (i, 0)
    return pl.pallas_call(
        project_kernel,
        grid=(width // DEPTH,),
        in_specs=[
            SMEM,
            pl.BlockSpec((length, width), whole),
            pl.BlockSpec((1, width), whole),
            pl.BlockSpec((1, width), whole),
            pl.BlockSpec((DEPTH, inner), deep),
            pl.BlockSpec((DEPTH, inner), deep),
            pl.BlockSpec((DEPTH, inner), deep),
            pl.BlockSpec((DEPTH, rank), deep),
            pl.BlockSpec((DEPTH, rank), deep),
            pl.BlockSpec((rank, inner), whole),
            pl.BlockSpec((rank, inner), whole),
        ],
        out_specs=[
            pl.BlockSpec((heads, length, length), lambda i: (0, 0, 0)),
            pl.BlockSpec((length, inner), whole),
            pl.BlockSpec((length, inner), whole),
            pl.BlockSpec((length, rank), whole),
            pl.BlockSpec((length, rank), whole),
            pl.BlockSpec((length, inner), whole),
        ],
        out_shape=[
            jax.ShapeDtypeStruct((heads, length, length), F32),
            jax.ShapeDtypeStruct((length, inner), BF16),
            jax.ShapeDtypeStruct((length, inner), BF16),
            jax.ShapeDtypeStruct((length, rank), F32),
            jax.ShapeDtypeStruct((length, rank), F32),
            jax.ShapeDtypeStruct((length, inner), F32),
        ],
        scratch_shapes=[
            pltpu.VMEM((length, width), BF16),
            pltpu.VMEM((length, inner), F32),
            pltpu.VMEM((length, inner), F32),
            pltpu.VMEM((length, inner), F32),
        ],
        compiler_params=pltpu.CompilerParams(vmem_limit_bytes=LIMIT),
        cost_estimate=pl.CostEstimate(
            flops=6 * length * width * inner, bytes_accessed=6 * width * inner, transcendentals=0
        ),
    )(limit, x, gain[None], bias[None], wq, wk, wv, aq, av, bq, bv)


def pair_kernel(core_ref, own_ref, got_ref, out_ref):
    inner = own_ref.shape[0]
    out_ref[:inner] = own_ref[...]
    out_ref[inner:] = got_ref[...].astype(BF16)


def pair_weights(core, w_out, got):
    inner, half = got.shape
    blocks = half // COLUMNS
    return pl.pallas_call(
        pair_kernel,
        grid_spec=pltpu.PrefetchScalarGridSpec(
            num_scalar_prefetch=1,
            grid=(blocks,),
            in_specs=[
                pl.BlockSpec((inner, COLUMNS), lambda i, core: (0, core[0] * blocks + i)),
                pl.BlockSpec((inner, COLUMNS), lambda i, core: (0, i)),
            ],
            out_specs=pl.BlockSpec((2 * inner, COLUMNS), lambda i, core: (0, i)),
        ),
        out_shape=jax.ShapeDtypeStruct((2 * inner, half), BF16),
        compiler_params=pltpu.CompilerParams(vmem_limit_bytes=LIMIT),
    )(core, w_out, got)


def spread_kernel(own_ref, got_ref, w_ref, out_ref):
    inner = own_ref.shape[1]
    out_ref[...] = dot32(own_ref[...].astype(BF16), w_ref[:inner]) + dot32(
        got_ref[...].astype(BF16), w_ref[inner:]
    )


def spread(own, got, pair):
    length, inner = own.shape
    half = pair.shape[1]
    whole = lambda i: (0, 0)
    across = lambda i: (0, i)
    return pl.pallas_call(
        spread_kernel,
        grid=(half // COLUMNS,),
        in_specs=[
            pl.BlockSpec((length, inner), whole),
            pl.BlockSpec((length, inner), whole),
            pl.BlockSpec((2 * inner, COLUMNS), across),
        ],
        out_specs=pl.BlockSpec((length, COLUMNS), across),
        out_shape=jax.ShapeDtypeStruct((length, half), F32),
        compiler_params=pltpu.CompilerParams(vmem_limit_bytes=LIMIT),
    )(own, got, pair)


def gather_kernel(has_gap, core_ref, *refs):
    if has_gap:
        limit_ref, total_ref, x_ref, t_ref, w_ref, own_ref, other_ref = refs
    else:
        total_ref, w_ref, own_ref, other_ref = refs
    step = pl.program_id(0)
    length, inner = own_ref.shape
    total = total_ref[...]
    if has_gap:
        gap = x_ref[...].astype(F32) - t_ref[...].astype(F32)
        kept = rows_below(limit_ref[0], length, total.shape[1])
        total = jnp.where(kept, total + gap, 0.0)

    @pl.when(step == 0)
    def _():
        own_ref[...] = jnp.zeros_like(own_ref)
        other_ref[...] = jnp.zeros_like(other_ref)

    rounded = total.astype(BF16)
    own_ref[...] += dot_nt(rounded, w_ref[:inner])
    other_ref[:length] += dot_nt(rounded, w_ref[inner:])
    other_ref[length:] += jnp.sum(total * total)


def gather(core, total, pair, gap):
    length, half = total.shape
    inner = pair.shape[0] // 2
    blocks = half // COLUMNS
    whole = lambda i, core: (0, 0)
    across = lambda i, core: (0, i)
    chosen = lambda i, core: (0, core[0] * blocks + i)
    specs = [pl.BlockSpec((length, COLUMNS), across)]
    args = [total]
    if gap is not None:
        limit, x, t = gap
        specs = [SMEM] + specs + [pl.BlockSpec((length, COLUMNS), chosen)] * 2
        args = [limit] + args + [x, t]
    specs.append(pl.BlockSpec((2 * inner, COLUMNS), across))
    args.append(pair)
    return pl.pallas_call(
        functools.partial(gather_kernel, gap is not None),
        grid_spec=pltpu.PrefetchScalarGridSpec(
            num_scalar_prefetch=1,
            grid=(blocks,),
            in_specs=specs,
            out_specs=[
                pl.BlockSpec((length, inner), whole),
                pl.BlockSpec((length + 8, inner), whole),
            ],
        ),
        out_shape=[
            jax.ShapeDtypeStruct((length, inner), F32),
            jax.ShapeDtypeStruct((length + 8, inner), F32),
        ],
        compiler_params=pltpu.CompilerParams(vmem_limit_bytes=LIMIT),
    )(core, *args)


def cotangent_kernel(
    share, limit_ref, own_ref, other_ref, got_ref, soft_ref, key_ref, value_ref, down_q_ref,
    down_v_ref, out_ref,
):
    length, inner = own_ref.shape
    rank = down_q_ref.shape[1]
    live = live_pairs(limit_ref[0], length)
    pulled = (own_ref[...] + got_ref[:length]).astype(BF16)
    out_ref[2 * rank :] = other_ref[length:] + got_ref[length:]
    for h in range(inner // HEAD_DIM):
        soft = soft_ref[h]
        rows = pulled[:, head(h)]
        d_probs = dot_nt(rows, value_ref[:, head(h)]).astype(BF16).astype(F32)
        d_value = dot_tn(soft.astype(BF16), rows).astype(BF16).astype(F32)
        d_scores = soft * (d_probs - jnp.sum(soft * d_probs, axis=-1, keepdims=True))
        d_scores = jnp.where(live, d_scores, 0.0) * SCALE
        d_query = dot32(d_scores.astype(BF16), key_ref[:, head(h)]).astype(BF16).astype(F32)
        out_ref[:rank, head(h)] = share * lax.dot_general(
            down_q_ref[...], d_query, (((0,), (0,)), ((), ())), precision=HIGH,
            preferred_element_type=F32,
        )
        out_ref[rank : 2 * rank, head(h)] = share * lax.dot_general(
            down_v_ref[...], d_value, (((0,), (0,)), ((), ())), precision=HIGH,
            preferred_element_type=F32,
        )


def cotangent(share, limit, own, other, got, attention):
    inner = own.shape[1]
    rank = attention[3].shape[1]
    return pl.pallas_call(
        functools.partial(cotangent_kernel, share),
        in_specs=[SMEM] + [VMEM] * 8,
        out_specs=VMEM,
        out_shape=jax.ShapeDtypeStruct((2 * rank + 8, inner), F32),
        compiler_params=pltpu.CompilerParams(vmem_limit_bytes=LIMIT),
    )(limit, own, other, got, *attention)


def tangent_of(vector, limit, soft_ref, key_ref, value_ref, down_q_ref, down_v_ref, out_ref):
    length = key_ref.shape[0]
    rank = down_q_ref.shape[1]
    live = live_pairs(limit, length)
    kept = rows_below(limit, length, HEAD_DIM)
    d_query = (ADAPTER_SCALE * high(down_q_ref[...], vector[:rank])).astype(BF16)
    d_value = (ADAPTER_SCALE * high(down_v_ref[...], vector[rank:])).astype(BF16)
    for h in range(key_ref.shape[1] // HEAD_DIM):
        soft = soft_ref[h]
        d_scores = dot_nt(d_query[:, head(h)], key_ref[:, head(h)]) * SCALE
        d_scores = jnp.where(live, d_scores, 0.0)
        d_probs = soft * (d_scores - jnp.sum(soft * d_scores, axis=-1, keepdims=True))
        d_mixed = dot32(d_probs.astype(BF16), value_ref[:, head(h)]) + dot32(
            soft.astype(BF16), d_value[:, head(h)]
        )
        out_ref[:, head(h)] = jnp.where(kept, d_mixed.astype(BF16).astype(F32), 0.0)


def total_of(terms):
    while len(terms) > 1:
        terms = [terms[i] + terms[i + 1] for i in range(0, len(terms), 2)]
    return terms[0]


def put_sums(sums_ref, remain, image):
    lane = lax.broadcasted_iota(jnp.int32, sums_ref.shape, 1)
    cross = 0.0 if image is None else jnp.sum(remain * image)
    sums_ref[...] = jnp.where(lane == 0, jnp.sum(remain * remain), cross)


def first_kernel(n_dp, *refs):
    terms, refs = refs[:n_dp], refs[n_dp:]
    limit_ref, *attention, remain_ref, sums_ref, out_ref = refs
    grads = total_of([term[...] for term in terms])
    remain = -grads[: remain_ref.shape[0]]
    remain_ref[...] = remain
    put_sums(sums_ref, remain, None)
    tangent_of(remain, limit_ref[0], *attention, out_ref)


def first_step(terms, limit, attention):
    inner = terms[0].shape[1]
    length = attention[1].shape[0]
    rank = attention[3].shape[1]
    return pl.pallas_call(
        functools.partial(first_kernel, len(terms)),
        in_specs=[VMEM] * len(terms) + [SMEM] + [VMEM] * 5,
        out_specs=[VMEM] * 3,
        out_shape=[
            jax.ShapeDtypeStruct((2 * rank, inner), F32),
            jax.ShapeDtypeStruct((8, 128), F32),
            jax.ShapeDtypeStruct((length, inner), F32),
        ],
        compiler_params=pltpu.CompilerParams(vmem_limit_bytes=LIMIT),
    )(*terms, limit, *attention)


def step_kernel(n_dp, token_count, index, last, *refs):
    terms, refs = refs[:n_dp], refs[n_dp:]
    sums_ref, remain_ref, *refs = refs
    if index:
        before_ref, newton_ref, direction_ref, image_ref, *refs = refs
    part = total_of([term[...] for term in terms])
    remain = remain_ref[...]
    rows = remain.shape[0]
    norm, cross = sums_ref[:1, 0:1], sums_ref[:1, 1:2]
    fresh = part[:rows] + DAMP * remain
    curv = part[rows : rows + 1, 0:1] / token_count + DAMP * norm
    if index:
        ratio = norm / before_ref[:1, 0:1]
        curv = curv + 2.0 * ratio * cross + ratio * ratio * before_ref[:1, 1:2]
        direction = remain + ratio * direction_ref[...]
        image = fresh + ratio * image_ref[...]
    else:
        direction, image = remain, fresh
    alpha = norm / curv
    newton = alpha * direction
    if index:
        newton = newton_ref[...] + newton
    remain = remain - alpha * image
    if last:
        step_q_ref, step_v_ref, remain_q_ref, remain_v_ref = refs
        rank = rows // 2
        step_q_ref[...] = newton[:rank]
        step_v_ref[...] = newton[rank:]
        remain_q_ref[...] = remain[:rank]
        remain_v_ref[...] = remain[rank:]
        return
    limit_ref, *refs = refs
    attention, refs = refs[:5], refs[5:]
    next_remain, next_before, next_newton, next_direction, next_image, next_sums, out_ref = refs
    lane = lax.broadcasted_iota(jnp.int32, next_before.shape, 1)
    next_remain[...] = remain
    next_before[...] = jnp.where(lane == 0, norm, curv)
    next_newton[...] = newton
    next_direction[...] = direction
    next_image[...] = image
    put_sums(next_sums, remain, image)
    tangent_of(remain, limit_ref[0], *attention, out_ref)


def cg_step(index, token_count, terms, sums, remain, state, limit, attention):
    last = index == CG_STEPS - 1
    rows, inner = remain.shape
    matrix = jax.ShapeDtypeStruct((rows, inner), F32)
    scalars = jax.ShapeDtypeStruct((8, 128), F32)
    args = [*terms, sums, remain, *state]
    specs = [VMEM] * len(args)
    if last:
        shapes = [jax.ShapeDtypeStruct((rows // 2, inner), F32)] * 4
    else:
        args += [limit, *attention]
        specs += [SMEM] + [VMEM] * 5
        length = attention[1].shape[0]
        shapes = [matrix, scalars, matrix, matrix, matrix, scalars]
        shapes.append(jax.ShapeDtypeStruct((length, inner), F32))
    return pl.pallas_call(
        functools.partial(step_kernel, len(terms), token_count, index, last),
        in_specs=specs,
        out_specs=[VMEM] * len(shapes),
        out_shape=shapes,
        compiler_params=pltpu.CompilerParams(vmem_limit_bytes=LIMIT),
    )(*args)


def on_device(
    inputs,
    targets,
    lengths,
    ln_gain,
    ln_bias,
    query_weight,
    w_key,
    value_weight,
    w_out,
    down_query,
    down_value,
    query_up_factor,
    value_up_factor,
):
    length, width = inputs.shape
    n_dp = lax.axis_size("dp")
    n_chip = lax.axis_size("chip")
    core = lax.axis_index("core")
    token_count = length * n_dp
    half = width // 2

    def swap(part):
        return lax.ppermute(part, "core", [(0, 1), (1, 0)])

    def data_terms(part):
        return [part] + [
            lax.ppermute(part, "dp", [(d, d ^ step) for d in range(n_dp)])
            for step in range(1, n_dp)
        ]

    def head_sum(part):
        part = part + swap(part)
        step = 1
        while step < n_chip:
            part = part + lax.ppermute(part, "chip", [(c, c ^ step) for c in range(n_chip)])
            step *= 2
        return part

    where = core.astype(jnp.int32)[None]
    sent = lax.dynamic_slice_in_dim(w_out, (1 - core) * half, half, 1).astype(F32)
    pair = pair_weights(where, w_out, swap(sent))

    soft, key, value, down_q, down_v, mixed = project(
        lengths, inputs, ln_gain, ln_bias, query_weight, w_key, value_weight, down_query,
        down_value, query_up_factor, value_up_factor,
    )
    attention = (soft, key, value, down_q, down_v)

    def product(rows, gap):
        total = lax.psum(spread(rows, swap(rows), pair), "chip")
        own, other = gather(where, total, pair, gap)
        share = ADAPTER_SCALE / token_count
        return data_terms(cotangent(share, lengths, own, other, swap(other), attention))

    terms = product(mixed, (lengths, inputs, targets))
    remain, sums, rows = first_step(terms, lengths, attention)
    state = ()
    for index in range(CG_STEPS):
        sums = head_sum(sums)
        terms = product(rows, None)
        out = cg_step(index, token_count, terms, sums, remain, state, lengths, attention)
        if index < CG_STEPS - 1:
            remain, *state, sums, rows = out
    return tuple(out)


def solution(mesh):
    fine = Mesh(mesh.devices.reshape(mesh.shape["dp"], -1, 2), ("dp", "chip", "core"))
    tensor = ("chip", "core")
    in_specs = (
        P("dp", None),
        P("dp", None),
        P("dp"),
        P(),
        P(),
        P(None, tensor),
        P(None, tensor),
        P(None, tensor),
        P(tensor, None),
        P(),
        P(),
        P(None, tensor),
        P(None, tensor),
    )
    out_specs = (P(None, tensor),) * 4
    return jax.shard_map(
        on_device, mesh=fine, in_specs=in_specs, out_specs=out_specs, check_vma=False
    )
```

time: 565 us -> 437 us (0.77)
  blocking collectives: 137 us -> 0 us
  matrix products: 67.5 us -> 0 us
  Pallas kernels: 0 us -> 48.9 us
  local copies, waits for them, and re-layouts: 4.1 us -> 34.9 us
  starting transfers between devices: 0.51 us -> 21.8 us
  other arithmetic: 22.4 us -> 4.47 us
  between operations: 29.8 us -> 14.7 us
  waiting for transfers between devices: 302 us -> 311 us
    psum x0 -> x4, waiting for transfers between devices: none -> 275 us  [product(): total = lax.psum(spread(rows, swap(rows), pair), 'chip')]
    reduce_scatter x4 -> x0, waiting for transfers between devices: 152 us -> none  [head_total(): lax.psum_scatter(partial_value, 'tensor', scatter_dimension=0, tiled=True)]
    all_gather x4 -> x0, waiting for transfers between devices: 150 us -> none  [head_total(): return lax.all_gather(sent, 'tensor', axis=0, tiled=True)]
    psum x9 -> x0, blocking collectives: 137 us -> none  [the longest x4 66.7 us: data_sum(): return lax.psum((part[0], part[1]), 'dp')]
    dot_general x52 -> x0, matrix products: 67.5 us -> none  [the longest x8 39.3 us: attend(): return jnp.dot(mixed, w_out, preferred_element_type=jnp.float32)]
    pallas_call x0 -> x18, Pallas kernels: none -> 48.9 us  [the longest x4 14.7 us: spread(): pl.pallas_call(spread_kernel, grid=(half // COLUMNS,), in_specs=[pl.Block...]
    ppermute x0 -> x30, waiting for transfers between devices: none -> 36.2 us  [the longest x6 18 us: head_sum(): lax.ppermute(part, 'chip', [(c, c ^ step) for c in range(n_chip)])]
    unnamed x26 -> x62, local copies, waits for them, and re-layouts: 1.31 us -> 34.9 us
  transfers between devices with their start and end apart: 8 -> 34, of which waited for: 8 -> 23; matrix products, arithmetic and copies ran while one was open for 0% -> 1% of each run, Pallas kernels for 0% -> 3%
where the time goes in v1:
time: 437 us; the launch traced here: 436 us
  waiting for transfers between devices  311 us (71%)
  Pallas kernels  48.9 us (11%)
  local copies, waits for them, and re-layouts  34.9 us (8%)
  starting transfers between devices  21.8 us (5%)
  between operations  14.7 us (3%)
  other arithmetic  4.47 us (1%)
    psum x4, waiting for transfers between devices, product(): total = lax.psum(spread(rows, swap(rows), pair), 'chip')  275 us
    unnamed x62, local copies, waits for them, and re-layouts  34.9 us
    ppermute x6, waiting for transfers between devices, head_sum(): lax.ppermute(part, 'chip', [(c, c ^ step) for c in range(n_chip)])  18 us
    pallas_call x4, Pallas kernels, spread(): pl.pallas_call(spread_kernel, grid=(half // COLUMNS,), in_specs=[pl.Block...  14.7 us
    ppermute x12, starting transfers between devices, data_terms(): lax.ppermute(part, 'dp', [(d, d ^ step) for d in range(n_dp)])  14 us
    ppermute x12, waiting for transfers between devices, swap(): return lax.ppermute(part, 'core', [(0, 1), (1, 0)])  13.6 us
    pallas_call x4, Pallas kernels, gather(): pl.pallas_call(functools.partial(gather_kernel, gap is not None), grid_sp...  12.2 us
  transfers between devices with their start and end apart: 34, of which 23 were waited for; matrix products, arithmetic and copies ran while one was open for 1% of the time, Pallas kernels for 3%

profile of v1, /device:TPU:0, one launch (start us, length us, event | category | flops | bytes accessed | tf_op | source)
XLA Modules:
  0.0 435.8 jit_solution(3260848455106276677)
XLA Ops:
  7.2 4.4 %dynamic-slice_convert_fusion = f32[384,3072]{1,0:T(8,128)} fusion(bf16[384,6144]{1,0:T(8,128)(2,1)} %own_ref.1, s32[]{:T(128)S(6)} %select_n.3), kind=kLoop, calls=%fused_computation | loop fusion | flops 1179648 | bytes 7077892 | tf_op jit(solution)/shard_map/convert_element_type | solution.py:479
  13.6 1.5 copy.18.av_ref
  15.1 1.6 copy-done.9
  16.7 2.5 copy-done.10
  19.2 2.3 copy-done.11
  21.5 2.3 copy-done.12
  26.8 8.4 %shard_map.156 = (f32[3,128,128]{2,1,0:T(8,128)S(1)}, bf16[128,384]{1,0:T(8,128)(2,1)S(1)}, bf16[128,384]{1,0:T(8,128)(2,1)S(1)}, f32[128,16]{1,0:T(8,128)S(1)},...) custom-call(s32[1]{0:T(128)S(6)} %copy.23.limit_ref.refs_0_.refs_4_.refs_6_.refs_10_, bf16[128,6144]{1,0:T(8,128)(2,1)S(1)} %copy-done.8, ...), custom_call_target="tpu_custom_call" | custom-call | flops 1811939328 | bytes 14155776 | tf_op jit(solution)/shard_map/pallas_call | solution.py:121
  35.5 4.3 shard_map.157.w_ref.refs_4_.refs_1_
  39.8 3.6 shard_map.158
  43.4 2.2 copy-done
  45.7 71.9 %all-reduce.5.cloned.1.call-done.refs_1_ = f32[128,3072]{1,0:T(8,128)} async-done(((f32[128,3072]{1,0:T(8,128)}), f32[128,3072]{1,0:T(8,128)}) %all-reduce.5.cloned.1.call-update) | async-done | bytes 1572880 | tf_op jit(solution)/shard_map/psum | solution.py:489
  117.6 2.3 copy-done.1
  122.7 3.5 shard_map.159
  127.7 1.5 shard_map.160.refs_0_
  129.2 1.5 collective-permute-start.3
  130.7 1.5 collective-permute-start.4
  133.5 1.5 collective-permute-done.4.refs_2_
  135.0 2.4 collective-permute-done.5.refs_3_
  139.6 3.7 shard_map.162
  143.4 66.5 %all-reduce.7.cloned.1.call-done.refs_0_ = f32[128,3072]{1,0:T(8,128)} async-done(((f32[128,3072]{1,0:T(8,128)}), f32[128,3072]{1,0:T(8,128)}) %all-reduce.7.cloned.1.call-update) | async-done | bytes 1572880 | tf_op jit(solution)/shard_map/psum | solution.py:489
  209.8 2.3 copy-done.3
  213.6 2.9 shard_map.163
  218.0 1.5 shard_map.164.refs_0_
  219.5 2.4 collective-permute-start.10
  224.9 3.0 collective-permute-done.12
  227.8 1.5 collective-permute-start.13
  229.3 3.0 collective-permute-done.13
  234.7 2.3 copy-done.4
  237.0 3.7 shard_map.166
  241.0 68.1 %all-reduce.9.cloned.1.call-done.refs_0_ = f32[128,3072]{1,0:T(8,128)} async-done(((f32[128,3072]{1,0:T(8,128)}), f32[128,3072]{1,0:T(8,128)}) %all-reduce.9.cloned.1.call-update) | async-done | bytes 1572880 | tf_op jit(solution)/shard_map/psum | solution.py:489
  309.0 2.3 copy-done.5
  312.8 2.9 shard_map.167
  317.2 1.5 shard_map.168.refs_0_
  318.8 1.5 collective-permute-start.16
  320.2 1.5 collective-permute-start.17
  324.1 3.0 collective-permute-done.20
  327.0 1.5 collective-permute-start.21
  328.5 3.0 collective-permute-done.21
  334.0 3.7 shard_map.170
  337.7 68.3 %all-reduce.11.cloned.1.call-done.refs_0_ = f32[128,3072]{1,0:T(8,128)} async-done(((f32[128,3072]{1,0:T(8,128)}), f32[128,3072]{1,0:T(8,128)}) %all-reduce.11.cloned.1.call-update) | async-done | bytes 1572880 | tf_op jit(solution)/shard_map/psum | solution.py:489
  406.0 2.3 copy-done.7
  409.7 2.9 shard_map.171
  414.2 1.5 shard_map.172.refs_0_
  415.7 1.5 collective-permute-start.24
  417.2 1.5 collective-permute-start.25
  421.0 3.0 collective-permute-done.28
  424.0 1.5 collective-permute-start.29
  425.4 3.0 collective-permute-done.29
  (115 shorter events, 34.6 us)
Async XLA Ops:
  7.2 110.4 %all-reduce.5.cloned.1.call-start = ((), (), s32[]{:S(2)}) async-start(), calls=%async_computation | async-start | bytes 3145728 | tf_op jit(solution)/shard_map/psum | solution.py:489
  7.2 5.6 %copy-start.26 = (bf16[6144,16]{0,1:T(8,128)(2,1)S(1)}, bf16[6144,16]{0,1:T(8,128)(2,1)}, u32[]{:S(2)}) copy-start(bf16[6144,16]{0,1:T(8,128)(2,1)} %param.22) | copy-start | bytes 589828
  11.7 23.8 %collective-permute-start.1 = (f32[384,3072]{1,0:T(8,128)}, f32[384,3072]{1,0:T(8,128)}, u32[]{:S(2)}, u32[]{:S(2)}) collective-permute-start(f32[384,3072]{1,0:T(8,128)} %dynamic-slice_convert_fusion), channel_id=1, source_target_pairs={{0,1},{1,0},{2,3},{3,2},{4,5},{5,4},{6,7},{7,6},{8,9},{9,8},{10,11... | collective-permute-start | bytes 14155784 | tf_op jit(solution)/shard_map/ppermute | solution.py:462
  15.1 20.4 %slice-start = ((s8[4718592]{0:T(1024)(128)(4,1)}), s8[4194304]{0:T(1024)(128)(4,1)S(1)}, s32[]{:S(2)}) async-start(s8[4718592]{0:T(1024)(128)(4,1)} %bitcast.3), calls=%async_computation.4 | async-start | bytes 8388608
  16.7 2.5 copy-start.10
  19.2 2.3 copy-start.11
  21.5 2.3 copy-start.12
  26.8 8.7 %slice-start.1 = ((s8[4718592]{0:T(1024)(128)(4,1)}), s8[524288]{0:T(1024)(128)(4,1)S(1)}, s32[]{:S(2)}) async-start(s8[4718592]{0:T(1024)(128)(4,1)} %bitcast.3), calls=%async_computation.5 | async-start | bytes 1048576
  35.3 4.5 %copy-start.13 = (f32[128,16]{1,0:T(8,128)}, f32[128,16]{1,0:T(8,128)S(1)}, u32[]{:S(2)}) copy-start(f32[128,16]{1,0:T(8,128)S(1)} %get-tuple-element.41.down_q_ref.refs_8_.refs_10_.refs_14_) | copy-start | bytes 24580
  35.3 4.5 %copy-start.15 = (f32[128,16]{1,0:T(8,128)}, f32[128,16]{1,0:T(8,128)S(1)}, u32[]{:S(2)}) copy-start(f32[128,16]{1,0:T(8,128)S(1)} %get-tuple-element.42.down_v_ref.refs_9_.refs_11_.refs_15_) | copy-start | bytes 24580
  35.3 4.5 %collective-permute-start = (f32[128,384]{1,0:T(8,128)S(1)}, f32[128,384]{1,0:T(8,128)S(1)}, u32[]{:S(2)}, u32[]{:S(2)}) collective-permute-start(f32[128,384]{1,0:T(8,128)S(1)} %get-tuple-element.35.own_ref), channel_id=1, source_target_pairs={{0,1},{1,0},{2,3},{3,2},{4,5},{5,4},{6,7},{7,6},{8,9},{9,8},{10,11... | collective-permute-start | bytes 589832 | tf_op jit(solution)/shard_map/ppermute | solution.py:462
  45.6 82.1 %copy-start.14 = (f32[128,16]{1,0:T(8,128)S(1)}, f32[128,16]{1,0:T(8,128)}, u32[]{:S(2)}) copy-start(f32[128,16]{1,0:T(8,128)} %copy-done.13) | copy-start | bytes 24580
  45.6 82.1 %copy-start.16 = (f32[128,16]{1,0:T(8,128)S(1)}, f32[128,16]{1,0:T(8,128)}, u32[]{:S(2)}) copy-start(f32[128,16]{1,0:T(8,128)} %copy-done.15) | copy-start | bytes 24580
  45.6 164.2 %all-reduce.7.cloned.1.call-start = ((), (), s32[]{:S(2)}) async-start(), calls=%async_computation.1 | async-start | bytes 3145728 | tf_op jit(solution)/shard_map/psum | solution.py:489
  122.7 16.9 %copy-start.2 = (bf16[768,3072]{1,0:T(8,128)(2,1)S(1)}, bf16[768,3072]{1,0:T(8,128)(2,1)}, u32[]{:S(2)}) copy-start(bf16[768,3072]{1,0:T(8,128)(2,1)} %copy-done) | copy-start | bytes 14155780
  126.2 1.5 collective-permute-start.2
  129.2 4.2 collective-permute-start.3
  130.7 4.2 collective-permute-start.4
  132.2 5.1 %collective-permute-start.5 = (f32[40,384]{1,0:T(8,128)S(1)}, f32[40,384]{1,0:T(8,128)S(1)}, u32[]{:S(2)}, u32[]{:S(2)}) collective-permute-start(f32[40,384]{1,0:T(8,128)S(1)} %shard_map.160.refs_0_), channel_id=1, source_target_pairs={{0,24},{8,16},{16,8},{24,0},{1,25},{9,17},{17,9},{25,1},{2,26},{10... | collective-permute-start | bytes 184328 | tf_op jit(solution)/shard_map/ppermute | solution.py:466
  138.1 1.5 collective-permute-start.6
  143.3 165.7 %all-reduce.9.cloned.1.call-start = ((), (), s32[]{:S(2)}) async-start(), calls=%async_computation.2 | async-start | bytes 3145728 | tf_op jit(solution)/shard_map/psum | solution.py:489
  209.8 2.3 copy-start.3
  216.5 1.5 collective-permute-start.7
  219.5 12.8 %collective-permute-start.10 = (f32[40,384]{1,0:T(8,128)S(1)}, f32[40,384]{1,0:T(8,128)S(1)}, u32[]{:S(2)}, u32[]{:S(2)}) collective-permute-start(f32[40,384]{1,0:T(8,128)S(1)} %shard_map.164.refs_0_), channel_id=1, source_target_pairs={{0,24},{8,16},{16,8},{24,0},{1,25},{9,17},{17,9},{25,1},{2,26},{10... | collective-permute-start | bytes 184328 | tf_op jit(solution)/shard_map/ppermute | solution.py:466
  221.9 10.4 %collective-permute-start.8 = (f32[40,384]{1,0:T(8,128)S(1)}, f32[40,384]{1,0:T(8,128)S(1)}, u32[]{:S(2)}, u32[]{:S(2)}) collective-permute-start(f32[40,384]{1,0:T(8,128)S(1)} %shard_map.164.refs_0_), channel_id=1, source_target_pairs={{0,8},{8,0},{16,24},{24,16},{1,9},{9,1},{17,25},{25,17},{2,10},{10... | collective-permute-start | bytes 184328 | tf_op jit(solution)/shard_map/ppermute | solution.py:466
  222.5 9.9 %collective-permute-start.9 = (f32[40,384]{1,0:T(8,128)S(1)}, f32[40,384]{1,0:T(8,128)S(1)}, u32[]{:S(2)}, u32[]{:S(2)}) collective-permute-start(f32[40,384]{1,0:T(8,128)S(1)} %shard_map.164.refs_0_), channel_id=1, source_target_pairs={{0,16},{8,24},{16,0},{24,8},{1,17},{9,25},{17,1},{25,9},{2,18},{10... | collective-permute-start | bytes 184328 | tf_op jit(solution)/shard_map/ppermute | solution.py:466
  223.0 1.2 collective-permute-start.11
  224.2 3.6 collective-permute-start.12
  227.8 4.5 %collective-permute-start.13 = (f32[8,128]{1,0:T(8,128)S(1)}, f32[8,128]{1,0:T(8,128)S(1)}, u32[]{:S(2)}, u32[]{:S(2)}) collective-permute-start(f32[8,128]{1,0:T(8,128)S(1)} %add.40), channel_id=1, source_target_pairs={{0,4},{2,6},{4,0},{6,2},{1,5},{3,7},{5,1},{7,3},{8,12},{10,14},{12... | collective-permute-start | bytes 12296 | tf_op jit(solution)/shard_map/ppermute | solution.py:474
  233.2 1.5 collective-permute-start.14
  234.7 2.3 copy-start.4
  240.7 165.3 %all-reduce.11.cloned.1.call-start = ((), (), s32[]{:S(2)}) async-start(), calls=%async_computation.3 | async-start | bytes 3145728 | tf_op jit(solution)/shard_map/psum | solution.py:489
  312.8 21.2 %copy-start.6 = (bf16[768,3072]{1,0:T(8,128)(2,1)S(1)}, bf16[768,3072]{1,0:T(8,128)(2,1)}, u32[]{:S(2)}) copy-start(bf16[768,3072]{1,0:T(8,128)(2,1)} %copy-done) | copy-start | bytes 14155780
  315.7 1.5 collective-permute-start.15
  318.8 12.8 %collective-permute-start.16 = (f32[40,384]{1,0:T(8,128)S(1)}, f32[40,384]{1,0:T(8,128)S(1)}, u32[]{:S(2)}, u32[]{:S(2)}) collective-permute-start(f32[40,384]{1,0:T(8,128)S(1)} %shard_map.168.refs_0_), channel_id=1, source_target_pairs={{0,8},{8,0},{16,24},{24,16},{1,9},{9,1},{17,25},{25,17},{2,10},{10... | collective-permute-start | bytes 184328 | tf_op jit(solution)/shard_map/ppermute | solution.py:466
  320.2 11.3 %collective-permute-start.17 = (f32[40,384]{1,0:T(8,128)S(1)}, f32[40,384]{1,0:T(8,128)S(1)}, u32[]{:S(2)}, u32[]{:S(2)}) collective-permute-start(f32[40,384]{1,0:T(8,128)S(1)} %shard_map.168.refs_0_), channel_id=1, source_target_pairs={{0,16},{8,24},{16,0},{24,8},{1,17},{9,25},{17,1},{25,9},{2,18},{10... | collective-permute-start | bytes 184328 | tf_op jit(solution)/shard_map/ppermute | solution.py:466
  321.7 9.9 %collective-permute-start.18 = (f32[40,384]{1,0:T(8,128)S(1)}, f32[40,384]{1,0:T(8,128)S(1)}, u32[]{:S(2)}, u32[]{:S(2)}) collective-permute-start(f32[40,384]{1,0:T(8,128)S(1)} %shard_map.168.refs_0_), channel_id=1, source_target_pairs={{0,24},{8,16},{16,8},{24,0},{1,25},{9,17},{17,9},{25,1},{2,26},{10... | collective-permute-start | bytes 184328 | tf_op jit(solution)/shard_map/ppermute | solution.py:466
  322.3 1.2 collective-permute-start.19
  323.4 3.6 collective-permute-start.20
  327.0 4.5 %collective-permute-start.21 = (f32[8,128]{1,0:T(8,128)S(1)}, f32[8,128]{1,0:T(8,128)S(1)}, u32[]{:S(2)}, u32[]{:S(2)}) collective-permute-start(f32[8,128]{1,0:T(8,128)S(1)} %add.43), channel_id=1, source_target_pairs={{0,4},{2,6},{4,0},{6,2},{1,5},{3,7},{5,1},{7,3},{8,12},{10,14},{12... | collective-permute-start | bytes 12296 | tf_op jit(solution)/shard_map/ppermute | solution.py:474
  332.4 1.5 collective-permute-start.22
  412.6 1.5 collective-permute-start.23
  415.7 12.8 %collective-permute-start.24 = (f32[40,384]{1,0:T(8,128)S(1)}, f32[40,384]{1,0:T(8,128)S(1)}, u32[]{:S(2)}, u32[]{:S(2)}) collective-permute-start(f32[40,384]{1,0:T(8,128)S(1)} %shard_map.172.refs_0_), channel_id=1, source_target_pairs={{0,8},{8,0},{16,24},{24,16},{1,9},{9,1},{17,25},{25,17},{2,10},{10... | collective-permute-start | bytes 184328 | tf_op jit(solution)/shard_map/ppermute | solution.py:466
  417.2 11.3 %collective-permute-start.25 = (f32[40,384]{1,0:T(8,128)S(1)}, f32[40,384]{1,0:T(8,128)S(1)}, u32[]{:S(2)}, u32[]{:S(2)}) collective-permute-start(f32[40,384]{1,0:T(8,128)S(1)} %shard_map.172.refs_0_), channel_id=1, source_target_pairs={{0,16},{8,24},{16,0},{24,8},{1,17},{9,25},{17,1},{25,9},{2,18},{10... | collective-permute-start | bytes 184328 | tf_op jit(solution)/shard_map/ppermute | solution.py:466
  418.6 9.9 %collective-permute-start.26 = (f32[40,384]{1,0:T(8,128)S(1)}, f32[40,384]{1,0:T(8,128)S(1)}, u32[]{:S(2)}, u32[]{:S(2)}) collective-permute-start(f32[40,384]{1,0:T(8,128)S(1)} %shard_map.172.refs_0_), channel_id=1, source_target_pairs={{0,24},{8,16},{16,8},{24,0},{1,25},{9,17},{17,9},{25,1},{2,26},{10... | collective-permute-start | bytes 184328 | tf_op jit(solution)/shard_map/ppermute | solution.py:466
  419.2 1.2 collective-permute-start.27
  420.4 3.6 collective-permute-start.28
  424.0 4.5 %collective-permute-start.29 = (f32[8,128]{1,0:T(8,128)S(1)}, f32[8,128]{1,0:T(8,128)S(1)}, u32[]{:S(2)}, u32[]{:S(2)}) collective-permute-start(f32[8,128]{1,0:T(8,128)S(1)} %add.46), channel_id=1, source_target_pairs={{0,4},{2,6},{4,0},{6,2},{1,5},{3,7},{5,1},{7,3},{8,12},{10,14},{12... | collective-permute-start | bytes 12296 | tf_op jit(solution)/shard_map/ppermute | solution.py:474
  (16 other events, 25.0 us)
Sparse Core Ops, SparseCore 0:
  45.7 71.7 all-reduce.4
  143.4 66.3 all-reduce.6
  240.8 68.1 all-reduce.8
  337.8 68.1 all-reduce.10

commit v2 on v1

--- a/solution.py
+++ b/solution.py
@@ -10,7 +10,8 @@
 
 HEAD_DIM = 128
 CG_STEPS = 3
-COLUMNS = 512
+CHUNKS = 4
+AHEAD = 2
 DEPTH = 512
 
 EPS = 1e-05
@@ -24,6 +25,8 @@
 VMEM = pl.BlockSpec(memory_space=pltpu.VMEM)
 SMEM = pl.BlockSpec(memory_space=pltpu.SMEM)
 LIMIT = 32 * 1024 * 1024
+STEP_COST = pl.CostEstimate(flops=10**9, bytes_accessed=10**7, transcendentals=0)
+STREAM_LIMIT = 56 * 1024 * 1024
 
 
 def dot32(first, second):
@@ -108,7 +111,8 @@
             soft = weights / jnp.sum(weights, axis=-1, keepdims=True)
             soft_ref[h] = soft
             mixed = dot32(soft.astype(BF16), value[:, head(h)]).astype(BF16)
-            mixed_ref[:, head(h)] = jnp.where(kept, mixed.astype(F32), 0.0)
+            mixed_ref[:length, head(h)] = jnp.where(kept, mixed.astype(F32), 0.0)
+        mixed_ref[length:] = jnp.zeros((8, key.shape[1]), F32)
 
 
 def project(limit, x, gain, bias, wq, wk, wv, aq, av, bq, bv):
@@ -140,7 +144,7 @@
             pl.BlockSpec((length, inner), whole),
             pl.BlockSpec((length, rank), whole),
             pl.BlockSpec((length, rank), whole),
-            pl.BlockSpec((length, inner), whole),
+            pl.BlockSpec((length + 8, inner), whole),
         ],
         out_shape=[
             jax.ShapeDtypeStruct((heads, length, length), F32),
@@ -148,7 +152,7 @@
             jax.ShapeDtypeStruct((length, inner), BF16),
             jax.ShapeDtypeStruct((length, rank), F32),
             jax.ShapeDtypeStruct((length, rank), F32),
-            jax.ShapeDtypeStruct((length, inner), F32),
+            jax.ShapeDtypeStruct((length + 8, inner), F32),
         ],
         scratch_shapes=[
             pltpu.VMEM((length, width), BF16),
@@ -156,120 +160,154 @@
             pltpu.VMEM((length, inner), F32),
             pltpu.VMEM((length, inner), F32),
         ],
-        compiler_params=pltpu.CompilerParams(vmem_limit_bytes=LIMIT),
+        compiler_params=pltpu.CompilerParams(vmem_limit_bytes=STREAM_LIMIT),
         cost_estimate=pl.CostEstimate(
             flops=6 * length * width * inner, bytes_accessed=6 * width * inner, transcendentals=0
         ),
     )(limit, x, gain[None], bias[None], wq, wk, wv, aq, av, bq, bv)
 
 
-def pair_kernel(core_ref, own_ref, got_ref, out_ref):
-    inner = own_ref.shape[0]
-    out_ref[:inner] = own_ref[...]
-    out_ref[inner:] = got_ref[...].astype(BF16)
-
-
-def pair_weights(core, w_out, got):
-    inner, half = got.shape
-    blocks = half // COLUMNS
+def token_spec():
+    return pl.BlockSpec(memory_space=pl.ANY)
+
+
+def call(kernel, ins, outs, token, scalars=()):
+    tokens = [] if token is None else [token]
+
+    def body(*refs):
+        count = len(scalars) + len(ins)
+        kernel(*refs[:count], *refs[count + len(tokens) :])
+
     return pl.pallas_call(
-        pair_kernel,
+        body,
+        in_specs=[SMEM] * len(scalars) + [VMEM] * len(ins) + [token_spec()] * len(tokens),
+        out_specs=[VMEM] * len(outs),
+        out_shape=[jax.ShapeDtypeStruct(shape, kind) for shape, kind in outs],
+        compiler_params=pltpu.CompilerParams(vmem_limit_bytes=LIMIT),
+        cost_estimate=STEP_COST,
+    )(*scalars, *ins, *tokens)
+
+
+def rows_of(own_ref, got_ref, length):
+    return jnp.concatenate(
+        [own_ref[:length].astype(BF16), got_ref[:length].astype(BF16)], axis=1
+    )
+
+
+def put_tail(out_ref, own_ref, got_ref, length):
+    inner = own_ref.shape[1]
+    out_ref[length:, inner:] = jnp.zeros((8, out_ref.shape[1] - inner), F32)
+    out_ref[length:, :inner] = own_ref[length:] + got_ref[length:]
+
+
+def first_spread_kernel(tail, length, core_ref, own_ref, got_ref, w_ref, other_w_ref, *refs):
+    out_ref, pair_ref = refs[-2:]
+    inner = own_ref.shape[1]
+    pair_ref[:inner] = w_ref[...]
+    pair_ref[inner:] = other_w_ref[...].astype(BF16)
+    out_ref[:length] = dot32(rows_of(own_ref, got_ref, length), pair_ref[...])
+    if tail:
+        put_tail(out_ref, own_ref, got_ref, length)
+
+
+def first_spread(index, chunks, length, core, own, got, w_out, other_w, token):
+    inner, half = other_w.shape
+    cols = half // chunks
+    height = length + (8 if index == 0 else 0)
+    whole = lambda i, core: (0, 0)
+    tokens = [] if token is None else [token]
+    return pl.pallas_call(
+        functools.partial(first_spread_kernel, index == 0, length),
         grid_spec=pltpu.PrefetchScalarGridSpec(
             num_scalar_prefetch=1,
-            grid=(blocks,),
+            grid=(1,),
             in_specs=[
-                pl.BlockSpec((inner, COLUMNS), lambda i, core: (0, core[0] * blocks + i)),
-                pl.BlockSpec((inner, COLUMNS), lambda i, core: (0, i)),
-            ],
-            out_specs=pl.BlockSpec((2 * inner, COLUMNS), lambda i, core: (0, i)),
-        ),
-        out_shape=jax.ShapeDtypeStruct((2 * inner, half), BF16),
-        compiler_params=pltpu.CompilerParams(vmem_limit_bytes=LIMIT),
-    )(core, w_out, got)
-
-
-def spread_kernel(own_ref, got_ref, w_ref, out_ref):
-    inner = own_ref.shape[1]
-    out_ref[...] = dot32(own_ref[...].astype(BF16), w_ref[:inner]) + dot32(
-        got_ref[...].astype(BF16), w_ref[inner:]
-    )
-
-
-def spread(own, got, pair):
-    length, inner = own.shape
-    half = pair.shape[1]
-    whole = lambda i: (0, 0)
-    across = lambda i: (0, i)
-    return pl.pallas_call(
-        spread_kernel,
-        grid=(half // COLUMNS,),
-        in_specs=[
-            pl.BlockSpec((length, inner), whole),
-            pl.BlockSpec((length, inner), whole),
-            pl.BlockSpec((2 * inner, COLUMNS), across),
-        ],
-        out_specs=pl.BlockSpec((length, COLUMNS), across),
-        out_shape=jax.ShapeDtypeStruct((length, half), F32),
-        compiler_params=pltpu.CompilerParams(vmem_limit_bytes=LIMIT),
-    )(own, got, pair)
-
-
-def gather_kernel(has_gap, core_ref, *refs):
-    if has_gap:
-        limit_ref, total_ref, x_ref, t_ref, w_ref, own_ref, other_ref = refs
-    else:
-        total_ref, w_ref, own_ref, other_ref = refs
-    step = pl.program_id(0)
-    length, inner = own_ref.shape
-    total = total_ref[...]
-    if has_gap:
-        gap = x_ref[...].astype(F32) - t_ref[...].astype(F32)
-        kept = rows_below(limit_ref[0], length, total.shape[1])
-        total = jnp.where(kept, total + gap, 0.0)
-
-    @pl.when(step == 0)
-    def _():
-        own_ref[...] = jnp.zeros_like(own_ref)
-        other_ref[...] = jnp.zeros_like(other_ref)
-
-    rounded = total.astype(BF16)
-    own_ref[...] += dot_nt(rounded, w_ref[:inner])
-    other_ref[:length] += dot_nt(rounded, w_ref[inner:])
-    other_ref[length:] += jnp.sum(total * total)
-
-
-def gather(core, total, pair, gap):
-    length, half = total.shape
-    inner = pair.shape[0] // 2
-    blocks = half // COLUMNS
-    whole = lambda i, core: (0, 0)
-    across = lambda i, core: (0, i)
-    chosen = lambda i, core: (0, core[0] * blocks + i)
-    specs = [pl.BlockSpec((length, COLUMNS), across)]
-    args = [total]
-    if gap is not None:
-        limit, x, t = gap
-        specs = [SMEM] + specs + [pl.BlockSpec((length, COLUMNS), chosen)] * 2
-        args = [limit] + args + [x, t]
-    specs.append(pl.BlockSpec((2 * inner, COLUMNS), across))
-    args.append(pair)
-    return pl.pallas_call(
-        functools.partial(gather_kernel, gap is not None),
-        grid_spec=pltpu.PrefetchScalarGridSpec(
-            num_scalar_prefetch=1,
-            grid=(blocks,),
-            in_specs=specs,
+                pl.BlockSpec(own.shape, whole),
+                pl.BlockSpec(own.shape, whole),
+                pl.BlockSpec((inner, cols), lambda i, core: (0, core[0] * chunks + index)),
+                pl.BlockSpec((inner, cols), lambda i, core: (0, index)),
+            ] + [token_spec()] * len(tokens),
             out_specs=[
-                pl.BlockSpec((length, inner), whole),
-                pl.BlockSpec((length + 8, inner), whole),
+                pl.BlockSpec((height, cols), whole),
+                pl.BlockSpec((2 * inner, cols), whole),
             ],
         ),
         out_shape=[
-            jax.ShapeDtypeStruct((length, inner), F32),
-            jax.ShapeDtypeStruct((length + 8, inner), F32),
+            jax.ShapeDtypeStruct((height, cols), F32),
+            jax.ShapeDtypeStruct((2 * inner, cols), BF16),
         ],
         compiler_params=pltpu.CompilerParams(vmem_limit_bytes=LIMIT),
-    )(core, *args)
+        cost_estimate=STEP_COST,
+    )(core, own, got, w_out, other_w, *tokens)
+
+
+def spread(index, length, own, got, pair, token):
+    height = length + (8 if index == 0 else 0)
+
+    def kernel(own_ref, got_ref, pair_ref, out_ref):
+        out_ref[:length] = dot32(rows_of(own_ref, got_ref, length), pair_ref[...])
+        if index == 0:
+            put_tail(out_ref, own_ref, got_ref, length)
+
+    return call(kernel, [own, got, pair], [((height, pair.shape[1]), F32)], token)[0]
+
+
+def add(first, second, token):
+    def kernel(first_ref, second_ref, out_ref):
+        out_ref[...] = first_ref[...] + second_ref[...]
+
+    return call(kernel, [first, second], [(first.shape, F32)], token)[0]
+
+
+def choose(takes, got, held, token):
+    def kernel(takes_ref, got_ref, held_ref, out_ref):
+        out_ref[...] = jnp.where(takes_ref[0] > 0, got_ref[...], held_ref[...])
+
+    return call(kernel, [got, held], [(held.shape, F32)], token, [takes])[0]
+
+
+def gather(index, takes, got, held, pair, sums, limit, gap, token):
+    inner = pair.shape[0] // 2
+    extra = [] if gap is None else [gap]
+    length = held.shape[0] - (8 if index == 0 else 0)
+
+    def kernel(takes_ref, limit_ref, got_ref, held_ref, pair_ref, *refs):
+        refs = list(refs)
+        gap_ref = refs.pop(0) if gap is not None else None
+        before = [refs.pop(0), refs.pop(0)] if index else None
+        own_ref, other_ref = refs[:2]
+        total = jnp.where(takes_ref[0] > 0, got_ref[...], held_ref[...])
+        if index == 0:
+            refs[2][...] = total[length:, :128]
+            total = total[:length]
+        if gap_ref is not None:
+            kept = rows_below(limit_ref[0], length, total.shape[1])
+            total = jnp.where(kept, total + gap_ref[...], 0.0)
+        rounded = total.astype(BF16)
+        own = dot_nt(rounded, pair_ref[:inner])
+        other = dot_nt(rounded, pair_ref[inner:])
+        squares = jnp.full((8, inner), jnp.sum(total * total), F32)
+        if index:
+            own = own + before[0][...]
+            other = other + before[1][:length]
+            squares = squares + before[1][length:]
+        own_ref[...] = own
+        other_ref[:length] = other
+        other_ref[length:] = squares
+
+    outs = [((length, inner), F32), ((length + 8, inner), F32)]
+    if index == 0:
+        outs.append(((8, 128), F32))
+    return call(kernel, [got, held, pair] + extra + sums, outs, token, [takes, limit])
+
+
+def line_hops(chips):
+    inward = []
+    for step in range(chips // 2 - 1):
+        inward.append([(step, step + 1), (chips - 1 - step, chips - 2 - step)])
+    middle = [(chips // 2 - 1, chips // 2), (chips // 2, chips // 2 - 1)]
+    outward = [[(b, a) for a, b in hop] for hop in reversed(inward)]
+    return inward + [middle], outward
 
 
 def cotangent_kernel(
@@ -326,7 +364,7 @@
         d_mixed = dot32(d_probs.astype(BF16), value_ref[:, head(h)]) + dot32(
             soft.astype(BF16), d_value[:, head(h)]
         )
-        out_ref[:, head(h)] = jnp.where(kept, d_mixed.astype(BF16).astype(F32), 0.0)
+        out_ref[:length, head(h)] = jnp.where(kept, d_mixed.astype(BF16).astype(F32), 0.0)
 
 
 def total_of(terms):
@@ -335,19 +373,19 @@
     return terms[0]
 
 
-def put_sums(sums_ref, remain, image):
-    lane = lax.broadcasted_iota(jnp.int32, sums_ref.shape, 1)
+def put_sums(out_ref, remain, image):
+    lane = lax.broadcasted_iota(jnp.int32, (8, out_ref.shape[1]), 1)
     cross = 0.0 if image is None else jnp.sum(remain * image)
-    sums_ref[...] = jnp.where(lane == 0, jnp.sum(remain * remain), cross)
+    out_ref[out_ref.shape[0] - 8 :] = jnp.where(lane == 0, jnp.sum(remain * remain), cross)
 
 
 def first_kernel(n_dp, *refs):
     terms, refs = refs[:n_dp], refs[n_dp:]
-    limit_ref, *attention, remain_ref, sums_ref, out_ref = refs
+    limit_ref, *attention, remain_ref, out_ref = refs
     grads = total_of([term[...] for term in terms])
     remain = -grads[: remain_ref.shape[0]]
     remain_ref[...] = remain
-    put_sums(sums_ref, remain, None)
+    put_sums(out_ref, remain, None)
     tangent_of(remain, limit_ref[0], *attention, out_ref)
 
 
@@ -358,11 +396,10 @@
     return pl.pallas_call(
         functools.partial(first_kernel, len(terms)),
         in_specs=[VMEM] * len(terms) + [SMEM] + [VMEM] * 5,
-        out_specs=[VMEM] * 3,
+        out_specs=[VMEM] * 2,
         out_shape=[
             jax.ShapeDtypeStruct((2 * rank, inner), F32),
-            jax.ShapeDtypeStruct((8, 128), F32),
-            jax.ShapeDtypeStruct((length, inner), F32),
+            jax.ShapeDtypeStruct((length + 8, inner), F32),
         ],
         compiler_params=pltpu.CompilerParams(vmem_limit_bytes=LIMIT),
     )(*terms, limit, *attention)
@@ -401,14 +438,14 @@
         return
     limit_ref, *refs = refs
     attention, refs = refs[:5], refs[5:]
-    next_remain, next_before, next_newton, next_direction, next_image, next_sums, out_ref = refs
+    next_remain, next_before, next_newton, next_direction, next_image, out_ref = refs
     lane = lax.broadcasted_iota(jnp.int32, next_before.shape, 1)
     next_remain[...] = remain
     next_before[...] = jnp.where(lane == 0, norm, curv)
     next_newton[...] = newton
     next_direction[...] = direction
     next_image[...] = image
-    put_sums(next_sums, remain, image)
+    put_sums(out_ref, remain, image)
     tangent_of(remain, limit_ref[0], *attention, out_ref)
 
 
@@ -425,8 +462,8 @@
         args += [limit, *attention]
         specs += [SMEM] + [VMEM] * 5
         length = attention[1].shape[0]
-        shapes = [matrix, scalars, matrix, matrix, matrix, scalars]
-        shapes.append(jax.ShapeDtypeStruct((length, inner), F32))
+        shapes = [matrix, scalars, matrix, matrix, matrix]
+        shapes.append(jax.ShapeDtypeStruct((length + 8, inner), F32))
     return pl.pallas_call(
         functools.partial(step_kernel, len(terms), token_count, index, last),
         in_specs=specs,
@@ -455,6 +492,7 @@
     n_dp = lax.axis_size("dp")
     n_chip = lax.axis_size("chip")
     core = lax.axis_index("core")
+    chip = lax.axis_index("chip")
     token_count = length * n_dp
     half = width // 2
 
@@ -462,22 +500,18 @@
         return lax.ppermute(part, "core", [(0, 1), (1, 0)])
 
     def data_terms(part):
-        return [part] + [
-            lax.ppermute(part, "dp", [(d, d ^ step) for d in range(n_dp)])
-            for step in range(1, n_dp)
-        ]
-
-    def head_sum(part):
-        part = part + swap(part)
         step = 1
-        while step < n_chip:
-            part = part + lax.ppermute(part, "chip", [(c, c ^ step) for c in range(n_chip)])
+        while 2 * step < n_dp:
+            part = part + lax.ppermute(part, "dp", [(d, d ^ step) for d in range(n_dp)])
             step *= 2
-        return part
+        return [part, lax.ppermute(part, "dp", [(d, d ^ step) for d in range(n_dp)])]
 
     where = core.astype(jnp.int32)[None]
     sent = lax.dynamic_slice_in_dim(w_out, (1 - core) * half, half, 1).astype(F32)
-    pair = pair_weights(where, w_out, swap(sent))
+    other_w = swap(sent)
+    cols = half // CHUNKS
+    gap = lax.dynamic_slice_in_dim(inputs, core * half, half, 1).astype(F32)
+    gap = gap - lax.dynamic_slice_in_dim(targets, core * half, half, 1).astype(F32)
 
     soft, key, value, down_q, down_v, mixed = project(
         lengths, inputs, ln_gain, ln_bias, query_weight, w_key, value_weight, down_query,
@@ -485,21 +519,74 @@
     )
     attention = (soft, key, value, down_q, down_v)
 
-    def product(rows, gap):
-        total = lax.psum(spread(rows, swap(rows), pair), "chip")
-        own, other = gather(where, total, pair, gap)
+    sums_in, sums_out = line_hops(n_chip)
+    hops = sums_in + sums_out
+    takes = []
+    for hop in sums_out:
+        inside = jnp.zeros((), jnp.bool_)
+        for _, to in hop:
+            inside = inside | (chip == to)
+        takes.append(inside.astype(jnp.int32)[None])
+
+    def product(rows, pairs):
+        got_rows = swap(rows)
+        first = not pairs
+        held, arriving = {}, {}
+        parts, scalars = [], None
+        token = None
+
+        def launch(k, hop):
+            arriving[k] = lax.ppermute(held[k], "chip", hops[hop])
+
+        def begin(k):
+            if first:
+                held[k], pair = first_spread(
+                    k, CHUNKS, length, where, rows, got_rows, w_out, other_w, token
+                )
+                pairs.append(pair)
+            else:
+                held[k] = spread(k, length, rows, got_rows, pairs[k], token)
+            launch(k, 0)
+            return held[k]
+
+        for k in range(AHEAD):
+            token = begin(k)
+        for tick in range(CHUNKS + len(hops) - 1):
+            for stage in range(len(hops)):
+                k = tick - stage
+                if 0 <= k < CHUNKS:
+                    if stage == len(hops) - 1:
+                        out = gather(
+                            k, takes[-1], arriving[k], held[k], pairs[k], parts, lengths,
+                            gap[:, k * cols : (k + 1) * cols] if first else None, token,
+                        )
+                        parts = list(out[:2])
+                        scalars = out[2] if k == 0 else scalars
+                        token = parts[0]
+                        continue
+                    if stage < len(sums_in):
+                        held[k] = add(held[k], arriving[k], token)
+                    else:
+                        flag = takes[stage - len(sums_in)]
+                        held[k] = choose(flag, arriving[k], held[k], token)
+                    token = held[k]
+                    launch(k, stage + 1)
+                if stage == 0 and tick + AHEAD < CHUNKS:
+                    token = begin(tick + AHEAD)
+        own, other = parts
         share = ADAPTER_SCALE / token_count
-        return data_terms(cotangent(share, lengths, own, other, swap(other), attention))
-
-    terms = product(mixed, (lengths, inputs, targets))
-    remain, sums, rows = first_step(terms, lengths, attention)
+        part = cotangent(share, lengths, own, other, swap(other), attention)
+        return data_terms(part), scalars
+
+    pairs = []
+    terms, _ = product(mixed, pairs)
+    remain, rows = first_step(terms, lengths, attention)
     state = ()
     for index in range(CG_STEPS):
-        sums = head_sum(sums)
-        terms = product(rows, None)
+        terms, sums = product(rows, pairs)
         out = cg_step(index, token_count, terms, sums, remain, state, lengths, attention)
         if index < CG_STEPS - 1:
-            remain, *state, sums, rows = out
+            remain, *state, rows = out
     return tuple(out)
 
 

time: 437 us -> 345 us (0.79)
  waiting for transfers between devices: 311 us -> 161 us
  starting transfers between devices: 21.8 us -> 115 us
  local copies, waits for them, and re-layouts: 34.9 us -> 7.54 us
  between operations: 14.7 us -> 2.31 us
    psum x4 -> x0, waiting for transfers between devices: 275 us -> none  [product(): total = lax.psum(spread(rows, swap(rows), pair), 'chip')]
    ppermute x6 -> x52, waiting for transfers between devices: 18 us -> 139 us  [the longest x48 128 us: launch(): arriving[k] = lax.ppermute(held[k], 'chip', hops[hop])]
    ppermute x6 -> x52, starting transfers between devices: 6.31 us -> 107 us  [the longest x48 101 us: launch(): arriving[k] = lax.ppermute(held[k], 'chip', hops[hop])]
    unnamed x62 -> x42, local copies, waits for them, and re-layouts: 34.9 us -> 7.41 us
    pallas_call x1, Pallas kernels: 8.44 us -> 16.4 us  [project(): pl.pallas_call(project_kernel, grid=(width // DEPTH,), in_specs=[SMEM, pl...]
    ppermute x12 -> x4, starting transfers between devices: 14 us -> 6.34 us  [data_terms(): lax.ppermute(part, 'dp', [(d, d ^ step) for d in range(n_dp)])]
    ppermute x12 -> x4, waiting for transfers between devices: 4.6 us -> 10.8 us  [data_terms(): lax.ppermute(part, 'dp', [(d, d ^ step) for d in range(n_dp)])]
    pallas_call x9 -> x64, Pallas kernels: 31.2 us -> 27.5 us  [the longest x60 19 us: call(): pl.pallas_call(body, in_specs=[SMEM] * len(scalars) + [VMEM] * len(ins) +...]
  transfers between devices with their start and end apart: 34 -> 65, of which waited for: 23 -> 42; matrix products, arithmetic and copies ran while one was open for 1% -> 1% of each run, Pallas kernels for 3% -> 11%
where the time goes in v2:
time: 345 us; the launch traced here: 344 us
  waiting for transfers between devices  161 us (47%)
  starting transfers between devices  115 us (33%)
  Pallas kernels  53.2 us (15%)
  local copies, waits for them, and re-layouts  7.54 us (2%)
  other arithmetic  4.72 us (1%)
    ppermute x48, waiting for transfers between devices, launch(): arriving[k] = lax.ppermute(held[k], 'chip', hops[hop])  128 us
    ppermute x48, starting transfers between devices, launch(): arriving[k] = lax.ppermute(held[k], 'chip', hops[hop])  101 us
    pallas_call x60, Pallas kernels, call(): pl.pallas_call(body, in_specs=[SMEM] * len(scalars) + [VMEM] * len(ins) +...  19 us
    pallas_call x1, Pallas kernels, project(): pl.pallas_call(project_kernel, grid=(width // DEPTH,), in_specs=[SMEM, pl...  16.4 us
    ppermute x9, waiting for transfers between devices, swap(): return lax.ppermute(part, 'core', [(0, 1), (1, 0)])  11.7 us
    ppermute x4, waiting for transfers between devices, data_terms(): lax.ppermute(part, 'dp', [(d, d ^ step) for d in range(n_dp)])  10.8 us
    ppermute x4, waiting for transfers between devices, data_terms(): part = part + lax.ppermute(part, 'dp', [(d, d ^ step) for d in range(n_dp)])  10.8 us
    pallas_call x4, Pallas kernels, first_spread(): pl.pallas_call(functools.partial(first_spread_kernel, index == 0, length)...  8.48 us
  transfers between devices with their start and end apart: 65, of which 42 were waited for; matrix products, arithmetic and copies ran while one was open for 1% of the time, Pallas kernels for 11%

profile of v2, /device:TPU:0, one launch (start us, length us, event | category | flops | bytes accessed | tf_op | source)
XLA Modules:
  0.0 343.7 jit_solution(10484331707499322863)
XLA Ops:
  0.6 4.5 %dynamic-slice_convert_fusion = f32[384,3072]{1,0:T(8,128)} fusion(bf16[384,6144]{1,0:T(8,128)(2,1)} %w_ref.7, s32[]{:T(128)S(6)} %select_n.7), kind=kLoop, calls=%fused_computation | loop fusion | flops 1179648 | bytes 7077892 | tf_op jit(solution)/shard_map/convert_element_type | solution.py:510
  9.2 16.4 %shard_map.156 = (f32[3,128,128]{2,1,0:T(8,128)}, bf16[128,384]{1,0:T(8,128)(2,1)}, bf16[128,384]{1,0:T(8,128)(2,1)}, f32[128,16]{1,0:T(8,128)}, f32[128,16]{1,0:T(8,128)}, /*index=5*/f32[136,384]{1,0:T(8,128)}) custom-call(s32[1]{0:T(128)S(6)} %copy.19.limit_ref.refs_1_.refs_2_.refs_4_.refs_8_, bf16[128,6144]{1,0:T(8,128)(2,1)} %x_ref.1, ...), custom_call_target="tpu_custom_call" | custom-call | flops 1811939328 | bytes 14155776 | tf_op jit(solution)/shard_map/pallas_call | solution.py:125
  28.3 1.8 shard_map.157
  31.2 4.6 %collective-permute-start.3 = (f32[136,768]{1,0:T(8,128)S(1)}, f32[136,768]{1,0:T(8,128)S(1)}, u32[]{:S(2)}, u32[]{:S(2)}) collective-permute-start(f32[136,768]{1,0:T(8,128)S(1)} %get-tuple-element.68.refs_0_), channel_id=1, source_target_pairs={{0,2},{6,4},{1,3},{7,5},{8,10},{14,12},{9,11},{15,13},{16,18},{22,... | collective-permute-start | bytes 1253384 | tf_op jit(solution)/shard_map/ppermute | solution.py:539
  35.9 2.3 copy-done
  38.2 1.7 shard_map.158
  39.9 1.7 collective-permute-start.2
  41.6 4.1 %collective-permute-done.3.refs_1_ = f32[136,768]{1,0:T(8,128)S(1)} collective-permute-done((f32[136,768]{1,0:T(8,128)S(1)}, f32[136,768]{1,0:T(8,128)S(1)}, u32[]{:S(2)}, u32[]{:S(2)}) %collective-permute-start.3) | collective-permute-done | bytes 417824 | tf_op jit(solution)/shard_map/ppermute | solution.py:539
  46.8 2.5 shard_map.160
  49.3 7.9 %collective-permute-start.8 = (f32[128,768]{1,0:T(8,128)}, f32[128,768]{1,0:T(8,128)}, u32[]{:S(2)}, u32[]{:S(2)}) collective-permute-start(f32[128,768]{1,0:T(8,128)} %get-tuple-element.70.refs_2_.refs_0_), channel_id=1, source_target_pairs={{0,2},{6,4},{1,3},{7,5},{8,10},{14,12},{9,11},{15,13},{16,18},{22,... | collective-permute-start | bytes 1179656 | tf_op jit(solution)/shard_map/ppermute | solution.py:539
  58.7 2.5 shard_map.162
  61.2 3.7 %collective-permute-start.4 = (f32[128,768]{1,0:T(8,128)}, f32[128,768]{1,0:T(8,128)}, u32[]{:S(2)}, u32[]{:S(2)}) collective-permute-start(f32[128,768]{1,0:T(8,128)} %get-tuple-element.71.refs_2_.refs_0_), channel_id=1, source_target_pairs={{0,2},{6,4},{1,3},{7,5},{8,10},{14,12},{9,11},{15,13},{16,18},{22,... | collective-permute-start | bytes 1179656 | tf_op jit(solution)/shard_map/ppermute | solution.py:539
  71.5 9.0 %collective-permute-done.6.refs_2_ = f32[136,768]{1,0:T(8,128)} collective-permute-done((f32[136,768]{1,0:T(8,128)}, f32[136,768]{1,0:T(8,128)}, u32[]{:S(2)}, u32[]{:S(2)}) %collective-permute-start.6) | collective-permute-done | bytes 417824 | tf_op jit(solution)/shard_map/ppermute | solution.py:539
  80.5 2.1 shard_map.166
  85.9 2.3 collective-permute-done.10.refs_2_
  90.1 8.4 %collective-permute-done.13.refs_2_ = f32[128,768]{1,0:T(8,128)S(1)} collective-permute-done((f32[128,768]{1,0:T(8,128)S(1)}, f32[128,768]{1,0:T(8,128)S(1)}, u32[]{:S(2)}, u32[]{:S(2)}) %collective-permute-start.13) | collective-permute-done | bytes 393248 | tf_op jit(solution)/shard_map/ppermute | solution.py:539
  99.1 4.5 %collective-permute-done.12.refs_2_ = f32[128,768]{1,0:T(8,128)S(1)} collective-permute-done((f32[128,768]{1,0:T(8,128)S(1)}, f32[128,768]{1,0:T(8,128)S(1)}, u32[]{:S(2)}, u32[]{:S(2)}) %collective-permute-start.12) | collective-permute-done | bytes 393248 | tf_op jit(solution)/shard_map/ppermute | solution.py:539
  108.8 2.7 collective-permute-done.15
  111.5 1.6 collective-permute-start.16
  113.1 2.7 collective-permute-done.16.refs_1_
  121.5 8.3 %collective-permute-done.19.refs_1_ = f32[136,768]{1,0:T(8,128)S(1)} collective-permute-done((f32[136,768]{1,0:T(8,128)S(1)}, f32[136,768]{1,0:T(8,128)S(1)}, u32[]{:S(2)}, u32[]{:S(2)}) %collective-permute-start.19) | collective-permute-done | bytes 417824 | tf_op jit(solution)/shard_map/ppermute | solution.py:539
  130.9 6.1 %collective-permute-start.24 = (f32[128,768]{1,0:T(8,128)S(1)}, f32[128,768]{1,0:T(8,128)S(1)}, u32[]{:S(2)}, u32[]{:S(2)}) collective-permute-start(f32[128,768]{1,0:T(8,128)S(1)} %shard_map.178.refs_2_.refs_0_), channel_id=1, source_target_pairs={{0,2},{6,4},{1,3},{7,5},{8,10},{14,12},{9,11},{15,13},{16,18},{22,... | collective-permute-start | bytes 1179656 | tf_op jit(solution)/shard_map/ppermute | solution.py:539
  140.9 7.5 %collective-permute-start.20 = (f32[128,768]{1,0:T(8,128)S(1)}, f32[128,768]{1,0:T(8,128)S(1)}, u32[]{:S(2)}, u32[]{:S(2)}) collective-permute-start(f32[128,768]{1,0:T(8,128)S(1)} %shard_map.180.refs_2_.refs_0_), channel_id=1, source_target_pairs={{0,2},{6,4},{1,3},{7,5},{8,10},{14,12},{9,11},{15,13},{16,18},{22,... | collective-permute-start | bytes 1179656 | tf_op jit(solution)/shard_map/ppermute | solution.py:539
  150.5 3.1 collective-permute-done.22.refs_2_
  156.5 5.5 %collective-permute-done.26.refs_2_ = f32[128,768]{1,0:T(8,128)S(1)} collective-permute-done((f32[128,768]{1,0:T(8,128)S(1)}, f32[128,768]{1,0:T(8,128)S(1)}, u32[]{:S(2)}, u32[]{:S(2)}) %collective-permute-start.26) | collective-permute-done | bytes 393248 | tf_op jit(solution)/shard_map/ppermute | solution.py:539
  163.9 7.1 %collective-permute-done.29.refs_2_ = f32[128,768]{1,0:T(8,128)S(1)} collective-permute-done((f32[128,768]{1,0:T(8,128)S(1)}, f32[128,768]{1,0:T(8,128)S(1)}, u32[]{:S(2)}, u32[]{:S(2)}) %collective-permute-start.29) | collective-permute-done | bytes 393248 | tf_op jit(solution)/shard_map/ppermute | solution.py:539
  171.5 7.9 %collective-permute-done.28.refs_2_ = f32[128,768]{1,0:T(8,128)S(1)} collective-permute-done((f32[128,768]{1,0:T(8,128)S(1)}, f32[128,768]{1,0:T(8,128)S(1)}, u32[]{:S(2)}, u32[]{:S(2)}) %collective-permute-start.28) | collective-permute-done | bytes 393248 | tf_op jit(solution)/shard_map/ppermute | solution.py:539
  184.5 2.7 collective-permute-done.31
  188.7 2.8 collective-permute-done.32.refs_1_
  197.3 8.3 %collective-permute-done.35.refs_1_ = f32[136,768]{1,0:T(8,128)S(1)} collective-permute-done((f32[136,768]{1,0:T(8,128)S(1)}, f32[136,768]{1,0:T(8,128)S(1)}, u32[]{:S(2)}, u32[]{:S(2)}) %collective-permute-start.35) | collective-permute-done | bytes 417824 | tf_op jit(solution)/shard_map/ppermute | solution.py:539
  206.7 6.4 %collective-permute-start.40 = (f32[128,768]{1,0:T(8,128)S(1)}, f32[128,768]{1,0:T(8,128)S(1)}, u32[]{:S(2)}, u32[]{:S(2)}) collective-permute-start(f32[128,768]{1,0:T(8,128)S(1)} %shard_map.196.refs_2_.refs_0_), channel_id=1, source_target_pairs={{0,2},{6,4},{1,3},{7,5},{8,10},{14,12},{9,11},{15,13},{16,18},{22,... | collective-permute-start | bytes 1179656 | tf_op jit(solution)/shard_map/ppermute | solution.py:539
  216.5 7.6 %collective-permute-start.36 = (f32[128,768]{1,0:T(8,128)S(1)}, f32[128,768]{1,0:T(8,128)S(1)}, u32[]{:S(2)}, u32[]{:S(2)}) collective-permute-start(f32[128,768]{1,0:T(8,128)S(1)} %shard_map.198.refs_2_.refs_0_), channel_id=1, source_target_pairs={{0,2},{6,4},{1,3},{7,5},{8,10},{14,12},{9,11},{15,13},{16,18},{22,... | collective-permute-start | bytes 1179656 | tf_op jit(solution)/shard_map/ppermute | solution.py:539
  226.2 3.1 collective-permute-done.38.refs_2_
  232.3 5.4 %collective-permute-done.42.refs_2_ = f32[128,768]{1,0:T(8,128)S(1)} collective-permute-done((f32[128,768]{1,0:T(8,128)S(1)}, f32[128,768]{1,0:T(8,128)S(1)}, u32[]{:S(2)}, u32[]{:S(2)}) %collective-permute-start.42) | collective-permute-done | bytes 393248 | tf_op jit(solution)/shard_map/ppermute | solution.py:539
  239.6 7.1 %collective-permute-done.45.refs_2_ = f32[128,768]{1,0:T(8,128)S(1)} collective-permute-done((f32[128,768]{1,0:T(8,128)S(1)}, f32[128,768]{1,0:T(8,128)S(1)}, u32[]{:S(2)}, u32[]{:S(2)}) %collective-permute-start.45) | collective-permute-done | bytes 393248 | tf_op jit(solution)/shard_map/ppermute | solution.py:539
  247.1 8.0 %collective-permute-done.44.refs_2_ = f32[128,768]{1,0:T(8,128)S(1)} collective-permute-done((f32[128,768]{1,0:T(8,128)S(1)}, f32[128,768]{1,0:T(8,128)S(1)}, u32[]{:S(2)}, u32[]{:S(2)}) %collective-permute-start.44) | collective-permute-done | bytes 393248 | tf_op jit(solution)/shard_map/ppermute | solution.py:539
  260.2 2.7 collective-permute-done.47
  264.4 2.7 collective-permute-done.48.refs_1_
  273.0 8.3 %collective-permute-done.51.refs_1_ = f32[136,768]{1,0:T(8,128)S(1)} collective-permute-done((f32[136,768]{1,0:T(8,128)S(1)}, f32[136,768]{1,0:T(8,128)S(1)}, u32[]{:S(2)}, u32[]{:S(2)}) %collective-permute-start.51) | collective-permute-done | bytes 417824 | tf_op jit(solution)/shard_map/ppermute | solution.py:539
  282.4 6.5 %collective-permute-start.56 = (f32[128,768]{1,0:T(8,128)S(1)}, f32[128,768]{1,0:T(8,128)S(1)}, u32[]{:S(2)}, u32[]{:S(2)}) collective-permute-start(f32[128,768]{1,0:T(8,128)S(1)} %shard_map.214.refs_2_.refs_0_), channel_id=1, source_target_pairs={{0,2},{6,4},{1,3},{7,5},{8,10},{14,12},{9,11},{15,13},{16,18},{22,... | collective-permute-start | bytes 1179656 | tf_op jit(solution)/shard_map/ppermute | solution.py:539
  292.2 7.6 %collective-permute-start.52 = (f32[128,768]{1,0:T(8,128)S(1)}, f32[128,768]{1,0:T(8,128)S(1)}, u32[]{:S(2)}, u32[]{:S(2)}) collective-permute-start(f32[128,768]{1,0:T(8,128)S(1)} %shard_map.216.refs_2_.refs_0_), channel_id=1, source_target_pairs={{0,2},{6,4},{1,3},{7,5},{8,10},{14,12},{9,11},{15,13},{16,18},{22,... | collective-permute-start | bytes 1179656 | tf_op jit(solution)/shard_map/ppermute | solution.py:539
  302.2 2.9 collective-permute-done.54.refs_2_
  308.0 5.4 %collective-permute-done.58.refs_2_ = f32[128,768]{1,0:T(8,128)S(1)} collective-permute-done((f32[128,768]{1,0:T(8,128)S(1)}, f32[128,768]{1,0:T(8,128)S(1)}, u32[]{:S(2)}, u32[]{:S(2)}) %collective-permute-start.58) | collective-permute-done | bytes 393248 | tf_op jit(solution)/shard_map/ppermute | solution.py:539
  315.3 7.1 %collective-permute-done.61.refs_2_ = f32[128,768]{1,0:T(8,128)S(1)} collective-permute-done((f32[128,768]{1,0:T(8,128)S(1)}, f32[128,768]{1,0:T(8,128)S(1)}, u32[]{:S(2)}, u32[]{:S(2)}) %collective-permute-start.61) | collective-permute-done | bytes 393248 | tf_op jit(solution)/shard_map/ppermute | solution.py:539
  322.9 8.0 %collective-permute-done.60.refs_2_ = f32[128,768]{1,0:T(8,128)S(1)} collective-permute-done((f32[128,768]{1,0:T(8,128)S(1)}, f32[128,768]{1,0:T(8,128)S(1)}, u32[]{:S(2)}, u32[]{:S(2)}) %collective-permute-start.60) | collective-permute-done | bytes 393248 | tf_op jit(solution)/shard_map/ppermute | solution.py:539
  335.9 2.7 collective-permute-done.63
  338.6 1.6 collective-permute-start.64
  340.3 2.7 collective-permute-done.64.refs_1_
  (205 shorter events, 99.2 us)
Async XLA Ops:
  5.1 22.2 %collective-permute-start.1 = (f32[384,3072]{1,0:T(8,128)}, f32[384,3072]{1,0:T(8,128)}, u32[]{:S(2)}, u32[]{:S(2)}) collective-permute-start(f32[384,3072]{1,0:T(8,128)} %dynamic-slice_convert_fusion), channel_id=1, source_target_pairs={{0,1},{1,0},{2,3},{3,2},{4,5},{5,4},{6,7},{7,6},{8,9},{9,8},{10,11... | collective-permute-start | bytes 14155784 | tf_op jit(solution)/shard_map/ppermute | solution.py:500
  31.2 14.6 %collective-permute-start.3 = (f32[136,768]{1,0:T(8,128)S(1)}, f32[136,768]{1,0:T(8,128)S(1)}, u32[]{:S(2)}, u32[]{:S(2)}) collective-permute-start(f32[136,768]{1,0:T(8,128)S(1)} %get-tuple-element.68.refs_0_), channel_id=1, source_target_pairs={{0,2},{6,4},{1,3},{7,5},{8,10},{14,12},{9,11},{15,13},{16,18},{22,... | collective-permute-start | bytes 1253384 | tf_op jit(solution)/shard_map/ppermute | solution.py:539
  39.9 17.2 %collective-permute-start.2 = (f32[128,768]{1,0:T(8,128)S(1)}, f32[128,768]{1,0:T(8,128)S(1)}, u32[]{:S(2)}, u32[]{:S(2)}) collective-permute-start(f32[128,768]{1,0:T(8,128)S(1)} %get-tuple-element.69.refs_2_.refs_0_), channel_id=1, source_target_pairs={{0,2},{6,4},{1,3},{7,5},{8,10},{14,12},{9,11},{15,13},{16,18},{22,... | collective-permute-start | bytes 1179656 | tf_op jit(solution)/shard_map/ppermute | solution.py:539
  45.8 19.0 %collective-permute-start.5 = (f32[136,768]{1,0:T(8,128)S(1)}, f32[136,768]{1,0:T(8,128)S(1)}, u32[]{:S(2)}, u32[]{:S(2)}) collective-permute-start(f32[136,768]{1,0:T(8,128)S(1)} %shard_map.159.refs_0_), channel_id=1, source_target_pairs={{2,4},{4,2},{3,5},{5,3},{10,12},{12,10},{11,13},{13,11},{18,20},{2... | collective-permute-start | bytes 1253384 | tf_op jit(solution)/shard_map/ppermute | solution.py:539
  49.3 17.9 %collective-permute-start.8 = (f32[128,768]{1,0:T(8,128)}, f32[128,768]{1,0:T(8,128)}, u32[]{:S(2)}, u32[]{:S(2)}) collective-permute-start(f32[128,768]{1,0:T(8,128)} %get-tuple-element.70.refs_2_.refs_0_), channel_id=1, source_target_pairs={{0,2},{6,4},{1,3},{7,5},{8,10},{14,12},{9,11},{15,13},{16,18},{22,... | collective-permute-start | bytes 1179656 | tf_op jit(solution)/shard_map/ppermute | solution.py:539
  57.2 11.9 %collective-permute-start.7 = (f32[128,768]{1,0:T(8,128)S(1)}, f32[128,768]{1,0:T(8,128)}, u32[]{:S(2)}, u32[]{:S(2)}) collective-permute-start(f32[128,768]{1,0:T(8,128)S(1)} %shard_map.161.refs_0_), channel_id=1, source_target_pairs={{2,4},{4,2},{3,5},{5,3},{10,12},{12,10},{11,13},{13,11},{18,20},{2... | collective-permute-start | bytes 1179656 | tf_op jit(solution)/shard_map/ppermute | solution.py:539
  61.2 21.4 %collective-permute-start.4 = (f32[128,768]{1,0:T(8,128)}, f32[128,768]{1,0:T(8,128)}, u32[]{:S(2)}, u32[]{:S(2)}) collective-permute-start(f32[128,768]{1,0:T(8,128)} %get-tuple-element.71.refs_2_.refs_0_), channel_id=1, source_target_pairs={{0,2},{6,4},{1,3},{7,5},{8,10},{14,12},{9,11},{15,13},{16,18},{22,... | collective-permute-start | bytes 1179656 | tf_op jit(solution)/shard_map/ppermute | solution.py:539
  65.7 14.8 %collective-permute-start.6 = (f32[136,768]{1,0:T(8,128)}, f32[136,768]{1,0:T(8,128)}, u32[]{:S(2)}, u32[]{:S(2)}) collective-permute-start(f32[136,768]{1,0:T(8,128)} %shard_map.163.refs_2_.refs_3_), channel_id=1, source_target_pairs={{2,0},{4,6},{3,1},{5,7},{10,8},{12,14},{11,9},{13,15},{18,16},{20,... | collective-permute-start | bytes 1253384 | tf_op jit(solution)/shard_map/ppermute | solution.py:539
  68.3 16.3 %collective-permute-start.11 = (f32[128,768]{1,0:T(8,128)S(1)}, f32[128,768]{1,0:T(8,128)S(1)}, u32[]{:S(2)}, u32[]{:S(2)}) collective-permute-start(f32[128,768]{1,0:T(8,128)S(1)} %shard_map.164.refs_2_.refs_0_), channel_id=1, source_target_pairs={{2,4},{4,2},{3,5},{5,3},{10,12},{12,10},{11,13},{13,11},{18,20},{2... | collective-permute-start | bytes 1179656 | tf_op jit(solution)/shard_map/ppermute | solution.py:539
  70.2 18.1 %collective-permute-start.10 = (f32[128,768]{1,0:T(8,128)S(1)}, f32[128,768]{1,0:T(8,128)S(1)}, u32[]{:S(2)}, u32[]{:S(2)}) collective-permute-start(f32[128,768]{1,0:T(8,128)S(1)} %shard_map.165.refs_6_.refs_3_), channel_id=1, source_target_pairs={{2,0},{4,6},{3,1},{5,7},{10,8},{12,14},{11,9},{13,15},{18,16},{20,... | collective-permute-start | bytes 1179656 | tf_op jit(solution)/shard_map/ppermute | solution.py:539
  84.6 13.9 %collective-permute-start.13 = (f32[128,768]{1,0:T(8,128)S(1)}, f32[128,768]{1,0:T(8,128)S(1)}, u32[]{:S(2)}, u32[]{:S(2)}) collective-permute-start(f32[128,768]{1,0:T(8,128)S(1)} %shard_map.168.refs_8_.refs_3_), channel_id=1, source_target_pairs={{2,0},{4,6},{3,1},{5,7},{10,8},{12,14},{11,9},{13,15},{18,16},{20,... | collective-permute-start | bytes 1179656 | tf_op jit(solution)/shard_map/ppermute | solution.py:539
  88.8 14.7 %collective-permute-start.12 = (f32[128,768]{1,0:T(8,128)S(1)}, f32[128,768]{1,0:T(8,128)S(1)}, u32[]{:S(2)}, u32[]{:S(2)}) collective-permute-start(f32[128,768]{1,0:T(8,128)S(1)} %shard_map.170.refs_8_.refs_3_), channel_id=1, source_target_pairs={{2,0},{4,6},{3,1},{5,7},{10,8},{12,14},{11,9},{13,15},{18,16},{20,... | collective-permute-start | bytes 1179656 | tf_op jit(solution)/shard_map/ppermute | solution.py:539
  118.4 11.4 %collective-permute-start.19 = (f32[136,768]{1,0:T(8,128)S(1)}, f32[136,768]{1,0:T(8,128)S(1)}, u32[]{:S(2)}, u32[]{:S(2)}) collective-permute-start(f32[136,768]{1,0:T(8,128)S(1)} %shard_map.175.refs_3_.refs_0_), channel_id=1, source_target_pairs={{0,2},{6,4},{1,3},{7,5},{8,10},{14,12},{9,11},{15,13},{16,18},{22,... | collective-permute-start | bytes 1253384 | tf_op jit(solution)/shard_map/ppermute | solution.py:539
  120.2 18.0 %collective-permute-start.18 = (f32[128,768]{1,0:T(8,128)S(1)}, f32[128,768]{1,0:T(8,128)S(1)}, u32[]{:S(2)}, u32[]{:S(2)}) collective-permute-start(f32[128,768]{1,0:T(8,128)S(1)} %shard_map.176.refs_2_.refs_0_), channel_id=1, source_target_pairs={{0,2},{6,4},{1,3},{7,5},{8,10},{14,12},{9,11},{15,13},{16,18},{22,... | collective-permute-start | bytes 1179656 | tf_op jit(solution)/shard_map/ppermute | solution.py:539
  129.9 9.6 %collective-permute-start.21 = (f32[136,768]{1,0:T(8,128)S(1)}, f32[136,768]{1,0:T(8,128)S(1)}, u32[]{:S(2)}, u32[]{:S(2)}) collective-permute-start(f32[136,768]{1,0:T(8,128)S(1)} %shard_map.177.refs_3_.refs_0_), channel_id=1, source_target_pairs={{2,4},{4,2},{3,5},{5,3},{10,12},{12,10},{11,13},{13,11},{18,20},{2... | collective-permute-start | bytes 1253384 | tf_op jit(solution)/shard_map/ppermute | solution.py:539
  130.9 17.5 %collective-permute-start.24 = (f32[128,768]{1,0:T(8,128)S(1)}, f32[128,768]{1,0:T(8,128)S(1)}, u32[]{:S(2)}, u32[]{:S(2)}) collective-permute-start(f32[128,768]{1,0:T(8,128)S(1)} %shard_map.178.refs_2_.refs_0_), channel_id=1, source_target_pairs={{0,2},{6,4},{1,3},{7,5},{8,10},{14,12},{9,11},{15,13},{16,18},{22,... | collective-permute-start | bytes 1179656 | tf_op jit(solution)/shard_map/ppermute | solution.py:539
  138.3 10.8 %collective-permute-start.23 = (f32[128,768]{1,0:T(8,128)S(1)}, f32[128,768]{1,0:T(8,128)S(1)}, u32[]{:S(2)}, u32[]{:S(2)}) collective-permute-start(f32[128,768]{1,0:T(8,128)S(1)} %shard_map.179.refs_3_.refs_0_), channel_id=1, source_target_pairs={{2,4},{4,2},{3,5},{5,3},{10,12},{12,10},{11,13},{13,11},{18,20},{2... | collective-permute-start | bytes 1179656 | tf_op jit(solution)/shard_map/ppermute | solution.py:539
  139.6 14.0 %collective-permute-start.22 = (f32[136,768]{1,0:T(8,128)S(1)}, f32[136,768]{1,0:T(8,128)S(1)}, u32[]{:S(2)}, u32[]{:S(2)}) collective-permute-start(f32[136,768]{1,0:T(8,128)S(1)} %shard_map.181.refs_2_.refs_3_), channel_id=1, source_target_pairs={{2,0},{4,6},{3,1},{5,7},{10,8},{12,14},{11,9},{13,15},{18,16},{20,... | collective-permute-start | bytes 1253384 | tf_op jit(solution)/shard_map/ppermute | solution.py:539
  140.9 13.6 %collective-permute-start.20 = (f32[128,768]{1,0:T(8,128)S(1)}, f32[128,768]{1,0:T(8,128)S(1)}, u32[]{:S(2)}, u32[]{:S(2)}) collective-permute-start(f32[128,768]{1,0:T(8,128)S(1)} %shard_map.180.refs_2_.refs_0_), channel_id=1, source_target_pairs={{0,2},{6,4},{1,3},{7,5},{8,10},{14,12},{9,11},{15,13},{16,18},{22,... | collective-permute-start | bytes 1179656 | tf_op jit(solution)/shard_map/ppermute | solution.py:539
  148.4 6.8 %collective-permute-start.27 = (f32[128,768]{1,0:T(8,128)S(1)}, f32[128,768]{1,0:T(8,128)S(1)}, u32[]{:S(2)}, u32[]{:S(2)}) collective-permute-start(f32[128,768]{1,0:T(8,128)S(1)} %shard_map.182.refs_2_.refs_0_), channel_id=1, source_target_pairs={{2,4},{4,2},{3,5},{5,3},{10,12},{12,10},{11,13},{13,11},{18,20},{2... | collective-permute-start | bytes 1179656 | tf_op jit(solution)/shard_map/ppermute | solution.py:539
  149.2 12.8 %collective-permute-start.26 = (f32[128,768]{1,0:T(8,128)S(1)}, f32[128,768]{1,0:T(8,128)S(1)}, u32[]{:S(2)}, u32[]{:S(2)}) collective-permute-start(f32[128,768]{1,0:T(8,128)S(1)} %shard_map.183.refs_5_.refs_3_), channel_id=1, source_target_pairs={{2,0},{4,6},{3,1},{5,7},{10,8},{12,14},{11,9},{13,15},{18,16},{20,... | collective-permute-start | bytes 1179656 | tf_op jit(solution)/shard_map/ppermute | solution.py:539
  154.5 8.0 %collective-permute-start.25 = (f32[128,768]{1,0:T(8,128)S(1)}, f32[128,768]{1,0:T(8,128)S(1)}, u32[]{:S(2)}, u32[]{:S(2)}) collective-permute-start(f32[128,768]{1,0:T(8,128)S(1)} %shard_map.185.refs_2_.refs_0_), channel_id=1, source_target_pairs={{2,4},{4,2},{3,5},{5,3},{10,12},{12,10},{11,13},{13,11},{18,20},{2... | collective-permute-start | bytes 1179656 | tf_op jit(solution)/shard_map/ppermute | solution.py:539
  155.2 15.8 %collective-permute-start.29 = (f32[128,768]{1,0:T(8,128)S(1)}, f32[128,768]{1,0:T(8,128)S(1)}, u32[]{:S(2)}, u32[]{:S(2)}) collective-permute-start(f32[128,768]{1,0:T(8,128)S(1)} %shard_map.186.refs_7_.refs_3_), channel_id=1, source_target_pairs={{2,0},{4,6},{3,1},{5,7},{10,8},{12,14},{11,9},{13,15},{18,16},{20,... | collective-permute-start | bytes 1179656 | tf_op jit(solution)/shard_map/ppermute | solution.py:539
  162.6 16.9 %collective-permute-start.28 = (f32[128,768]{1,0:T(8,128)S(1)}, f32[128,768]{1,0:T(8,128)S(1)}, u32[]{:S(2)}, u32[]{:S(2)}) collective-permute-start(f32[128,768]{1,0:T(8,128)S(1)} %shard_map.188.refs_7_.refs_3_), channel_id=1, source_target_pairs={{2,0},{4,6},{3,1},{5,7},{10,8},{12,14},{11,9},{13,15},{18,16},{20,... | collective-permute-start | bytes 1179656 | tf_op jit(solution)/shard_map/ppermute | solution.py:539
  194.1 11.4 %collective-permute-start.35 = (f32[136,768]{1,0:T(8,128)S(1)}, f32[136,768]{1,0:T(8,128)S(1)}, u32[]{:S(2)}, u32[]{:S(2)}) collective-permute-start(f32[136,768]{1,0:T(8,128)S(1)} %shard_map.193.refs_3_.refs_0_), channel_id=1, source_target_pairs={{0,2},{6,4},{1,3},{7,5},{8,10},{14,12},{9,11},{15,13},{16,18},{22,... | collective-permute-start | bytes 1253384 | tf_op jit(solution)/shard_map/ppermute | solution.py:539
  196.0 18.0 %collective-permute-start.34 = (f32[128,768]{1,0:T(8,128)S(1)}, f32[128,768]{1,0:T(8,128)S(1)}, u32[]{:S(2)}, u32[]{:S(2)}) collective-permute-start(f32[128,768]{1,0:T(8,128)S(1)} %shard_map.194.refs_2_.refs_0_), channel_id=1, source_target_pairs={{0,2},{6,4},{1,3},{7,5},{8,10},{14,12},{9,11},{15,13},{16,18},{22,... | collective-permute-start | bytes 1179656 | tf_op jit(solution)/shard_map/ppermute | solution.py:539
  205.6 9.5 %collective-permute-start.37 = (f32[136,768]{1,0:T(8,128)S(1)}, f32[136,768]{1,0:T(8,128)S(1)}, u32[]{:S(2)}, u32[]{:S(2)}) collective-permute-start(f32[136,768]{1,0:T(8,128)S(1)} %shard_map.195.refs_3_.refs_0_), channel_id=1, source_target_pairs={{2,4},{4,2},{3,5},{5,3},{10,12},{12,10},{11,13},{13,11},{18,20},{2... | collective-permute-start | bytes 1253384 | tf_op jit(solution)/shard_map/ppermute | solution.py:539
  206.7 17.4 %collective-permute-start.40 = (f32[128,768]{1,0:T(8,128)S(1)}, f32[128,768]{1,0:T(8,128)S(1)}, u32[]{:S(2)}, u32[]{:S(2)}) collective-permute-start(f32[128,768]{1,0:T(8,128)S(1)} %shard_map.196.refs_2_.refs_0_), channel_id=1, source_target_pairs={{0,2},{6,4},{1,3},{7,5},{8,10},{14,12},{9,11},{15,13},{16,18},{22,... | collective-permute-start | bytes 1179656 | tf_op jit(solution)/shard_map/ppermute | solution.py:539
  214.0 10.8 %collective-permute-start.39 = (f32[128,768]{1,0:T(8,128)S(1)}, f32[128,768]{1,0:T(8,128)S(1)}, u32[]{:S(2)}, u32[]{:S(2)}) collective-permute-start(f32[128,768]{1,0:T(8,128)S(1)} %shard_map.197.refs_3_.refs_0_), channel_id=1, source_target_pairs={{2,4},{4,2},{3,5},{5,3},{10,12},{12,10},{11,13},{13,11},{18,20},{2... | collective-permute-start | bytes 1179656 | tf_op jit(solution)/shard_map/ppermute | solution.py:539
  215.2 14.1 %collective-permute-start.38 = (f32[136,768]{1,0:T(8,128)S(1)}, f32[136,768]{1,0:T(8,128)S(1)}, u32[]{:S(2)}, u32[]{:S(2)}) collective-permute-start(f32[136,768]{1,0:T(8,128)S(1)} %shard_map.199.refs_2_.refs_3_), channel_id=1, source_target_pairs={{2,0},{4,6},{3,1},{5,7},{10,8},{12,14},{11,9},{13,15},{18,16},{20,... | collective-permute-start | bytes 1253384 | tf_op jit(solution)/shard_map/ppermute | solution.py:539
  216.5 13.7 %collective-permute-start.36 = (f32[128,768]{1,0:T(8,128)S(1)}, f32[128,768]{1,0:T(8,128)S(1)}, u32[]{:S(2)}, u32[]{:S(2)}) collective-permute-start(f32[128,768]{1,0:T(8,128)S(1)} %shard_map.198.refs_2_.refs_0_), channel_id=1, source_target_pairs={{0,2},{6,4},{1,3},{7,5},{8,10},{14,12},{9,11},{15,13},{16,18},{22,... | collective-permute-start | bytes 1179656 | tf_op jit(solution)/shard_map/ppermute | solution.py:539
  224.1 6.8 %collective-permute-start.43 = (f32[128,768]{1,0:T(8,128)S(1)}, f32[128,768]{1,0:T(8,128)S(1)}, u32[]{:S(2)}, u32[]{:S(2)}) collective-permute-start(f32[128,768]{1,0:T(8,128)S(1)} %shard_map.200.refs_2_.refs_0_), channel_id=1, source_target_pairs={{2,4},{4,2},{3,5},{5,3},{10,12},{12,10},{11,13},{13,11},{18,20},{2... | collective-permute-start | bytes 1179656 | tf_op jit(solution)/shard_map/ppermute | solution.py:539
  224.9 12.8 %collective-permute-start.42 = (f32[128,768]{1,0:T(8,128)S(1)}, f32[128,768]{1,0:T(8,128)S(1)}, u32[]{:S(2)}, u32[]{:S(2)}) collective-permute-start(f32[128,768]{1,0:T(8,128)S(1)} %shard_map.201.refs_5_.refs_3_), channel_id=1, source_target_pairs={{2,0},{4,6},{3,1},{5,7},{10,8},{12,14},{11,9},{13,15},{18,16},{20,... | collective-permute-start | bytes 1179656 | tf_op jit(solution)/shard_map/ppermute | solution.py:539
  230.2 8.0 %collective-permute-start.41 = (f32[128,768]{1,0:T(8,128)S(1)}, f32[128,768]{1,0:T(8,128)S(1)}, u32[]{:S(2)}, u32[]{:S(2)}) collective-permute-start(f32[128,768]{1,0:T(8,128)S(1)} %shard_map.203.refs_2_.refs_0_), channel_id=1, source_target_pairs={{2,4},{4,2},{3,5},{5,3},{10,12},{12,10},{11,13},{13,11},{18,20},{2... | collective-permute-start | bytes 1179656 | tf_op jit(solution)/shard_map/ppermute | solution.py:539
  231.0 15.7 %collective-permute-start.45 = (f32[128,768]{1,0:T(8,128)S(1)}, f32[128,768]{1,0:T(8,128)S(1)}, u32[]{:S(2)}, u32[]{:S(2)}) collective-permute-start(f32[128,768]{1,0:T(8,128)S(1)} %shard_map.204.refs_7_.refs_3_), channel_id=1, source_target_pairs={{2,0},{4,6},{3,1},{5,7},{10,8},{12,14},{11,9},{13,15},{18,16},{20,... | collective-permute-start | bytes 1179656 | tf_op jit(solution)/shard_map/ppermute | solution.py:539
  238.3 16.8 %collective-permute-start.44 = (f32[128,768]{1,0:T(8,128)S(1)}, f32[128,768]{1,0:T(8,128)S(1)}, u32[]{:S(2)}, u32[]{:S(2)}) collective-permute-start(f32[128,768]{1,0:T(8,128)S(1)} %shard_map.206.refs_7_.refs_3_), channel_id=1, source_target_pairs={{2,0},{4,6},{3,1},{5,7},{10,8},{12,14},{11,9},{13,15},{18,16},{20,... | collective-permute-start | bytes 1179656 | tf_op jit(solution)/shard_map/ppermute | solution.py:539
  269.9 11.4 %collective-permute-start.51 = (f32[136,768]{1,0:T(8,128)S(1)}, f32[136,768]{1,0:T(8,128)S(1)}, u32[]{:S(2)}, u32[]{:S(2)}) collective-permute-start(f32[136,768]{1,0:T(8,128)S(1)} %shard_map.211.refs_3_.refs_0_), channel_id=1, source_target_pairs={{0,2},{6,4},{1,3},{7,5},{8,10},{14,12},{9,11},{15,13},{16,18},{22,... | collective-permute-start | bytes 1253384 | tf_op jit(solution)/shard_map/ppermute | solution.py:539
  271.7 18.0 %collective-permute-start.50 = (f32[128,768]{1,0:T(8,128)S(1)}, f32[128,768]{1,0:T(8,128)S(1)}, u32[]{:S(2)}, u32[]{:S(2)}) collective-permute-start(f32[128,768]{1,0:T(8,128)S(1)} %shard_map.212.refs_2_.refs_0_), channel_id=1, source_target_pairs={{0,2},{6,4},{1,3},{7,5},{8,10},{14,12},{9,11},{15,13},{16,18},{22,... | collective-permute-start | bytes 1179656 | tf_op jit(solution)/shard_map/ppermute | solution.py:539
  281.4 9.5 %collective-permute-start.53 = (f32[136,768]{1,0:T(8,128)S(1)}, f32[136,768]{1,0:T(8,128)S(1)}, u32[]{:S(2)}, u32[]{:S(2)}) collective-permute-start(f32[136,768]{1,0:T(8,128)S(1)} %shard_map.213.refs_3_.refs_0_), channel_id=1, source_target_pairs={{2,4},{4,2},{3,5},{5,3},{10,12},{12,10},{11,13},{13,11},{18,20},{2... | collective-permute-start | bytes 1253384 | tf_op jit(solution)/shard_map/ppermute | solution.py:539
  282.4 17.4 %collective-permute-start.56 = (f32[128,768]{1,0:T(8,128)S(1)}, f32[128,768]{1,0:T(8,128)S(1)}, u32[]{:S(2)}, u32[]{:S(2)}) collective-permute-start(f32[128,768]{1,0:T(8,128)S(1)} %shard_map.214.refs_2_.refs_0_), channel_id=1, source_target_pairs={{0,2},{6,4},{1,3},{7,5},{8,10},{14,12},{9,11},{15,13},{16,18},{22,... | collective-permute-start | bytes 1179656 | tf_op jit(solution)/shard_map/ppermute | solution.py:539
  289.8 10.8 %collective-permute-start.55 = (f32[128,768]{1,0:T(8,128)S(1)}, f32[128,768]{1,0:T(8,128)S(1)}, u32[]{:S(2)}, u32[]{:S(2)}) collective-permute-start(f32[128,768]{1,0:T(8,128)S(1)} %shard_map.215.refs_3_.refs_0_), channel_id=1, source_target_pairs={{2,4},{4,2},{3,5},{5,3},{10,12},{12,10},{11,13},{13,11},{18,20},{2... | collective-permute-start | bytes 1179656 | tf_op jit(solution)/shard_map/ppermute | solution.py:539
  290.9 14.2 %collective-permute-start.54 = (f32[136,768]{1,0:T(8,128)S(1)}, f32[136,768]{1,0:T(8,128)S(1)}, u32[]{:S(2)}, u32[]{:S(2)}) collective-permute-start(f32[136,768]{1,0:T(8,128)S(1)} %shard_map.217.refs_2_.refs_3_), channel_id=1, source_target_pairs={{2,0},{4,6},{3,1},{5,7},{10,8},{12,14},{11,9},{13,15},{18,16},{20,... | collective-permute-start | bytes 1253384 | tf_op jit(solution)/shard_map/ppermute | solution.py:539
  292.2 13.7 %collective-permute-start.52 = (f32[128,768]{1,0:T(8,128)S(1)}, f32[128,768]{1,0:T(8,128)S(1)}, u32[]{:S(2)}, u32[]{:S(2)}) collective-permute-start(f32[128,768]{1,0:T(8,128)S(1)} %shard_map.216.refs_2_.refs_0_), channel_id=1, source_target_pairs={{0,2},{6,4},{1,3},{7,5},{8,10},{14,12},{9,11},{15,13},{16,18},{22,... | collective-permute-start | bytes 1179656 | tf_op jit(solution)/shard_map/ppermute | solution.py:539
  299.9 6.8 %collective-permute-start.59 = (f32[128,768]{1,0:T(8,128)S(1)}, f32[128,768]{1,0:T(8,128)S(1)}, u32[]{:S(2)}, u32[]{:S(2)}) collective-permute-start(f32[128,768]{1,0:T(8,128)S(1)} %shard_map.218.refs_2_.refs_0_), channel_id=1, source_target_pairs={{2,4},{4,2},{3,5},{5,3},{10,12},{12,10},{11,13},{13,11},{18,20},{2... | collective-permute-start | bytes 1179656 | tf_op jit(solution)/shard_map/ppermute | solution.py:539
  300.7 12.8 %collective-permute-start.58 = (f32[128,768]{1,0:T(8,128)S(1)}, f32[128,768]{1,0:T(8,128)S(1)}, u32[]{:S(2)}, u32[]{:S(2)}) collective-permute-start(f32[128,768]{1,0:T(8,128)S(1)} %shard_map.219.refs_5_.refs_3_), channel_id=1, source_target_pairs={{2,0},{4,6},{3,1},{5,7},{10,8},{12,14},{11,9},{13,15},{18,16},{20,... | collective-permute-start | bytes 1179656 | tf_op jit(solution)/shard_map/ppermute | solution.py:539
  306.0 8.0 %collective-permute-start.57 = (f32[128,768]{1,0:T(8,128)S(1)}, f32[128,768]{1,0:T(8,128)S(1)}, u32[]{:S(2)}, u32[]{:S(2)}) collective-permute-start(f32[128,768]{1,0:T(8,128)S(1)} %shard_map.221.refs_2_.refs_0_), channel_id=1, source_target_pairs={{2,4},{4,2},{3,5},{5,3},{10,12},{12,10},{11,13},{13,11},{18,20},{2... | collective-permute-start | bytes 1179656 | tf_op jit(solution)/shard_map/ppermute | solution.py:539
  306.7 15.7 %collective-permute-start.61 = (f32[128,768]{1,0:T(8,128)S(1)}, f32[128,768]{1,0:T(8,128)S(1)}, u32[]{:S(2)}, u32[]{:S(2)}) collective-permute-start(f32[128,768]{1,0:T(8,128)S(1)} %shard_map.222.refs_7_.refs_3_), channel_id=1, source_target_pairs={{2,0},{4,6},{3,1},{5,7},{10,8},{12,14},{11,9},{13,15},{18,16},{20,... | collective-permute-start | bytes 1179656 | tf_op jit(solution)/shard_map/ppermute | solution.py:539
  314.0 16.8 %collective-permute-start.60 = (f32[128,768]{1,0:T(8,128)S(1)}, f32[128,768]{1,0:T(8,128)S(1)}, u32[]{:S(2)}, u32[]{:S(2)}) collective-permute-start(f32[128,768]{1,0:T(8,128)S(1)} %shard_map.224.refs_7_.refs_3_), channel_id=1, source_target_pairs={{2,0},{4,6},{3,1},{5,7},{10,8},{12,14},{11,9},{13,15},{18,16},{20,... | collective-permute-start | bytes 1179656 | tf_op jit(solution)/shard_map/ppermute | solution.py:539
  (37 other events, 163.6 us)

commit v3 on v2

--- a/solution.py
+++ b/solution.py
@@ -10,7 +10,7 @@
 
 HEAD_DIM = 128
 CG_STEPS = 3
-CHUNKS = 4
+CHUNKS = 8
 AHEAD = 2
 DEPTH = 512
 
@@ -24,7 +24,7 @@
 SCALE = HEAD_DIM ** (-0.5)
 VMEM = pl.BlockSpec(memory_space=pltpu.VMEM)
 SMEM = pl.BlockSpec(memory_space=pltpu.SMEM)
-LIMIT = 32 * 1024 * 1024
+LIMIT = 16 * 1024 * 1024
 STEP_COST = pl.CostEstimate(flops=10**9, bytes_accessed=10**7, transcendentals=0)
 STREAM_LIMIT = 56 * 1024 * 1024
 
@@ -89,8 +89,8 @@
     query_sum[...] += dot32(part, wq_ref[...])
     key_sum[...] += dot32(part, wk_ref[...])
     value_sum[...] += dot32(part, wv_ref[...])
-    down_q_ref[...] += dot32(part, aq_ref[...])
-    down_v_ref[...] += dot32(part, av_ref[...])
+    down_q_ref[...] += dot_nt(part, aq_ref[...])
+    down_v_ref[...] += dot_nt(part, av_ref[...])
 
     @pl.when(step == pl.num_programs(0) - 1)
     def _():
@@ -133,8 +133,8 @@
             pl.BlockSpec((DEPTH, inner), deep),
             pl.BlockSpec((DEPTH, inner), deep),
             pl.BlockSpec((DEPTH, inner), deep),
-            pl.BlockSpec((DEPTH, rank), deep),
-            pl.BlockSpec((DEPTH, rank), deep),
+            pl.BlockSpec((rank, DEPTH), lambda i: (0, i)),
+            pl.BlockSpec((rank, DEPTH), lambda i: (0, i)),
             pl.BlockSpec((rank, inner), whole),
             pl.BlockSpec((rank, inner), whole),
         ],
@@ -164,7 +164,7 @@
         cost_estimate=pl.CostEstimate(
             flops=6 * length * width * inner, bytes_accessed=6 * width * inner, transcendentals=0
         ),
-    )(limit, x, gain[None], bias[None], wq, wk, wv, aq, av, bq, bv)
+    )(limit, x, gain[None], bias[None], wq, wk, wv, aq.T, av.T, bq, bv)
 
 
 def token_spec():
@@ -195,9 +195,8 @@
 
 
 def put_tail(out_ref, own_ref, got_ref, length):
-    inner = own_ref.shape[1]
-    out_ref[length:, inner:] = jnp.zeros((8, out_ref.shape[1] - inner), F32)
-    out_ref[length:, :inner] = own_ref[length:] + got_ref[length:]
+    out_ref[length:] = jnp.zeros((8, out_ref.shape[1]), F32)
+    out_ref[length:, :HEAD_DIM] = own_ref[length:, :HEAD_DIM] + got_ref[length:, :HEAD_DIM]
 
 
 def first_spread_kernel(tail, length, core_ref, own_ref, got_ref, w_ref, other_w_ref, *refs):

time: 345 us -> 415 us (1.20)
  starting transfers between devices: 115 us -> 242 us
  waiting for transfers between devices: 161 us -> 97.7 us
  Pallas kernels: 53.2 us -> 58.2 us
    ppermute x48 -> x96, starting transfers between devices: 101 us -> 229 us  [launch(): arriving[k] = lax.ppermute(held[k], 'chip', hops[hop])]
    ppermute x48 -> x96, waiting for transfers between devices: 128 us -> 65.6 us  [launch(): arriving[k] = lax.ppermute(held[k], 'chip', hops[hop])]
    pallas_call x4 -> x8, Pallas kernels: 8.48 us -> 11.6 us  [first_spread(): pl.pallas_call(functools.partial(first_spread_kernel, index == 0, length)...]
    pallas_call x60 -> x120, Pallas kernels: 19 us -> 21.2 us  [call(): pl.pallas_call(body, in_specs=[SMEM] * len(scalars) + [VMEM] * len(ins) +...]
  transfers between devices with their start and end apart: 65 -> 113, of which waited for: 42 -> 36; matrix products, arithmetic and copies ran while one was open for 1% -> 0% of each run, Pallas kernels for 11% -> 11%
where the time goes in v3:
time: 415 us; the launch traced here: 412 us
  starting transfers between devices  242 us (58%)
  waiting for transfers between devices  97.7 us (24%)
  Pallas kernels  58.2 us (14%)
  other arithmetic  5.71 us (1%)
  local copies, waits for them, and re-layouts  4.82 us (1%)
    ppermute x96, starting transfers between devices, launch(): arriving[k] = lax.ppermute(held[k], 'chip', hops[hop])  229 us
    ppermute x96, waiting for transfers between devices, launch(): arriving[k] = lax.ppermute(held[k], 'chip', hops[hop])  65.6 us
    pallas_call x120, Pallas kernels, call(): pl.pallas_call(body, in_specs=[SMEM] * len(scalars) + [VMEM] * len(ins) +...  21.2 us
    pallas_call x1, Pallas kernels, project(): pl.pallas_call(project_kernel, grid=(width // DEPTH,), in_specs=[SMEM, pl...  16 us
    pallas_call x8, Pallas kernels, first_spread(): pl.pallas_call(functools.partial(first_spread_kernel, index == 0, length)...  11.6 us
    ppermute x4, waiting for transfers between devices, data_terms(): part = part + lax.ppermute(part, 'dp', [(d, d ^ step) for d in range(n_dp)])  10.9 us
    ppermute x4, waiting for transfers between devices, data_terms(): lax.ppermute(part, 'dp', [(d, d ^ step) for d in range(n_dp)])  10.8 us
    ppermute x9, waiting for transfers between devices, swap(): return lax.ppermute(part, 'core', [(0, 1), (1, 0)])  10.4 us
  transfers between devices with their start and end apart: 113, of which 36 were waited for; matrix products, arithmetic and copies ran while one was open for 0% of the time, Pallas kernels for 11%

profile of v3, /device:TPU:0, one launch (start us, length us, event | category | flops | bytes accessed | tf_op | source)
XLA Modules:
  0.0 412.2 jit_solution(7200639561025758498)
XLA Ops:
  0.6 4.4 %dynamic-slice_convert_fusion = f32[384,3072]{1,0:T(8,128)} fusion(bf16[384,6144]{1,0:T(8,128)(2,1)} %w_ref.15, s32[]{:T(128)S(6)} %select_n.7), kind=kLoop, calls=%fused_computation | loop fusion | flops 1179648 | bytes 7077892 | tf_op jit(solution)/shard_map/convert_element_type | solution.py:509
  6.1 16.0 %shard_map.156 = (f32[3,128,128]{2,1,0:T(8,128)}, bf16[128,384]{1,0:T(8,128)(2,1)}, bf16[128,384]{1,0:T(8,128)(2,1)}, f32[128,16]{1,0:T(8,128)}, f32[128,16]{1,0:T(8,128)}, /*index=5*/f32[136,384]{1,0:T(8,128)}) custom-call(s32[1]{0:T(128)S(6)} %copy.17.limit_ref.refs_1_.refs_2_.refs_4_.refs_8_, bf16[128,6144]{1,0:T(8,128)(2,1)} %x_ref.1, ...), custom_call_target="tpu_custom_call" | custom-call | flops 1811939328 | bytes 14155776 | tf_op jit(solution)/shard_map/pallas_call | solution.py:125
  27.6 5.4 %collective-permute-start.3 = (f32[136,384]{1,0:T(8,128)S(1)}, f32[136,384]{1,0:T(8,128)}, u32[]{:S(2)}, u32[]{:S(2)}) collective-permute-start(f32[136,384]{1,0:T(8,128)S(1)} %get-tuple-element.108.refs_0_), channel_id=1, source_target_pairs={{0,2},{6,4},{1,3},{7,5},{8,10},{14,12},{9,11},{15,13},{16,18},{22,... | collective-permute-start | bytes 626696 | tf_op jit(solution)/shard_map/ppermute | solution.py:538
  42.7 7.3 %collective-permute-start.8 = (f32[128,384]{1,0:T(8,128)S(1)}, f32[128,384]{1,0:T(8,128)S(1)}, u32[]{:S(2)}, u32[]{:S(2)}) collective-permute-start(f32[128,384]{1,0:T(8,128)S(1)} %get-tuple-element.110.refs_2_.refs_0_), channel_id=1, source_target_pairs={{0,2},{6,4},{1,3},{7,5},{8,10},{14,12},{9,11},{15,13},{16,18},{22,... | collective-permute-start | bytes 589832 | tf_op jit(solution)/shard_map/ppermute | solution.py:538
  53.1 3.0 collective-permute-start.4
  59.5 7.4 %collective-permute-start.14 = (f32[128,384]{1,0:T(8,128)S(1)}, f32[128,384]{1,0:T(8,128)S(1)}, u32[]{:S(2)}, u32[]{:S(2)}) collective-permute-start(f32[128,384]{1,0:T(8,128)S(1)} %get-tuple-element.113.refs_2_.refs_0_), channel_id=1, source_target_pairs={{0,2},{6,4},{1,3},{7,5},{8,10},{14,12},{9,11},{15,13},{16,18},{22,... | collective-permute-start | bytes 589832 | tf_op jit(solution)/shard_map/ppermute | solution.py:538
  71.2 6.3 %collective-permute-start.9 = (f32[128,384]{1,0:T(8,128)S(1)}, f32[128,384]{1,0:T(8,128)S(1)}, u32[]{:S(2)}, u32[]{:S(2)}) collective-permute-start(f32[128,384]{1,0:T(8,128)S(1)} %get-tuple-element.115.refs_2_.refs_0_), channel_id=1, source_target_pairs={{0,2},{6,4},{1,3},{7,5},{8,10},{14,12},{9,11},{15,13},{16,18},{22,... | collective-permute-start | bytes 589832 | tf_op jit(solution)/shard_map/ppermute | solution.py:538
  81.2 7.4 %collective-permute-start.20 = (f32[128,384]{1,0:T(8,128)S(1)}, f32[128,384]{1,0:T(8,128)S(1)}, u32[]{:S(2)}, u32[]{:S(2)}) collective-permute-start(f32[128,384]{1,0:T(8,128)S(1)} %get-tuple-element.121.refs_2_.refs_0_), channel_id=1, source_target_pairs={{0,2},{6,4},{1,3},{7,5},{8,10},{14,12},{9,11},{15,13},{16,18},{22,... | collective-permute-start | bytes 589832 | tf_op jit(solution)/shard_map/ppermute | solution.py:538
  92.4 6.3 %collective-permute-start.15 = (f32[128,384]{1,0:T(8,128)S(1)}, f32[128,384]{1,0:T(8,128)S(1)}, u32[]{:S(2)}, u32[]{:S(2)}) collective-permute-start(f32[128,384]{1,0:T(8,128)S(1)} %get-tuple-element.123.refs_2_.refs_0_), channel_id=1, source_target_pairs={{0,2},{6,4},{1,3},{7,5},{8,10},{14,12},{9,11},{15,13},{16,18},{22,... | collective-permute-start | bytes 589832 | tf_op jit(solution)/shard_map/ppermute | solution.py:538
  102.4 5.4 %collective-permute-done.17.refs_2_ = f32[128,384]{1,0:T(8,128)S(1)} collective-permute-done((f32[128,384]{1,0:T(8,128)S(1)}, f32[128,384]{1,0:T(8,128)S(1)}, u32[]{:S(2)}, u32[]{:S(2)}) %collective-permute-start.17) | collective-permute-done | bytes 196640 | tf_op jit(solution)/shard_map/ppermute | solution.py:538
  113.6 3.3 collective-permute-done.25.refs_2_
  117.3 3.5 collective-permute-done.24.refs_2_
  125.8 2.7 collective-permute-done.27
  138.4 3.9 collective-permute-done.31.refs_1_
  143.3 6.3 %collective-permute-start.36 = (f32[128,384]{1,0:T(8,128)S(1)}, f32[128,384]{1,0:T(8,128)S(1)}, u32[]{:S(2)}, u32[]{:S(2)}) collective-permute-start(f32[128,384]{1,0:T(8,128)S(1)} %shard_map.194.refs_2_.refs_0_), channel_id=1, source_target_pairs={{0,2},{6,4},{1,3},{7,5},{8,10},{14,12},{9,11},{15,13},{16,18},{22,... | collective-permute-start | bytes 589832 | tf_op jit(solution)/shard_map/ppermute | solution.py:538
  150.6 3.9 collective-permute-start.32
  156.8 6.5 %collective-permute-start.42 = (f32[128,384]{1,0:T(8,128)S(1)}, f32[128,384]{1,0:T(8,128)S(1)}, u32[]{:S(2)}, u32[]{:S(2)}) collective-permute-start(f32[128,384]{1,0:T(8,128)S(1)} %shard_map.199.refs_2_.refs_0_), channel_id=1, source_target_pairs={{0,2},{6,4},{1,3},{7,5},{8,10},{14,12},{9,11},{15,13},{16,18},{22,... | collective-permute-start | bytes 589832 | tf_op jit(solution)/shard_map/ppermute | solution.py:538
  166.0 7.1 %collective-permute-start.37 = (f32[128,384]{1,0:T(8,128)S(1)}, f32[128,384]{1,0:T(8,128)S(1)}, u32[]{:S(2)}, u32[]{:S(2)}) collective-permute-start(f32[128,384]{1,0:T(8,128)S(1)} %shard_map.203.refs_2_.refs_0_), channel_id=1, source_target_pairs={{0,2},{6,4},{1,3},{7,5},{8,10},{14,12},{9,11},{15,13},{16,18},{22,... | collective-permute-start | bytes 589832 | tf_op jit(solution)/shard_map/ppermute | solution.py:538
  175.8 6.5 %collective-permute-start.48 = (f32[128,384]{1,0:T(8,128)S(1)}, f32[128,384]{1,0:T(8,128)S(1)}, u32[]{:S(2)}, u32[]{:S(2)}) collective-permute-start(f32[128,384]{1,0:T(8,128)S(1)} %shard_map.207.refs_2_.refs_0_), channel_id=1, source_target_pairs={{0,2},{6,4},{1,3},{7,5},{8,10},{14,12},{9,11},{15,13},{16,18},{22,... | collective-permute-start | bytes 589832 | tf_op jit(solution)/shard_map/ppermute | solution.py:538
  185.0 7.1 %collective-permute-start.43 = (f32[128,384]{1,0:T(8,128)S(1)}, f32[128,384]{1,0:T(8,128)S(1)}, u32[]{:S(2)}, u32[]{:S(2)}) collective-permute-start(f32[128,384]{1,0:T(8,128)S(1)} %shard_map.211.refs_2_.refs_0_), channel_id=1, source_target_pairs={{0,2},{6,4},{1,3},{7,5},{8,10},{14,12},{9,11},{15,13},{16,18},{22,... | collective-permute-start | bytes 589832 | tf_op jit(solution)/shard_map/ppermute | solution.py:538
  195.9 3.9 collective-permute-done.45.refs_2_
  206.3 2.7 collective-permute-done.53.refs_2_
  209.4 4.0 collective-permute-done.52.refs_2_
  218.3 2.7 collective-permute-done.55
  222.6 2.7 collective-permute-done.56.refs_1_
  231.0 3.9 collective-permute-done.59.refs_1_
  235.8 7.0 %collective-permute-start.64 = (f32[128,384]{1,0:T(8,128)S(1)}, f32[128,384]{1,0:T(8,128)S(1)}, u32[]{:S(2)}, u32[]{:S(2)}) collective-permute-start(f32[128,384]{1,0:T(8,128)S(1)} %shard_map.228.refs_2_.refs_0_), channel_id=1, source_target_pairs={{0,2},{6,4},{1,3},{7,5},{8,10},{14,12},{9,11},{15,13},{16,18},{22,... | collective-permute-start | bytes 589832 | tf_op jit(solution)/shard_map/ppermute | solution.py:538
  243.8 3.2 collective-permute-start.60
  249.4 7.1 %collective-permute-start.70 = (f32[128,384]{1,0:T(8,128)S(1)}, f32[128,384]{1,0:T(8,128)S(1)}, u32[]{:S(2)}, u32[]{:S(2)}) collective-permute-start(f32[128,384]{1,0:T(8,128)S(1)} %shard_map.233.refs_2_.refs_0_), channel_id=1, source_target_pairs={{0,2},{6,4},{1,3},{7,5},{8,10},{14,12},{9,11},{15,13},{16,18},{22,... | collective-permute-start | bytes 589832 | tf_op jit(solution)/shard_map/ppermute | solution.py:538
  259.4 6.5 %collective-permute-start.65 = (f32[128,384]{1,0:T(8,128)S(1)}, f32[128,384]{1,0:T(8,128)S(1)}, u32[]{:S(2)}, u32[]{:S(2)}) collective-permute-start(f32[128,384]{1,0:T(8,128)S(1)} %shard_map.237.refs_2_.refs_0_), channel_id=1, source_target_pairs={{0,2},{6,4},{1,3},{7,5},{8,10},{14,12},{9,11},{15,13},{16,18},{22,... | collective-permute-start | bytes 589832 | tf_op jit(solution)/shard_map/ppermute | solution.py:538
  268.6 7.1 %collective-permute-start.76 = (f32[128,384]{1,0:T(8,128)S(1)}, f32[128,384]{1,0:T(8,128)S(1)}, u32[]{:S(2)}, u32[]{:S(2)}) collective-permute-start(f32[128,384]{1,0:T(8,128)S(1)} %shard_map.241.refs_2_.refs_0_), channel_id=1, source_target_pairs={{0,2},{6,4},{1,3},{7,5},{8,10},{14,12},{9,11},{15,13},{16,18},{22,... | collective-permute-start | bytes 589832 | tf_op jit(solution)/shard_map/ppermute | solution.py:538
  278.5 6.5 %collective-permute-start.71 = (f32[128,384]{1,0:T(8,128)S(1)}, f32[128,384]{1,0:T(8,128)S(1)}, u32[]{:S(2)}, u32[]{:S(2)}) collective-permute-start(f32[128,384]{1,0:T(8,128)S(1)} %shard_map.245.refs_2_.refs_0_), channel_id=1, source_target_pairs={{0,2},{6,4},{1,3},{7,5},{8,10},{14,12},{9,11},{15,13},{16,18},{22,... | collective-permute-start | bytes 589832 | tf_op jit(solution)/shard_map/ppermute | solution.py:538
  288.7 4.3 %collective-permute-done.73.refs_2_ = f32[128,384]{1,0:T(8,128)S(1)} collective-permute-done((f32[128,384]{1,0:T(8,128)S(1)}, f32[128,384]{1,0:T(8,128)S(1)}, u32[]{:S(2)}, u32[]{:S(2)}) %collective-permute-start.73) | collective-permute-done | bytes 196640 | tf_op jit(solution)/shard_map/ppermute | solution.py:538
  302.4 4.5 %collective-permute-done.80.refs_2_ = f32[128,384]{1,0:T(8,128)S(1)} collective-permute-done((f32[128,384]{1,0:T(8,128)S(1)}, f32[128,384]{1,0:T(8,128)S(1)}, u32[]{:S(2)}, u32[]{:S(2)}) %collective-permute-start.80) | collective-permute-done | bytes 196640 | tf_op jit(solution)/shard_map/ppermute | solution.py:538
  311.8 2.7 collective-permute-done.83
  316.1 2.7 collective-permute-done.84.refs_1_
  324.5 3.9 collective-permute-done.87.refs_1_
  329.4 6.3 %collective-permute-start.92 = (f32[128,384]{1,0:T(8,128)S(1)}, f32[128,384]{1,0:T(8,128)S(1)}, u32[]{:S(2)}, u32[]{:S(2)}) collective-permute-start(f32[128,384]{1,0:T(8,128)S(1)} %shard_map.262.refs_2_.refs_0_), channel_id=1, source_target_pairs={{0,2},{6,4},{1,3},{7,5},{8,10},{14,12},{9,11},{15,13},{16,18},{22,... | collective-permute-start | bytes 589832 | tf_op jit(solution)/shard_map/ppermute | solution.py:538
  336.7 3.9 collective-permute-start.88
  342.9 6.5 %collective-permute-start.98 = (f32[128,384]{1,0:T(8,128)S(1)}, f32[128,384]{1,0:T(8,128)S(1)}, u32[]{:S(2)}, u32[]{:S(2)}) collective-permute-start(f32[128,384]{1,0:T(8,128)S(1)} %shard_map.267.refs_2_.refs_0_), channel_id=1, source_target_pairs={{0,2},{6,4},{1,3},{7,5},{8,10},{14,12},{9,11},{15,13},{16,18},{22,... | collective-permute-start | bytes 589832 | tf_op jit(solution)/shard_map/ppermute | solution.py:538
  352.1 7.1 %collective-permute-start.93 = (f32[128,384]{1,0:T(8,128)S(1)}, f32[128,384]{1,0:T(8,128)S(1)}, u32[]{:S(2)}, u32[]{:S(2)}) collective-permute-start(f32[128,384]{1,0:T(8,128)S(1)} %shard_map.271.refs_2_.refs_0_), channel_id=1, source_target_pairs={{0,2},{6,4},{1,3},{7,5},{8,10},{14,12},{9,11},{15,13},{16,18},{22,... | collective-permute-start | bytes 589832 | tf_op jit(solution)/shard_map/ppermute | solution.py:538
  361.9 6.5 %collective-permute-start.104 = (f32[128,384]{1,0:T(8,128)S(1)}, f32[128,384]{1,0:T(8,128)S(1)}, u32[]{:S(2)}, u32[]{:S(2)}) collective-permute-start(f32[128,384]{1,0:T(8,128)S(1)} %shard_map.275.refs_2_.refs_0_), channel_id=1, source_target_pairs={{0,2},{6,4},{1,3},{7,5},{8,10},{14,12},{9,11},{15,13},{16,18},{22,... | collective-permute-start | bytes 589832 | tf_op jit(solution)/shard_map/ppermute | solution.py:538
  371.1 7.1 %collective-permute-start.99 = (f32[128,384]{1,0:T(8,128)S(1)}, f32[128,384]{1,0:T(8,128)S(1)}, u32[]{:S(2)}, u32[]{:S(2)}) collective-permute-start(f32[128,384]{1,0:T(8,128)S(1)} %shard_map.279.refs_2_.refs_0_), channel_id=1, source_target_pairs={{0,2},{6,4},{1,3},{7,5},{8,10},{14,12},{9,11},{15,13},{16,18},{22,... | collective-permute-start | bytes 589832 | tf_op jit(solution)/shard_map/ppermute | solution.py:538
  382.0 3.9 collective-permute-done.101.refs_2_
  392.5 2.7 collective-permute-done.109.refs_2_
  395.6 4.0 collective-permute-done.108.refs_2_
  404.4 2.7 collective-permute-done.111
  408.8 2.7 collective-permute-done.112.refs_1_
  (340 shorter events, 160.3 us)
Async XLA Ops:
  5.0 18.9 %collective-permute-start.1 = (f32[384,3072]{1,0:T(8,128)}, f32[384,3072]{1,0:T(8,128)}, u32[]{:S(2)}, u32[]{:S(2)}) collective-permute-start(f32[384,3072]{1,0:T(8,128)} %dynamic-slice_convert_fusion), channel_id=1, source_target_pairs={{0,1},{1,0},{2,3},{3,2},{4,5},{5,4},{6,7},{7,6},{8,9},{9,8},{10,11... | collective-permute-start | bytes 14155784 | tf_op jit(solution)/shard_map/ppermute | solution.py:499
  35.0 15.0 %collective-permute-start.2 = (f32[128,384]{1,0:T(8,128)}, f32[128,384]{1,0:T(8,128)}, u32[]{:S(2)}, u32[]{:S(2)}) collective-permute-start(f32[128,384]{1,0:T(8,128)} %get-tuple-element.109.refs_2_.refs_0_), channel_id=1, source_target_pairs={{0,2},{6,4},{1,3},{7,5},{8,10},{14,12},{9,11},{15,13},{16,18},{22,... | collective-permute-start | bytes 589832 | tf_op jit(solution)/shard_map/ppermute | solution.py:538
  38.3 17.8 %collective-permute-start.5 = (f32[136,384]{1,0:T(8,128)S(1)}, f32[136,384]{1,0:T(8,128)S(1)}, u32[]{:S(2)}, u32[]{:S(2)}) collective-permute-start(f32[136,384]{1,0:T(8,128)S(1)} %shard_map.159.refs_0_), channel_id=1, source_target_pairs={{2,4},{4,2},{3,5},{5,3},{10,12},{12,10},{11,13},{13,11},{18,20},{2... | collective-permute-start | bytes 626696 | tf_op jit(solution)/shard_map/ppermute | solution.py:538
  42.7 14.8 %collective-permute-start.8 = (f32[128,384]{1,0:T(8,128)S(1)}, f32[128,384]{1,0:T(8,128)S(1)}, u32[]{:S(2)}, u32[]{:S(2)}) collective-permute-start(f32[128,384]{1,0:T(8,128)S(1)} %get-tuple-element.110.refs_2_.refs_0_), channel_id=1, source_target_pairs={{0,2},{6,4},{1,3},{7,5},{8,10},{14,12},{9,11},{15,13},{16,18},{22,... | collective-permute-start | bytes 589832 | tf_op jit(solution)/shard_map/ppermute | solution.py:538
  51.0 15.9 %collective-permute-start.7 = (f32[128,384]{1,0:T(8,128)S(1)}, f32[128,384]{1,0:T(8,128)S(1)}, u32[]{:S(2)}, u32[]{:S(2)}) collective-permute-start(f32[128,384]{1,0:T(8,128)S(1)} %shard_map.161.refs_0_), channel_id=1, source_target_pairs={{2,4},{4,2},{3,5},{5,3},{10,12},{12,10},{11,13},{13,11},{18,20},{2... | collective-permute-start | bytes 589832 | tf_op jit(solution)/shard_map/ppermute | solution.py:538
  53.1 16.0 %collective-permute-start.4 = (f32[128,384]{1,0:T(8,128)S(1)}, f32[128,384]{1,0:T(8,128)S(1)}, u32[]{:S(2)}, u32[]{:S(2)}) collective-permute-start(f32[128,384]{1,0:T(8,128)S(1)} %get-tuple-element.111.refs_2_.refs_0_), channel_id=1, source_target_pairs={{0,2},{6,4},{1,3},{7,5},{8,10},{14,12},{9,11},{15,13},{16,18},{22,... | collective-permute-start | bytes 589832 | tf_op jit(solution)/shard_map/ppermute | solution.py:538
  57.5 19.9 %collective-permute-start.10 = (f32[128,384]{1,0:T(8,128)S(1)}, f32[128,384]{1,0:T(8,128)S(1)}, u32[]{:S(2)}, u32[]{:S(2)}) collective-permute-start(f32[128,384]{1,0:T(8,128)S(1)} %shard_map.164.refs_0_), channel_id=1, source_target_pairs={{2,4},{4,2},{3,5},{5,3},{10,12},{12,10},{11,13},{13,11},{18,20},{2... | collective-permute-start | bytes 589832 | tf_op jit(solution)/shard_map/ppermute | solution.py:538
  59.5 19.6 %collective-permute-start.14 = (f32[128,384]{1,0:T(8,128)S(1)}, f32[128,384]{1,0:T(8,128)S(1)}, u32[]{:S(2)}, u32[]{:S(2)}) collective-permute-start(f32[128,384]{1,0:T(8,128)S(1)} %get-tuple-element.113.refs_2_.refs_0_), channel_id=1, source_target_pairs={{0,2},{6,4},{1,3},{7,5},{8,10},{14,12},{9,11},{15,13},{16,18},{22,... | collective-permute-start | bytes 589832 | tf_op jit(solution)/shard_map/ppermute | solution.py:538
  69.1 19.5 %collective-permute-start.13 = (f32[128,384]{1,0:T(8,128)S(1)}, f32[128,384]{1,0:T(8,128)S(1)}, u32[]{:S(2)}, u32[]{:S(2)}) collective-permute-start(f32[128,384]{1,0:T(8,128)S(1)} %shard_map.168.refs_0_), channel_id=1, source_target_pairs={{2,4},{4,2},{3,5},{5,3},{10,12},{12,10},{11,13},{13,11},{18,20},{2... | collective-permute-start | bytes 589832 | tf_op jit(solution)/shard_map/ppermute | solution.py:538
  71.2 19.1 %collective-permute-start.9 = (f32[128,384]{1,0:T(8,128)S(1)}, f32[128,384]{1,0:T(8,128)S(1)}, u32[]{:S(2)}, u32[]{:S(2)}) collective-permute-start(f32[128,384]{1,0:T(8,128)S(1)} %get-tuple-element.115.refs_2_.refs_0_), channel_id=1, source_target_pairs={{0,2},{6,4},{1,3},{7,5},{8,10},{14,12},{9,11},{15,13},{16,18},{22,... | collective-permute-start | bytes 589832 | tf_op jit(solution)/shard_map/ppermute | solution.py:538
  77.5 12.5 %collective-permute-start.11 = (f32[128,384]{1,0:T(8,128)S(1)}, f32[128,384]{1,0:T(8,128)S(1)}, u32[]{:S(2)}, u32[]{:S(2)}) collective-permute-start(f32[128,384]{1,0:T(8,128)S(1)} %shard_map.170.refs_8_.refs_3_), channel_id=1, source_target_pairs={{2,0},{4,6},{3,1},{5,7},{10,8},{12,14},{11,9},{13,15},{18,16},{20,... | collective-permute-start | bytes 589832 | tf_op jit(solution)/shard_map/ppermute | solution.py:538
  79.2 19.5 %collective-permute-start.16 = (f32[128,384]{1,0:T(8,128)S(1)}, f32[128,384]{1,0:T(8,128)S(1)}, u32[]{:S(2)}, u32[]{:S(2)}) collective-permute-start(f32[128,384]{1,0:T(8,128)S(1)} %shard_map.172.refs_0_), channel_id=1, source_target_pairs={{2,4},{4,2},{3,5},{5,3},{10,12},{12,10},{11,13},{13,11},{18,20},{2... | collective-permute-start | bytes 589832 | tf_op jit(solution)/shard_map/ppermute | solution.py:538
  81.2 19.2 %collective-permute-start.20 = (f32[128,384]{1,0:T(8,128)S(1)}, f32[128,384]{1,0:T(8,128)S(1)}, u32[]{:S(2)}, u32[]{:S(2)}) collective-permute-start(f32[128,384]{1,0:T(8,128)S(1)} %get-tuple-element.121.refs_2_.refs_0_), channel_id=1, source_target_pairs={{0,2},{6,4},{1,3},{7,5},{8,10},{14,12},{9,11},{15,13},{16,18},{22,... | collective-permute-start | bytes 589832 | tf_op jit(solution)/shard_map/ppermute | solution.py:538
  92.4 15.7 %collective-permute-start.15 = (f32[128,384]{1,0:T(8,128)S(1)}, f32[128,384]{1,0:T(8,128)S(1)}, u32[]{:S(2)}, u32[]{:S(2)}) collective-permute-start(f32[128,384]{1,0:T(8,128)S(1)} %get-tuple-element.123.refs_2_.refs_0_), channel_id=1, source_target_pairs={{0,2},{6,4},{1,3},{7,5},{8,10},{14,12},{9,11},{15,13},{16,18},{22,... | collective-permute-start | bytes 589832 | tf_op jit(solution)/shard_map/ppermute | solution.py:538
  137.1 12.5 %collective-permute-start.30 = (f32[128,384]{1,0:T(8,128)S(1)}, f32[128,384]{1,0:T(8,128)S(1)}, u32[]{:S(2)}, u32[]{:S(2)}) collective-permute-start(f32[128,384]{1,0:T(8,128)S(1)} %shard_map.192.refs_2_.refs_0_), channel_id=1, source_target_pairs={{0,2},{6,4},{1,3},{7,5},{8,10},{14,12},{9,11},{15,13},{16,18},{22,... | collective-permute-start | bytes 589832 | tf_op jit(solution)/shard_map/ppermute | solution.py:538
  143.3 12.5 %collective-permute-start.36 = (f32[128,384]{1,0:T(8,128)S(1)}, f32[128,384]{1,0:T(8,128)S(1)}, u32[]{:S(2)}, u32[]{:S(2)}) collective-permute-start(f32[128,384]{1,0:T(8,128)S(1)} %shard_map.194.refs_2_.refs_0_), channel_id=1, source_target_pairs={{0,2},{6,4},{1,3},{7,5},{8,10},{14,12},{9,11},{15,13},{16,18},{22,... | collective-permute-start | bytes 589832 | tf_op jit(solution)/shard_map/ppermute | solution.py:538
  149.6 13.7 %collective-permute-start.35 = (f32[128,384]{1,0:T(8,128)S(1)}, f32[128,384]{1,0:T(8,128)S(1)}, u32[]{:S(2)}, u32[]{:S(2)}) collective-permute-start(f32[128,384]{1,0:T(8,128)S(1)} %shard_map.195.refs_3_.refs_0_), channel_id=1, source_target_pairs={{2,4},{4,2},{3,5},{5,3},{10,12},{12,10},{11,13},{13,11},{18,20},{2... | collective-permute-start | bytes 589832 | tf_op jit(solution)/shard_map/ppermute | solution.py:538
  150.6 14.4 %collective-permute-start.32 = (f32[128,384]{1,0:T(8,128)S(1)}, f32[128,384]{1,0:T(8,128)S(1)}, u32[]{:S(2)}, u32[]{:S(2)}) collective-permute-start(f32[128,384]{1,0:T(8,128)S(1)} %shard_map.196.refs_2_.refs_0_), channel_id=1, source_target_pairs={{0,2},{6,4},{1,3},{7,5},{8,10},{14,12},{9,11},{15,13},{16,18},{22,... | collective-permute-start | bytes 589832 | tf_op jit(solution)/shard_map/ppermute | solution.py:538
  155.8 17.3 %collective-permute-start.38 = (f32[128,384]{1,0:T(8,128)S(1)}, f32[128,384]{1,0:T(8,128)S(1)}, u32[]{:S(2)}, u32[]{:S(2)}) collective-permute-start(f32[128,384]{1,0:T(8,128)S(1)} %shard_map.198.refs_3_.refs_0_), channel_id=1, source_target_pairs={{2,4},{4,2},{3,5},{5,3},{10,12},{12,10},{11,13},{13,11},{18,20},{2... | collective-permute-start | bytes 589832 | tf_op jit(solution)/shard_map/ppermute | solution.py:538
  156.8 18.0 %collective-permute-start.42 = (f32[128,384]{1,0:T(8,128)S(1)}, f32[128,384]{1,0:T(8,128)S(1)}, u32[]{:S(2)}, u32[]{:S(2)}) collective-permute-start(f32[128,384]{1,0:T(8,128)S(1)} %shard_map.199.refs_2_.refs_0_), channel_id=1, source_target_pairs={{0,2},{6,4},{1,3},{7,5},{8,10},{14,12},{9,11},{15,13},{16,18},{22,... | collective-permute-start | bytes 589832 | tf_op jit(solution)/shard_map/ppermute | solution.py:538
  165.0 17.3 %collective-permute-start.41 = (f32[128,384]{1,0:T(8,128)S(1)}, f32[128,384]{1,0:T(8,128)S(1)}, u32[]{:S(2)}, u32[]{:S(2)}) collective-permute-start(f32[128,384]{1,0:T(8,128)S(1)} %shard_map.202.refs_3_.refs_0_), channel_id=1, source_target_pairs={{2,4},{4,2},{3,5},{5,3},{10,12},{12,10},{11,13},{13,11},{18,20},{2... | collective-permute-start | bytes 589832 | tf_op jit(solution)/shard_map/ppermute | solution.py:538
  166.0 18.0 %collective-permute-start.37 = (f32[128,384]{1,0:T(8,128)S(1)}, f32[128,384]{1,0:T(8,128)S(1)}, u32[]{:S(2)}, u32[]{:S(2)}) collective-permute-start(f32[128,384]{1,0:T(8,128)S(1)} %shard_map.203.refs_2_.refs_0_), channel_id=1, source_target_pairs={{0,2},{6,4},{1,3},{7,5},{8,10},{14,12},{9,11},{15,13},{16,18},{22,... | collective-permute-start | bytes 589832 | tf_op jit(solution)/shard_map/ppermute | solution.py:538
  174.9 17.3 %collective-permute-start.44 = (f32[128,384]{1,0:T(8,128)S(1)}, f32[128,384]{1,0:T(8,128)S(1)}, u32[]{:S(2)}, u32[]{:S(2)}) collective-permute-start(f32[128,384]{1,0:T(8,128)S(1)} %shard_map.206.refs_3_.refs_0_), channel_id=1, source_target_pairs={{2,4},{4,2},{3,5},{5,3},{10,12},{12,10},{11,13},{13,11},{18,20},{2... | collective-permute-start | bytes 589832 | tf_op jit(solution)/shard_map/ppermute | solution.py:538
  175.8 18.0 %collective-permute-start.48 = (f32[128,384]{1,0:T(8,128)S(1)}, f32[128,384]{1,0:T(8,128)S(1)}, u32[]{:S(2)}, u32[]{:S(2)}) collective-permute-start(f32[128,384]{1,0:T(8,128)S(1)} %shard_map.207.refs_2_.refs_0_), channel_id=1, source_target_pairs={{0,2},{6,4},{1,3},{7,5},{8,10},{14,12},{9,11},{15,13},{16,18},{22,... | collective-permute-start | bytes 589832 | tf_op jit(solution)/shard_map/ppermute | solution.py:538
  185.0 15.1 %collective-permute-start.43 = (f32[128,384]{1,0:T(8,128)S(1)}, f32[128,384]{1,0:T(8,128)S(1)}, u32[]{:S(2)}, u32[]{:S(2)}) collective-permute-start(f32[128,384]{1,0:T(8,128)S(1)} %shard_map.211.refs_2_.refs_0_), channel_id=1, source_target_pairs={{0,2},{6,4},{1,3},{7,5},{8,10},{14,12},{9,11},{15,13},{16,18},{22,... | collective-permute-start | bytes 589832 | tf_op jit(solution)/shard_map/ppermute | solution.py:538
  229.7 13.2 %collective-permute-start.58 = (f32[128,384]{1,0:T(8,128)S(1)}, f32[128,384]{1,0:T(8,128)S(1)}, u32[]{:S(2)}, u32[]{:S(2)}) collective-permute-start(f32[128,384]{1,0:T(8,128)S(1)} %shard_map.226.refs_2_.refs_0_), channel_id=1, source_target_pairs={{0,2},{6,4},{1,3},{7,5},{8,10},{14,12},{9,11},{15,13},{16,18},{22,... | collective-permute-start | bytes 589832 | tf_op jit(solution)/shard_map/ppermute | solution.py:538
  234.9 12.1 %collective-permute-start.61 = (f32[136,384]{1,0:T(8,128)S(1)}, f32[136,384]{1,0:T(8,128)S(1)}, u32[]{:S(2)}, u32[]{:S(2)}) collective-permute-start(f32[136,384]{1,0:T(8,128)S(1)} %shard_map.227.refs_3_.refs_0_), channel_id=1, source_target_pairs={{2,4},{4,2},{3,5},{5,3},{10,12},{12,10},{11,13},{13,11},{18,20},{2... | collective-permute-start | bytes 626696 | tf_op jit(solution)/shard_map/ppermute | solution.py:538
  235.8 12.5 %collective-permute-start.64 = (f32[128,384]{1,0:T(8,128)S(1)}, f32[128,384]{1,0:T(8,128)S(1)}, u32[]{:S(2)}, u32[]{:S(2)}) collective-permute-start(f32[128,384]{1,0:T(8,128)S(1)} %shard_map.228.refs_2_.refs_0_), channel_id=1, source_target_pairs={{0,2},{6,4},{1,3},{7,5},{8,10},{14,12},{9,11},{15,13},{16,18},{22,... | collective-permute-start | bytes 589832 | tf_op jit(solution)/shard_map/ppermute | solution.py:538
  242.9 13.7 %collective-permute-start.63 = (f32[128,384]{1,0:T(8,128)S(1)}, f32[128,384]{1,0:T(8,128)S(1)}, u32[]{:S(2)}, u32[]{:S(2)}) collective-permute-start(f32[128,384]{1,0:T(8,128)S(1)} %shard_map.229.refs_3_.refs_0_), channel_id=1, source_target_pairs={{2,4},{4,2},{3,5},{5,3},{10,12},{12,10},{11,13},{13,11},{18,20},{2... | collective-permute-start | bytes 589832 | tf_op jit(solution)/shard_map/ppermute | solution.py:538
  243.8 14.4 %collective-permute-start.60 = (f32[128,384]{1,0:T(8,128)S(1)}, f32[128,384]{1,0:T(8,128)S(1)}, u32[]{:S(2)}, u32[]{:S(2)}) collective-permute-start(f32[128,384]{1,0:T(8,128)S(1)} %shard_map.230.refs_2_.refs_0_), channel_id=1, source_target_pairs={{0,2},{6,4},{1,3},{7,5},{8,10},{14,12},{9,11},{15,13},{16,18},{22,... | collective-permute-start | bytes 589832 | tf_op jit(solution)/shard_map/ppermute | solution.py:538
  248.4 17.5 %collective-permute-start.66 = (f32[128,384]{1,0:T(8,128)S(1)}, f32[128,384]{1,0:T(8,128)S(1)}, u32[]{:S(2)}, u32[]{:S(2)}) collective-permute-start(f32[128,384]{1,0:T(8,128)S(1)} %shard_map.232.refs_3_.refs_0_), channel_id=1, source_target_pairs={{2,4},{4,2},{3,5},{5,3},{10,12},{12,10},{11,13},{13,11},{18,20},{2... | collective-permute-start | bytes 589832 | tf_op jit(solution)/shard_map/ppermute | solution.py:538
  249.4 18.2 %collective-permute-start.70 = (f32[128,384]{1,0:T(8,128)S(1)}, f32[128,384]{1,0:T(8,128)S(1)}, u32[]{:S(2)}, u32[]{:S(2)}) collective-permute-start(f32[128,384]{1,0:T(8,128)S(1)} %shard_map.233.refs_2_.refs_0_), channel_id=1, source_target_pairs={{0,2},{6,4},{1,3},{7,5},{8,10},{14,12},{9,11},{15,13},{16,18},{22,... | collective-permute-start | bytes 589832 | tf_op jit(solution)/shard_map/ppermute | solution.py:538
  258.2 17.5 %collective-permute-start.69 = (f32[128,384]{1,0:T(8,128)S(1)}, f32[128,384]{1,0:T(8,128)S(1)}, u32[]{:S(2)}, u32[]{:S(2)}) collective-permute-start(f32[128,384]{1,0:T(8,128)S(1)} %shard_map.236.refs_3_.refs_0_), channel_id=1, source_target_pairs={{2,4},{4,2},{3,5},{5,3},{10,12},{12,10},{11,13},{13,11},{18,20},{2... | collective-permute-start | bytes 589832 | tf_op jit(solution)/shard_map/ppermute | solution.py:538
  259.4 18.0 %collective-permute-start.65 = (f32[128,384]{1,0:T(8,128)S(1)}, f32[128,384]{1,0:T(8,128)S(1)}, u32[]{:S(2)}, u32[]{:S(2)}) collective-permute-start(f32[128,384]{1,0:T(8,128)S(1)} %shard_map.237.refs_2_.refs_0_), channel_id=1, source_target_pairs={{0,2},{6,4},{1,3},{7,5},{8,10},{14,12},{9,11},{15,13},{16,18},{22,... | collective-permute-start | bytes 589832 | tf_op jit(solution)/shard_map/ppermute | solution.py:538
  267.7 17.3 %collective-permute-start.72 = (f32[128,384]{1,0:T(8,128)S(1)}, f32[128,384]{1,0:T(8,128)S(1)}, u32[]{:S(2)}, u32[]{:S(2)}) collective-permute-start(f32[128,384]{1,0:T(8,128)S(1)} %shard_map.240.refs_3_.refs_0_), channel_id=1, source_target_pairs={{2,4},{4,2},{3,5},{5,3},{10,12},{12,10},{11,13},{13,11},{18,20},{2... | collective-permute-start | bytes 589832 | tf_op jit(solution)/shard_map/ppermute | solution.py:538
  268.6 18.0 %collective-permute-start.76 = (f32[128,384]{1,0:T(8,128)S(1)}, f32[128,384]{1,0:T(8,128)S(1)}, u32[]{:S(2)}, u32[]{:S(2)}) collective-permute-start(f32[128,384]{1,0:T(8,128)S(1)} %shard_map.241.refs_2_.refs_0_), channel_id=1, source_target_pairs={{0,2},{6,4},{1,3},{7,5},{8,10},{14,12},{9,11},{15,13},{16,18},{22,... | collective-permute-start | bytes 589832 | tf_op jit(solution)/shard_map/ppermute | solution.py:538
  278.5 14.9 %collective-permute-start.71 = (f32[128,384]{1,0:T(8,128)S(1)}, f32[128,384]{1,0:T(8,128)S(1)}, u32[]{:S(2)}, u32[]{:S(2)}) collective-permute-start(f32[128,384]{1,0:T(8,128)S(1)} %shard_map.245.refs_2_.refs_0_), channel_id=1, source_target_pairs={{0,2},{6,4},{1,3},{7,5},{8,10},{14,12},{9,11},{15,13},{16,18},{22,... | collective-permute-start | bytes 589832 | tf_op jit(solution)/shard_map/ppermute | solution.py:538
  323.2 12.5 %collective-permute-start.86 = (f32[128,384]{1,0:T(8,128)S(1)}, f32[128,384]{1,0:T(8,128)S(1)}, u32[]{:S(2)}, u32[]{:S(2)}) collective-permute-start(f32[128,384]{1,0:T(8,128)S(1)} %shard_map.260.refs_2_.refs_0_), channel_id=1, source_target_pairs={{0,2},{6,4},{1,3},{7,5},{8,10},{14,12},{9,11},{15,13},{16,18},{22,... | collective-permute-start | bytes 589832 | tf_op jit(solution)/shard_map/ppermute | solution.py:538
  329.4 12.5 %collective-permute-start.92 = (f32[128,384]{1,0:T(8,128)S(1)}, f32[128,384]{1,0:T(8,128)S(1)}, u32[]{:S(2)}, u32[]{:S(2)}) collective-permute-start(f32[128,384]{1,0:T(8,128)S(1)} %shard_map.262.refs_2_.refs_0_), channel_id=1, source_target_pairs={{0,2},{6,4},{1,3},{7,5},{8,10},{14,12},{9,11},{15,13},{16,18},{22,... | collective-permute-start | bytes 589832 | tf_op jit(solution)/shard_map/ppermute | solution.py:538
  335.8 13.7 %collective-permute-start.91 = (f32[128,384]{1,0:T(8,128)S(1)}, f32[128,384]{1,0:T(8,128)S(1)}, u32[]{:S(2)}, u32[]{:S(2)}) collective-permute-start(f32[128,384]{1,0:T(8,128)S(1)} %shard_map.263.refs_3_.refs_0_), channel_id=1, source_target_pairs={{2,4},{4,2},{3,5},{5,3},{10,12},{12,10},{11,13},{13,11},{18,20},{2... | collective-permute-start | bytes 589832 | tf_op jit(solution)/shard_map/ppermute | solution.py:538
  336.7 14.4 %collective-permute-start.88 = (f32[128,384]{1,0:T(8,128)S(1)}, f32[128,384]{1,0:T(8,128)S(1)}, u32[]{:S(2)}, u32[]{:S(2)}) collective-permute-start(f32[128,384]{1,0:T(8,128)S(1)} %shard_map.264.refs_2_.refs_0_), channel_id=1, source_target_pairs={{0,2},{6,4},{1,3},{7,5},{8,10},{14,12},{9,11},{15,13},{16,18},{22,... | collective-permute-start | bytes 589832 | tf_op jit(solution)/shard_map/ppermute | solution.py:538
  342.0 17.3 %collective-permute-start.94 = (f32[128,384]{1,0:T(8,128)S(1)}, f32[128,384]{1,0:T(8,128)S(1)}, u32[]{:S(2)}, u32[]{:S(2)}) collective-permute-start(f32[128,384]{1,0:T(8,128)S(1)} %shard_map.266.refs_3_.refs_0_), channel_id=1, source_target_pairs={{2,4},{4,2},{3,5},{5,3},{10,12},{12,10},{11,13},{13,11},{18,20},{2... | collective-permute-start | bytes 589832 | tf_op jit(solution)/shard_map/ppermute | solution.py:538
  342.9 18.0 %collective-permute-start.98 = (f32[128,384]{1,0:T(8,128)S(1)}, f32[128,384]{1,0:T(8,128)S(1)}, u32[]{:S(2)}, u32[]{:S(2)}) collective-permute-start(f32[128,384]{1,0:T(8,128)S(1)} %shard_map.267.refs_2_.refs_0_), channel_id=1, source_target_pairs={{0,2},{6,4},{1,3},{7,5},{8,10},{14,12},{9,11},{15,13},{16,18},{22,... | collective-permute-start | bytes 589832 | tf_op jit(solution)/shard_map/ppermute | solution.py:538
  351.1 17.3 %collective-permute-start.97 = (f32[128,384]{1,0:T(8,128)S(1)}, f32[128,384]{1,0:T(8,128)S(1)}, u32[]{:S(2)}, u32[]{:S(2)}) collective-permute-start(f32[128,384]{1,0:T(8,128)S(1)} %shard_map.270.refs_3_.refs_0_), channel_id=1, source_target_pairs={{2,4},{4,2},{3,5},{5,3},{10,12},{12,10},{11,13},{13,11},{18,20},{2... | collective-permute-start | bytes 589832 | tf_op jit(solution)/shard_map/ppermute | solution.py:538
  352.1 18.0 %collective-permute-start.93 = (f32[128,384]{1,0:T(8,128)S(1)}, f32[128,384]{1,0:T(8,128)S(1)}, u32[]{:S(2)}, u32[]{:S(2)}) collective-permute-start(f32[128,384]{1,0:T(8,128)S(1)} %shard_map.271.refs_2_.refs_0_), channel_id=1, source_target_pairs={{0,2},{6,4},{1,3},{7,5},{8,10},{14,12},{9,11},{15,13},{16,18},{22,... | collective-permute-start | bytes 589832 | tf_op jit(solution)/shard_map/ppermute | solution.py:538
  361.0 17.3 %collective-permute-start.100 = (f32[128,384]{1,0:T(8,128)S(1)}, f32[128,384]{1,0:T(8,128)S(1)}, u32[]{:S(2)}, u32[]{:S(2)}) collective-permute-start(f32[128,384]{1,0:T(8,128)S(1)} %shard_map.274.refs_3_.refs_0_), channel_id=1, source_target_pairs={{2,4},{4,2},{3,5},{5,3},{10,12},{12,10},{11,13},{13,11},{18,20},{2... | collective-permute-start | bytes 589832 | tf_op jit(solution)/shard_map/ppermute | solution.py:538
  361.9 18.0 %collective-permute-start.104 = (f32[128,384]{1,0:T(8,128)S(1)}, f32[128,384]{1,0:T(8,128)S(1)}, u32[]{:S(2)}, u32[]{:S(2)}) collective-permute-start(f32[128,384]{1,0:T(8,128)S(1)} %shard_map.275.refs_2_.refs_0_), channel_id=1, source_target_pairs={{0,2},{6,4},{1,3},{7,5},{8,10},{14,12},{9,11},{15,13},{16,18},{22,... | collective-permute-start | bytes 589832 | tf_op jit(solution)/shard_map/ppermute | solution.py:538
  371.1 15.2 %collective-permute-start.99 = (f32[128,384]{1,0:T(8,128)S(1)}, f32[128,384]{1,0:T(8,128)S(1)}, u32[]{:S(2)}, u32[]{:S(2)}) collective-permute-start(f32[128,384]{1,0:T(8,128)S(1)} %shard_map.279.refs_2_.refs_0_), channel_id=1, source_target_pairs={{0,2},{6,4},{1,3},{7,5},{8,10},{14,12},{9,11},{15,13},{16,18},{22,... | collective-permute-start | bytes 589832 | tf_op jit(solution)/shard_map/ppermute | solution.py:538
  (74 other events, 544.8 us)

commit v4 on v3

--- a/solution.py
+++ b/solution.py
@@ -10,8 +10,7 @@
 
 HEAD_DIM = 128
 CG_STEPS = 3
-CHUNKS = 8
-AHEAD = 2
+CHUNKS = 6
 DEPTH = 512
 
 EPS = 1e-05
@@ -253,29 +252,35 @@
 
 def add(first, second, token):
     def kernel(first_ref, second_ref, out_ref):
-        out_ref[...] = first_ref[...] + second_ref[...]
+        out_ref[...] = first_ref[...] + second_ref[: first_ref.shape[0]]
 
     return call(kernel, [first, second], [(first.shape, F32)], token)[0]
 
 
-def choose(takes, got, held, token):
-    def kernel(takes_ref, got_ref, held_ref, out_ref):
-        out_ref[...] = jnp.where(takes_ref[0] > 0, got_ref[...], held_ref[...])
-
-    return call(kernel, [got, held], [(held.shape, F32)], token, [takes])[0]
-
-
-def gather(index, takes, got, held, pair, sums, limit, gap, token):
+def add_and_pick(first, second, ends, outer, token):
+    def kernel(ends_ref, first_ref, second_ref, outer_ref, sum_ref, sent_ref):
+        total = first_ref[...] + second_ref[...]
+        sum_ref[...] = total
+        rows = outer_ref.shape[0]
+        sent_ref[:rows] = jnp.where(ends_ref[0] > 0, outer_ref[...], total[:rows])
+        if total.shape[0] > rows:
+            sent_ref[rows:] = total[rows:]
+
+    outs = [(first.shape, F32)] * 2
+    return call(kernel, [first, second, outer], outs, token, [ends])
+
+
+def gather(index, ends, got, held, pair, sums, limit, gap, token):
     inner = pair.shape[0] // 2
     extra = [] if gap is None else [gap]
     length = held.shape[0] - (8 if index == 0 else 0)
 
-    def kernel(takes_ref, limit_ref, got_ref, held_ref, pair_ref, *refs):
+    def kernel(ends_ref, limit_ref, got_ref, held_ref, pair_ref, *refs):
         refs = list(refs)
         gap_ref = refs.pop(0) if gap is not None else None
         before = [refs.pop(0), refs.pop(0)] if index else None
         own_ref, other_ref = refs[:2]
-        total = jnp.where(takes_ref[0] > 0, got_ref[...], held_ref[...])
+        total = jnp.where(ends_ref[0] > 0, got_ref[...], held_ref[...])
         if index == 0:
             refs[2][...] = total[length:, :128]
             total = total[:length]
@@ -297,16 +302,7 @@
     outs = [((length, inner), F32), ((length + 8, inner), F32)]
     if index == 0:
         outs.append(((8, 128), F32))
-    return call(kernel, [got, held, pair] + extra + sums, outs, token, [takes, limit])
-
-
-def line_hops(chips):
-    inward = []
-    for step in range(chips // 2 - 1):
-        inward.append([(step, step + 1), (chips - 1 - step, chips - 2 - step)])
-    middle = [(chips // 2 - 1, chips // 2), (chips // 2, chips // 2 - 1)]
-    outward = [[(b, a) for a, b in hop] for hop in reversed(inward)]
-    return inward + [middle], outward
+    return call(kernel, [got, held, pair] + extra + sums, outs, token, [ends, limit])
 
 
 def cotangent_kernel(
@@ -518,60 +514,71 @@
     )
     attention = (soft, key, value, down_q, down_v)
 
-    sums_in, sums_out = line_hops(n_chip)
-    hops = sums_in + sums_out
-    takes = []
-    for hop in sums_out:
-        inside = jnp.zeros((), jnp.bool_)
-        for _, to in hop:
-            inside = inside | (chip == to)
-        takes.append(inside.astype(jnp.int32)[None])
+    ends = ((chip == 0) | (chip == n_chip - 1)).astype(jnp.int32)[None]
+
+    def outer_swap(part):
+        return lax.ppermute(part, "chip", [(0, 1), (1, 0), (2, 3), (3, 2)])
+
+    def inner_swap(part):
+        return lax.ppermute(part, "chip", [(0, 0), (1, 2), (2, 1), (3, 3)])
 
     def product(rows, pairs):
         got_rows = swap(rows)
         first = not pairs
-        held, arriving = {}, {}
+        pairs.extend([None] * (CHUNKS - len(pairs)))
         parts, scalars = [], None
+        own_part, total, outer, inner = {}, {}, {}, {}
         token = None
-
-        def launch(k, hop):
-            arriving[k] = lax.ppermute(held[k], "chip", hops[hop])
 
         def begin(k):
             if first:
-                held[k], pair = first_spread(
+                own_part[k], pairs[k] = first_spread(
                     k, CHUNKS, length, where, rows, got_rows, w_out, other_w, token
                 )
-                pairs.append(pair)
             else:
-                held[k] = spread(k, length, rows, got_rows, pairs[k], token)
-            launch(k, 0)
-            return held[k]
-
-        for k in range(AHEAD):
-            token = begin(k)
-        for tick in range(CHUNKS + len(hops) - 1):
-            for stage in range(len(hops)):
-                k = tick - stage
-                if 0 <= k < CHUNKS:
-                    if stage == len(hops) - 1:
-                        out = gather(
-                            k, takes[-1], arriving[k], held[k], pairs[k], parts, lengths,
-                            gap[:, k * cols : (k + 1) * cols] if first else None, token,
+                own_part[k] = spread(k, length, rows, got_rows, pairs[k], token)
+            return own_part[k]
+
+        def finish(k, got):
+            gap_part = gap[:, k * cols : (k + 1) * cols] if first else None
+            return gather(k, ends, got, total[k], pairs[k], parts, lengths, gap_part, token)
+
+        if n_chip != 4:
+            for k in range(CHUNKS):
+                token = begin(k)
+            for k in range(CHUNKS):
+                total[k] = lax.psum(own_part[k], "chip")
+                out = finish(k, total[k])
+                parts, scalars = list(out[:2]), out[2] if k == 0 else scalars
+        else:
+            for k in [0, 1, 2] if first else [0, *range(2, CHUNKS), 1]:
+                token = begin(k)
+            for k in (0, 1):
+                outer[k] = outer_swap(own_part[k])
+            for tick in range(CHUNKS + 3):
+                if tick < CHUNKS:
+                    own_part[tick] = add(own_part[tick], outer[tick], token)
+                    token = own_part[tick]
+                    inner[tick] = inner_swap(token)
+                later = tick + 2
+                if 1 <= tick <= CHUNKS:
+                    k = tick - 1
+                    if later < CHUNKS:
+                        total[k], sent = add_and_pick(
+                            own_part[k], inner[k], ends, own_part[later], token
                         )
-                        parts = list(out[:2])
-                        scalars = out[2] if k == 0 else scalars
-                        token = parts[0]
-                        continue
-                    if stage < len(sums_in):
-                        held[k] = add(held[k], arriving[k], token)
                     else:
-                        flag = takes[stage - len(sums_in)]
-                        held[k] = choose(flag, arriving[k], held[k], token)
-                    token = held[k]
-                    launch(k, stage + 1)
-                if stage == 0 and tick + AHEAD < CHUNKS:
-                    token = begin(tick + AHEAD)
+                        total[k] = sent = add(own_part[k], inner[k], token)
+                    token = sent
+                    outer[later] = outer_swap(sent)
+                elif tick == 0:
+                    outer[later] = outer_swap(own_part[later])
+                if tick + 3 < CHUNKS and first:
+                    token = begin(tick + 3)
+                if tick >= 3:
+                    out = finish(tick - 3, outer[tick])
+                    parts, scalars = list(out[:2]), out[2] if tick == 3 else scalars
+                    token = parts[0]
         own, other = parts
         share = ADAPTER_SCALE / token_count
         part = cotangent(share, lengths, own, other, swap(other), attention)

time: 415 us -> 320 us (0.77)
  starting transfers between devices: 242 us -> 155 us
  Pallas kernels: 58.2 us -> 52.7 us
    ppermute x96 -> x60, starting transfers between devices: 229 us -> 142 us  [the longest x36 125 us: outer_swap(): return lax.ppermute(part, 'chip', [(0, 1), (1, 0), (2, 3), (3, 2)])]
    ppermute x96 -> x60, waiting for transfers between devices: 65.6 us -> 62.8 us  [the longest x36 62.8 us: outer_swap(): return lax.ppermute(part, 'chip', [(0, 1), (1, 0), (2, 3), (3, 2)])]
    pallas_call x120 -> x90, Pallas kernels: 21.2 us -> 18.5 us  [call(): pl.pallas_call(body, in_specs=[SMEM] * len(scalars) + [VMEM] * len(ins) +...]
    pallas_call x8 -> x6, Pallas kernels: 11.6 us -> 8.99 us  [first_spread(): pl.pallas_call(functools.partial(first_spread_kernel, index == 0, length)...]
  transfers between devices with their start and end apart: 113 -> 77, of which waited for: 36 -> 42; matrix products, arithmetic and copies ran while one was open for 0% -> 0% of each run, Pallas kernels for 11% -> 12%
where the time goes in v4:
time: 320 us; the launch traced here: 318 us
  starting transfers between devices  155 us (48%)
  waiting for transfers between devices  96.3 us (30%)
  Pallas kernels  52.7 us (16%)
  local copies, waits for them, and re-layouts  6.95 us (2%)
  other arithmetic  4.62 us (1%)
    ppermute x36, starting transfers between devices, outer_swap(): return lax.ppermute(part, 'chip', [(0, 1), (1, 0), (2, 3), (3, 2)])  125 us
    ppermute x36, waiting for transfers between devices, outer_swap(): return lax.ppermute(part, 'chip', [(0, 1), (1, 0), (2, 3), (3, 2)])  62.8 us
    pallas_call x90, Pallas kernels, call(): pl.pallas_call(body, in_specs=[SMEM] * len(scalars) + [VMEM] * len(ins) +...  18.5 us
    ppermute x24, starting transfers between devices, inner_swap(): return lax.ppermute(part, 'chip', [(0, 0), (1, 2), (2, 1), (3, 3)])  17.4 us
    pallas_call x1, Pallas kernels, project(): pl.pallas_call(project_kernel, grid=(width // DEPTH,), in_specs=[SMEM, pl...  15.9 us
    ppermute x9, waiting for transfers between devices, swap(): return lax.ppermute(part, 'core', [(0, 1), (1, 0)])  11.7 us
    ppermute x4, waiting for transfers between devices, data_terms(): part = part + lax.ppermute(part, 'dp', [(d, d ^ step) for d in range(n_dp)])  10.9 us
    ppermute x4, waiting for transfers between devices, data_terms(): lax.ppermute(part, 'dp', [(d, d ^ step) for d in range(n_dp)])  10.8 us
  transfers between devices with their start and end apart: 77, of which 42 were waited for; matrix products, arithmetic and copies ran while one was open for 0% of the time, Pallas kernels for 12%

profile of v4, /device:TPU:0, one launch (start us, length us, event | category | flops | bytes accessed | tf_op | source)
XLA Modules:
  0.0 318.3 jit_solution(4765284247142025901)
XLA Ops:
  0.6 4.4 %dynamic-slice_convert_fusion = f32[384,3072]{1,0:T(8,128)} fusion(bf16[384,6144]{1,0:T(8,128)(2,1)} %w_ref.11, s32[]{:T(128)S(6)} %select_n.7), kind=kLoop, calls=%fused_computation | loop fusion | flops 1179648 | bytes 7077892 | tf_op jit(solution)/shard_map/convert_element_type | solution.py:505
  6.1 15.9 %shard_map.156 = (f32[3,128,128]{2,1,0:T(8,128)}, bf16[128,384]{1,0:T(8,128)(2,1)}, bf16[128,384]{1,0:T(8,128)(2,1)}, f32[128,16]{1,0:T(8,128)}, f32[128,16]{1,0:T(8,128)}, /*index=5*/f32[136,384]{1,0:T(8,128)}) custom-call(s32[1]{0:T(128)S(6)} %copy.17.limit_ref.refs_1_.refs_2_.refs_4_.refs_8_, bf16[128,6144]{1,0:T(8,128)(2,1)} %x_ref.1, ...), custom_call_target="tpu_custom_call" | custom-call | flops 1811939328 | bytes 14155776 | tf_op jit(solution)/shard_map/pallas_call | solution.py:124
  29.5 2.7 collective-permute-start.3
  36.2 3.5 %collective-permute-done.3.refs_1_ = f32[136,512]{1,0:T(8,128)S(1)} collective-permute-done((f32[136,512]{1,0:T(8,128)S(1)}, f32[136,512]{1,0:T(8,128)S(1)}, u32[]{:S(2)}, u32[]{:S(2)}) %collective-permute-start.3) | collective-permute-done | bytes 278560 | tf_op jit(solution)/shard_map/ppermute | solution.py:520
  41.3 4.2 %collective-permute-start.6 = (f32[128,512]{1,0:T(8,128)}, f32[128,512]{1,0:T(8,128)S(1)}, u32[]{:S(2)}, u32[]{:S(2)}) collective-permute-start(f32[128,512]{1,0:T(8,128)} %copy-done.13), channel_id=1, source_target_pairs={{0,2},{2,0},{4,6},{6,4},{1,3},{3,1},{5,7},{7,5},{8,10},{10,8},{12,... | collective-permute-start | bytes 786440 | tf_op jit(solution)/shard_map/ppermute | solution.py:520
  56.7 2.8 collective-permute-start.10
  62.2 4.0 %collective-permute-start.9 = (f32[128,512]{1,0:T(8,128)S(1)}, f32[128,512]{1,0:T(8,128)S(1)}, u32[]{:S(2)}, u32[]{:S(2)}) collective-permute-start(f32[128,512]{1,0:T(8,128)S(1)} %get-tuple-element.120.refs_6_), channel_id=1, source_target_pairs={{0,2},{2,0},{4,6},{6,4},{1,3},{3,1},{5,7},{7,5},{8,10},{10,8},{12,... | collective-permute-start | bytes 786440 | tf_op jit(solution)/shard_map/ppermute | solution.py:520
  71.6 4.6 %collective-permute-start.16 = (f32[128,512]{1,0:T(8,128)S(1)}, f32[128,512]{1,0:T(8,128)S(1)}, u32[]{:S(2)}, u32[]{:S(2)}) collective-permute-start(f32[128,512]{1,0:T(8,128)S(1)} %shard_map.172.refs_8_.refs_3_), channel_id=1, source_target_pairs={{0,2},{2,0},{4,6},{6,4},{1,3},{3,1},{5,7},{7,5},{8,10},{10,8},{12,... | collective-permute-start | bytes 786440 | tf_op jit(solution)/shard_map/ppermute | solution.py:520
  76.3 3.5 %collective-permute-start.15 = (f32[128,512]{1,0:T(8,128)S(1)}, f32[128,512]{1,0:T(8,128)S(1)}, u32[]{:S(2)}, u32[]{:S(2)}) collective-permute-start(f32[128,512]{1,0:T(8,128)S(1)} %shard_map.175.refs_8_.refs_3_), channel_id=1, source_target_pairs={{0,2},{2,0},{4,6},{6,4},{1,3},{3,1},{5,7},{7,5},{8,10},{10,8},{12,... | collective-permute-start | bytes 786440 | tf_op jit(solution)/shard_map/ppermute | solution.py:520
  83.2 4.4 %collective-permute-done.15.refs_2_ = f32[128,512]{1,0:T(8,128)S(1)} collective-permute-done((f32[128,512]{1,0:T(8,128)S(1)}, f32[128,512]{1,0:T(8,128)S(1)}, u32[]{:S(2)}, u32[]{:S(2)}) %collective-permute-start.15) | collective-permute-done | bytes 262176 | tf_op jit(solution)/shard_map/ppermute | solution.py:520
  95.4 2.7 collective-permute-done.18
  99.7 2.7 collective-permute-done.19.refs_1_
  108.5 6.0 %collective-permute-done.22.refs_1_ = f32[136,512]{1,0:T(8,128)S(1)} collective-permute-done((f32[136,512]{1,0:T(8,128)S(1)}, f32[136,512]{1,0:T(8,128)S(1)}, u32[]{:S(2)}, u32[]{:S(2)}) %collective-permute-start.22) | collective-permute-done | bytes 278560 | tf_op jit(solution)/shard_map/ppermute | solution.py:520
  115.3 4.1 %collective-permute-start.21 = (f32[128,512]{1,0:T(8,128)S(1)}, f32[128,512]{1,0:T(8,128)S(1)}, u32[]{:S(2)}, u32[]{:S(2)}) collective-permute-start(f32[128,512]{1,0:T(8,128)S(1)} %shard_map.184.refs_3_.refs_0_), channel_id=1, source_target_pairs={{0,2},{2,0},{4,6},{6,4},{1,3},{3,1},{5,7},{7,5},{8,10},{10,8},{12,... | collective-permute-start | bytes 786440 | tf_op jit(solution)/shard_map/ppermute | solution.py:520
  120.9 4.7 %collective-permute-start.26 = (f32[136,512]{1,0:T(8,128)S(1)}, f32[136,512]{1,0:T(8,128)S(1)}, u32[]{:S(2)}, u32[]{:S(2)}) collective-permute-start(f32[136,512]{1,0:T(8,128)S(1)} %get-tuple-element.148.refs_2_), channel_id=1, source_target_pairs={{0,2},{2,0},{4,6},{6,4},{1,3},{3,1},{5,7},{7,5},{8,10},{10,8},{12,... | collective-permute-start | bytes 835592 | tf_op jit(solution)/shard_map/ppermute | solution.py:520
  126.5 5.8 %collective-permute-start.29 = (f32[128,512]{1,0:T(8,128)S(1)}, f32[128,512]{1,0:T(8,128)S(1)}, u32[]{:S(2)}, u32[]{:S(2)}) collective-permute-start(f32[128,512]{1,0:T(8,128)S(1)} %get-tuple-element.149.refs_2_), channel_id=1, source_target_pairs={{0,2},{2,0},{4,6},{6,4},{1,3},{3,1},{5,7},{7,5},{8,10},{10,8},{12,... | collective-permute-start | bytes 786440 | tf_op jit(solution)/shard_map/ppermute | solution.py:520
  133.4 5.0 %collective-permute-start.28 = (f32[128,512]{1,0:T(8,128)S(1)}, f32[128,512]{1,0:T(8,128)S(1)}, u32[]{:S(2)}, u32[]{:S(2)}) collective-permute-start(f32[128,512]{1,0:T(8,128)S(1)} %get-tuple-element.150.refs_5_), channel_id=1, source_target_pairs={{0,2},{2,0},{4,6},{6,4},{1,3},{3,1},{5,7},{7,5},{8,10},{10,8},{12,... | collective-permute-start | bytes 786440 | tf_op jit(solution)/shard_map/ppermute | solution.py:520
  139.9 2.8 collective-permute-done.28.refs_1_.refs_2_
  143.4 4.4 %collective-permute-start.35 = (f32[128,512]{1,0:T(8,128)S(1)}, f32[128,512]{1,0:T(8,128)S(1)}, u32[]{:S(2)}, u32[]{:S(2)}) collective-permute-start(f32[128,512]{1,0:T(8,128)S(1)} %shard_map.198.refs_7_.refs_3_), channel_id=1, source_target_pairs={{0,2},{2,0},{4,6},{6,4},{1,3},{3,1},{5,7},{7,5},{8,10},{10,8},{12,... | collective-permute-start | bytes 786440 | tf_op jit(solution)/shard_map/ppermute | solution.py:520
  147.9 3.3 %collective-permute-start.34 = (f32[128,512]{1,0:T(8,128)S(1)}, f32[128,512]{1,0:T(8,128)S(1)}, u32[]{:S(2)}, u32[]{:S(2)}) collective-permute-start(f32[128,512]{1,0:T(8,128)S(1)} %shard_map.201.refs_7_.refs_3_), channel_id=1, source_target_pairs={{0,2},{2,0},{4,6},{6,4},{1,3},{3,1},{5,7},{7,5},{8,10},{10,8},{12,... | collective-permute-start | bytes 786440 | tf_op jit(solution)/shard_map/ppermute | solution.py:520
  151.6 2.7 collective-permute-start.33
  154.9 4.4 %collective-permute-done.34.refs_2_ = f32[128,512]{1,0:T(8,128)S(1)} collective-permute-done((f32[128,512]{1,0:T(8,128)S(1)}, f32[128,512]{1,0:T(8,128)S(1)}, u32[]{:S(2)}, u32[]{:S(2)}) %collective-permute-start.34) | collective-permute-done | bytes 262176 | tf_op jit(solution)/shard_map/ppermute | solution.py:520
  167.0 2.7 collective-permute-done.37
  171.4 2.7 collective-permute-done.38.refs_1_
  180.2 6.0 %collective-permute-done.41.refs_1_ = f32[136,512]{1,0:T(8,128)S(1)} collective-permute-done((f32[136,512]{1,0:T(8,128)S(1)}, f32[136,512]{1,0:T(8,128)S(1)}, u32[]{:S(2)}, u32[]{:S(2)}) %collective-permute-start.41) | collective-permute-done | bytes 278560 | tf_op jit(solution)/shard_map/ppermute | solution.py:520
  187.0 4.1 %collective-permute-start.40 = (f32[128,512]{1,0:T(8,128)S(1)}, f32[128,512]{1,0:T(8,128)S(1)}, u32[]{:S(2)}, u32[]{:S(2)}) collective-permute-start(f32[128,512]{1,0:T(8,128)S(1)} %shard_map.210.refs_3_.refs_0_), channel_id=1, source_target_pairs={{0,2},{2,0},{4,6},{6,4},{1,3},{3,1},{5,7},{7,5},{8,10},{10,8},{12,... | collective-permute-start | bytes 786440 | tf_op jit(solution)/shard_map/ppermute | solution.py:520
  192.6 4.7 %collective-permute-start.45 = (f32[136,512]{1,0:T(8,128)S(1)}, f32[136,512]{1,0:T(8,128)S(1)}, u32[]{:S(2)}, u32[]{:S(2)}) collective-permute-start(f32[136,512]{1,0:T(8,128)S(1)} %get-tuple-element.169.refs_2_), channel_id=1, source_target_pairs={{0,2},{2,0},{4,6},{6,4},{1,3},{3,1},{5,7},{7,5},{8,10},{10,8},{12,... | collective-permute-start | bytes 835592 | tf_op jit(solution)/shard_map/ppermute | solution.py:520
  198.2 5.8 %collective-permute-start.48 = (f32[128,512]{1,0:T(8,128)S(1)}, f32[128,512]{1,0:T(8,128)S(1)}, u32[]{:S(2)}, u32[]{:S(2)}) collective-permute-start(f32[128,512]{1,0:T(8,128)S(1)} %get-tuple-element.170.refs_2_), channel_id=1, source_target_pairs={{0,2},{2,0},{4,6},{6,4},{1,3},{3,1},{5,7},{7,5},{8,10},{10,8},{12,... | collective-permute-start | bytes 786440 | tf_op jit(solution)/shard_map/ppermute | solution.py:520
  204.9 5.2 %collective-permute-start.47 = (f32[128,512]{1,0:T(8,128)S(1)}, f32[128,512]{1,0:T(8,128)S(1)}, u32[]{:S(2)}, u32[]{:S(2)}) collective-permute-start(f32[128,512]{1,0:T(8,128)S(1)} %get-tuple-element.171.refs_5_), channel_id=1, source_target_pairs={{0,2},{2,0},{4,6},{6,4},{1,3},{3,1},{5,7},{7,5},{8,10},{10,8},{12,... | collective-permute-start | bytes 786440 | tf_op jit(solution)/shard_map/ppermute | solution.py:520
  211.6 2.8 collective-permute-done.47.refs_1_.refs_2_
  215.1 4.4 %collective-permute-start.54 = (f32[128,512]{1,0:T(8,128)S(1)}, f32[128,512]{1,0:T(8,128)S(1)}, u32[]{:S(2)}, u32[]{:S(2)}) collective-permute-start(f32[128,512]{1,0:T(8,128)S(1)} %shard_map.224.refs_7_.refs_3_), channel_id=1, source_target_pairs={{0,2},{2,0},{4,6},{6,4},{1,3},{3,1},{5,7},{7,5},{8,10},{10,8},{12,... | collective-permute-start | bytes 786440 | tf_op jit(solution)/shard_map/ppermute | solution.py:520
  219.5 3.3 %collective-permute-start.53 = (f32[128,512]{1,0:T(8,128)S(1)}, f32[128,512]{1,0:T(8,128)S(1)}, u32[]{:S(2)}, u32[]{:S(2)}) collective-permute-start(f32[128,512]{1,0:T(8,128)S(1)} %shard_map.227.refs_7_.refs_3_), channel_id=1, source_target_pairs={{0,2},{2,0},{4,6},{6,4},{1,3},{3,1},{5,7},{7,5},{8,10},{10,8},{12,... | collective-permute-start | bytes 786440 | tf_op jit(solution)/shard_map/ppermute | solution.py:520
  223.3 2.7 collective-permute-start.52
  226.6 4.4 %collective-permute-done.53.refs_2_ = f32[128,512]{1,0:T(8,128)S(1)} collective-permute-done((f32[128,512]{1,0:T(8,128)S(1)}, f32[128,512]{1,0:T(8,128)S(1)}, u32[]{:S(2)}, u32[]{:S(2)}) %collective-permute-start.53) | collective-permute-done | bytes 262176 | tf_op jit(solution)/shard_map/ppermute | solution.py:520
  238.7 2.7 collective-permute-done.56
  243.1 2.7 collective-permute-done.57.refs_1_
  252.0 6.0 %collective-permute-done.60.refs_1_ = f32[136,512]{1,0:T(8,128)S(1)} collective-permute-done((f32[136,512]{1,0:T(8,128)S(1)}, f32[136,512]{1,0:T(8,128)S(1)}, u32[]{:S(2)}, u32[]{:S(2)}) %collective-permute-start.60) | collective-permute-done | bytes 278560 | tf_op jit(solution)/shard_map/ppermute | solution.py:520
  258.7 4.1 %collective-permute-start.59 = (f32[128,512]{1,0:T(8,128)S(1)}, f32[128,512]{1,0:T(8,128)S(1)}, u32[]{:S(2)}, u32[]{:S(2)}) collective-permute-start(f32[128,512]{1,0:T(8,128)S(1)} %shard_map.236.refs_3_.refs_0_), channel_id=1, source_target_pairs={{0,2},{2,0},{4,6},{6,4},{1,3},{3,1},{5,7},{7,5},{8,10},{10,8},{12,... | collective-permute-start | bytes 786440 | tf_op jit(solution)/shard_map/ppermute | solution.py:520
  264.4 4.7 %collective-permute-start.64 = (f32[136,512]{1,0:T(8,128)S(1)}, f32[136,512]{1,0:T(8,128)S(1)}, u32[]{:S(2)}, u32[]{:S(2)}) collective-permute-start(f32[136,512]{1,0:T(8,128)S(1)} %get-tuple-element.194.refs_2_), channel_id=1, source_target_pairs={{0,2},{2,0},{4,6},{6,4},{1,3},{3,1},{5,7},{7,5},{8,10},{10,8},{12,... | collective-permute-start | bytes 835592 | tf_op jit(solution)/shard_map/ppermute | solution.py:520
  270.0 5.8 %collective-permute-start.67 = (f32[128,512]{1,0:T(8,128)S(1)}, f32[128,512]{1,0:T(8,128)S(1)}, u32[]{:S(2)}, u32[]{:S(2)}) collective-permute-start(f32[128,512]{1,0:T(8,128)S(1)} %get-tuple-element.195.refs_2_), channel_id=1, source_target_pairs={{0,2},{2,0},{4,6},{6,4},{1,3},{3,1},{5,7},{7,5},{8,10},{10,8},{12,... | collective-permute-start | bytes 786440 | tf_op jit(solution)/shard_map/ppermute | solution.py:520
  276.6 5.2 %collective-permute-start.66 = (f32[128,512]{1,0:T(8,128)S(1)}, f32[128,512]{1,0:T(8,128)S(1)}, u32[]{:S(2)}, u32[]{:S(2)}) collective-permute-start(f32[128,512]{1,0:T(8,128)S(1)} %get-tuple-element.196.refs_5_), channel_id=1, source_target_pairs={{0,2},{2,0},{4,6},{6,4},{1,3},{3,1},{5,7},{7,5},{8,10},{10,8},{12,... | collective-permute-start | bytes 786440 | tf_op jit(solution)/shard_map/ppermute | solution.py:520
  283.4 2.8 collective-permute-done.66.refs_1_.refs_2_
  286.9 4.4 %collective-permute-start.73 = (f32[128,512]{1,0:T(8,128)S(1)}, f32[128,512]{1,0:T(8,128)S(1)}, u32[]{:S(2)}, u32[]{:S(2)}) collective-permute-start(f32[128,512]{1,0:T(8,128)S(1)} %shard_map.250.refs_7_.refs_3_), channel_id=1, source_target_pairs={{0,2},{2,0},{4,6},{6,4},{1,3},{3,1},{5,7},{7,5},{8,10},{10,8},{12,... | collective-permute-start | bytes 786440 | tf_op jit(solution)/shard_map/ppermute | solution.py:520
  291.3 3.3 %collective-permute-start.72 = (f32[128,512]{1,0:T(8,128)S(1)}, f32[128,512]{1,0:T(8,128)S(1)}, u32[]{:S(2)}, u32[]{:S(2)}) collective-permute-start(f32[128,512]{1,0:T(8,128)S(1)} %shard_map.253.refs_7_.refs_3_), channel_id=1, source_target_pairs={{0,2},{2,0},{4,6},{6,4},{1,3},{3,1},{5,7},{7,5},{8,10},{10,8},{12,... | collective-permute-start | bytes 786440 | tf_op jit(solution)/shard_map/ppermute | solution.py:520
  295.1 2.7 collective-permute-start.71
  298.3 4.4 %collective-permute-done.72.refs_2_ = f32[128,512]{1,0:T(8,128)S(1)} collective-permute-done((f32[128,512]{1,0:T(8,128)S(1)}, f32[128,512]{1,0:T(8,128)S(1)}, u32[]{:S(2)}, u32[]{:S(2)}) %collective-permute-start.72) | collective-permute-done | bytes 262176 | tf_op jit(solution)/shard_map/ppermute | solution.py:520
  310.5 2.7 collective-permute-done.75
  314.8 2.7 collective-permute-done.76.refs_1_
  (252 shorter events, 113.9 us)
Async XLA Ops:
  5.0 18.7 %collective-permute-start.1 = (f32[384,3072]{1,0:T(8,128)}, f32[384,3072]{1,0:T(8,128)}, u32[]{:S(2)}, u32[]{:S(2)}) collective-permute-start(f32[384,3072]{1,0:T(8,128)} %dynamic-slice_convert_fusion), channel_id=1, source_target_pairs={{0,1},{1,0},{2,3},{3,2},{4,5},{5,4},{6,7},{7,6},{8,9},{9,8},{10,11... | collective-permute-start | bytes 14155784 | tf_op jit(solution)/shard_map/ppermute | solution.py:495
  29.5 10.2 %collective-permute-start.3 = (f32[136,512]{1,0:T(8,128)S(1)}, f32[136,512]{1,0:T(8,128)S(1)}, u32[]{:S(2)}, u32[]{:S(2)}) collective-permute-start(f32[136,512]{1,0:T(8,128)S(1)} %get-tuple-element.112.refs_0_), channel_id=1, source_target_pairs={{0,2},{2,0},{4,6},{6,4},{1,3},{3,1},{5,7},{7,5},{8,10},{10,8},{12,... | collective-permute-start | bytes 835592 | tf_op jit(solution)/shard_map/ppermute | solution.py:520
  34.0 15.4 %collective-permute-start.2 = (f32[128,512]{1,0:T(8,128)S(1)}, f32[128,512]{1,0:T(8,128)}, u32[]{:S(2)}, u32[]{:S(2)}) collective-permute-start(f32[128,512]{1,0:T(8,128)S(1)} %get-tuple-element.113.refs_0_), channel_id=1, source_target_pairs={{0,2},{2,0},{4,6},{6,4},{1,3},{3,1},{5,7},{7,5},{8,10},{10,8},{12,... | collective-permute-start | bytes 786440 | tf_op jit(solution)/shard_map/ppermute | solution.py:520
  39.8 11.2 %collective-permute-start.5 = (f32[136,512]{1,0:T(8,128)S(1)}, f32[136,512]{1,0:T(8,128)}, u32[]{:S(2)}, u32[]{:S(2)}) collective-permute-start(f32[136,512]{1,0:T(8,128)S(1)} %shard_map.160.refs_0_.refs_1_), channel_id=1, source_target_pairs={{0,0},{2,4},{4,2},{6,6},{1,1},{3,5},{5,3},{7,7},{8,8},{10,12},{12,... | collective-permute-start | bytes 835592 | tf_op jit(solution)/shard_map/ppermute | solution.py:523
  41.3 14.5 %collective-permute-start.6 = (f32[128,512]{1,0:T(8,128)}, f32[128,512]{1,0:T(8,128)S(1)}, u32[]{:S(2)}, u32[]{:S(2)}) collective-permute-start(f32[128,512]{1,0:T(8,128)} %copy-done.13), channel_id=1, source_target_pairs={{0,2},{2,0},{4,6},{6,4},{1,3},{3,1},{5,7},{7,5},{8,10},{10,8},{12,... | collective-permute-start | bytes 786440 | tf_op jit(solution)/shard_map/ppermute | solution.py:520
  52.1 9.2 %collective-permute-start.8 = (f32[136,512]{1,0:T(8,128)S(1)}, f32[136,512]{1,0:T(8,128)S(1)}, u32[]{:S(2)}, u32[]{:S(2)}) collective-permute-start(f32[136,512]{1,0:T(8,128)S(1)} %get-tuple-element.116.refs_0_), channel_id=1, source_target_pairs={{0,2},{2,0},{4,6},{6,4},{1,3},{3,1},{5,7},{7,5},{8,10},{10,8},{12,... | collective-permute-start | bytes 835592 | tf_op jit(solution)/shard_map/ppermute | solution.py:520
  56.7 10.3 %collective-permute-start.10 = (f32[128,512]{1,0:T(8,128)S(1)}, f32[128,512]{1,0:T(8,128)S(1)}, u32[]{:S(2)}, u32[]{:S(2)}) collective-permute-start(f32[128,512]{1,0:T(8,128)S(1)} %get-tuple-element.118.refs_0_), channel_id=1, source_target_pairs={{0,2},{2,0},{4,6},{6,4},{1,3},{3,1},{5,7},{7,5},{8,10},{10,8},{12,... | collective-permute-start | bytes 786440 | tf_op jit(solution)/shard_map/ppermute | solution.py:520
  62.2 8.7 %collective-permute-start.9 = (f32[128,512]{1,0:T(8,128)S(1)}, f32[128,512]{1,0:T(8,128)S(1)}, u32[]{:S(2)}, u32[]{:S(2)}) collective-permute-start(f32[128,512]{1,0:T(8,128)S(1)} %get-tuple-element.120.refs_6_), channel_id=1, source_target_pairs={{0,2},{2,0},{4,6},{6,4},{1,3},{3,1},{5,7},{7,5},{8,10},{10,8},{12,... | collective-permute-start | bytes 786440 | tf_op jit(solution)/shard_map/ppermute | solution.py:520
  67.1 9.2 %collective-permute-start.13 = (f32[128,512]{1,0:T(8,128)S(1)}, f32[128,512]{1,0:T(8,128)S(1)}, u32[]{:S(2)}, u32[]{:S(2)}) collective-permute-start(f32[128,512]{1,0:T(8,128)S(1)} %shard_map.171.refs_2_.refs_0_), channel_id=1, source_target_pairs={{0,0},{2,4},{4,2},{6,6},{1,1},{3,5},{5,3},{7,7},{8,8},{10,12},{12,... | collective-permute-start | bytes 786440 | tf_op jit(solution)/shard_map/ppermute | solution.py:523
  70.9 9.2 %collective-permute-start.12 = (f32[128,512]{1,0:T(8,128)S(1)}, f32[128,512]{1,0:T(8,128)S(1)}, u32[]{:S(2)}, u32[]{:S(2)}) collective-permute-start(f32[128,512]{1,0:T(8,128)S(1)} %shard_map.174.refs_2_.refs_0_), channel_id=1, source_target_pairs={{0,0},{2,4},{4,2},{6,6},{1,1},{3,5},{5,3},{7,7},{8,8},{10,12},{12,... | collective-permute-start | bytes 786440 | tf_op jit(solution)/shard_map/ppermute | solution.py:523
  71.6 11.2 %collective-permute-start.16 = (f32[128,512]{1,0:T(8,128)S(1)}, f32[128,512]{1,0:T(8,128)S(1)}, u32[]{:S(2)}, u32[]{:S(2)}) collective-permute-start(f32[128,512]{1,0:T(8,128)S(1)} %shard_map.172.refs_8_.refs_3_), channel_id=1, source_target_pairs={{0,2},{2,0},{4,6},{6,4},{1,3},{3,1},{5,7},{7,5},{8,10},{10,8},{12,... | collective-permute-start | bytes 786440 | tf_op jit(solution)/shard_map/ppermute | solution.py:520
  76.3 11.3 %collective-permute-start.15 = (f32[128,512]{1,0:T(8,128)S(1)}, f32[128,512]{1,0:T(8,128)S(1)}, u32[]{:S(2)}, u32[]{:S(2)}) collective-permute-start(f32[128,512]{1,0:T(8,128)S(1)} %shard_map.175.refs_8_.refs_3_), channel_id=1, source_target_pairs={{0,2},{2,0},{4,6},{6,4},{1,3},{3,1},{5,7},{7,5},{8,10},{10,8},{12,... | collective-permute-start | bytes 786440 | tf_op jit(solution)/shard_map/ppermute | solution.py:520
  80.2 10.2 %collective-permute-start.14 = (f32[128,512]{1,0:T(8,128)S(1)}, f32[128,512]{1,0:T(8,128)S(1)}, u32[]{:S(2)}, u32[]{:S(2)}) collective-permute-start(f32[128,512]{1,0:T(8,128)S(1)} %shard_map.177.refs_8_.refs_3_), channel_id=1, source_target_pairs={{0,2},{2,0},{4,6},{6,4},{1,3},{3,1},{5,7},{7,5},{8,10},{10,8},{12,... | collective-permute-start | bytes 786440 | tf_op jit(solution)/shard_map/ppermute | solution.py:520
  105.0 9.6 %collective-permute-start.22 = (f32[136,512]{1,0:T(8,128)S(1)}, f32[136,512]{1,0:T(8,128)S(1)}, u32[]{:S(2)}, u32[]{:S(2)}) collective-permute-start(f32[136,512]{1,0:T(8,128)S(1)} %shard_map.183.refs_3_.refs_0_), channel_id=1, source_target_pairs={{0,2},{2,0},{4,6},{6,4},{1,3},{3,1},{5,7},{7,5},{8,10},{10,8},{12,... | collective-permute-start | bytes 835592 | tf_op jit(solution)/shard_map/ppermute | solution.py:520
  108.2 12.0 %collective-permute-start.24 = (f32[128,512]{1,0:T(8,128)S(1)}, f32[128,512]{1,0:T(8,128)S(1)}, u32[]{:S(2)}, u32[]{:S(2)}) collective-permute-start(f32[128,512]{1,0:T(8,128)S(1)} %shard_map.188.refs_2_.refs_0_), channel_id=1, source_target_pairs={{0,2},{2,0},{4,6},{6,4},{1,3},{3,1},{5,7},{7,5},{8,10},{10,8},{12,... | collective-permute-start | bytes 786440 | tf_op jit(solution)/shard_map/ppermute | solution.py:520
  115.3 10.5 %collective-permute-start.21 = (f32[128,512]{1,0:T(8,128)S(1)}, f32[128,512]{1,0:T(8,128)S(1)}, u32[]{:S(2)}, u32[]{:S(2)}) collective-permute-start(f32[128,512]{1,0:T(8,128)S(1)} %shard_map.184.refs_3_.refs_0_), channel_id=1, source_target_pairs={{0,2},{2,0},{4,6},{6,4},{1,3},{3,1},{5,7},{7,5},{8,10},{10,8},{12,... | collective-permute-start | bytes 786440 | tf_op jit(solution)/shard_map/ppermute | solution.py:520
  120.9 11.4 %collective-permute-start.26 = (f32[136,512]{1,0:T(8,128)S(1)}, f32[136,512]{1,0:T(8,128)S(1)}, u32[]{:S(2)}, u32[]{:S(2)}) collective-permute-start(f32[136,512]{1,0:T(8,128)S(1)} %get-tuple-element.148.refs_2_), channel_id=1, source_target_pairs={{0,2},{2,0},{4,6},{6,4},{1,3},{3,1},{5,7},{7,5},{8,10},{10,8},{12,... | collective-permute-start | bytes 835592 | tf_op jit(solution)/shard_map/ppermute | solution.py:520
  125.8 7.5 %collective-permute-start.25 = (f32[128,512]{1,0:T(8,128)S(1)}, f32[128,512]{1,0:T(8,128)S(1)}, u32[]{:S(2)}, u32[]{:S(2)}) collective-permute-start(f32[128,512]{1,0:T(8,128)S(1)} %shard_map.192.refs_4_.refs_1_), channel_id=1, source_target_pairs={{0,0},{2,4},{4,2},{6,6},{1,1},{3,5},{5,3},{7,7},{8,8},{10,12},{12,... | collective-permute-start | bytes 786440 | tf_op jit(solution)/shard_map/ppermute | solution.py:523
  126.5 12.2 %collective-permute-start.29 = (f32[128,512]{1,0:T(8,128)S(1)}, f32[128,512]{1,0:T(8,128)S(1)}, u32[]{:S(2)}, u32[]{:S(2)}) collective-permute-start(f32[128,512]{1,0:T(8,128)S(1)} %get-tuple-element.149.refs_2_), channel_id=1, source_target_pairs={{0,2},{2,0},{4,6},{6,4},{1,3},{3,1},{5,7},{7,5},{8,10},{10,8},{12,... | collective-permute-start | bytes 786440 | tf_op jit(solution)/shard_map/ppermute | solution.py:520
  133.4 9.4 %collective-permute-start.28 = (f32[128,512]{1,0:T(8,128)S(1)}, f32[128,512]{1,0:T(8,128)S(1)}, u32[]{:S(2)}, u32[]{:S(2)}) collective-permute-start(f32[128,512]{1,0:T(8,128)S(1)} %get-tuple-element.150.refs_5_), channel_id=1, source_target_pairs={{0,2},{2,0},{4,6},{6,4},{1,3},{3,1},{5,7},{7,5},{8,10},{10,8},{12,... | collective-permute-start | bytes 786440 | tf_op jit(solution)/shard_map/ppermute | solution.py:520
  138.8 9.0 %collective-permute-start.32 = (f32[128,512]{1,0:T(8,128)S(1)}, f32[128,512]{1,0:T(8,128)S(1)}, u32[]{:S(2)}, u32[]{:S(2)}) collective-permute-start(f32[128,512]{1,0:T(8,128)S(1)} %shard_map.197.refs_2_.refs_0_), channel_id=1, source_target_pairs={{0,0},{2,4},{4,2},{6,6},{1,1},{3,5},{5,3},{7,7},{8,8},{10,12},{12,... | collective-permute-start | bytes 786440 | tf_op jit(solution)/shard_map/ppermute | solution.py:523
  142.8 8.8 %collective-permute-start.31 = (f32[128,512]{1,0:T(8,128)S(1)}, f32[128,512]{1,0:T(8,128)S(1)}, u32[]{:S(2)}, u32[]{:S(2)}) collective-permute-start(f32[128,512]{1,0:T(8,128)S(1)} %shard_map.200.refs_2_.refs_0_), channel_id=1, source_target_pairs={{0,0},{2,4},{4,2},{6,6},{1,1},{3,5},{5,3},{7,7},{8,8},{10,12},{12,... | collective-permute-start | bytes 786440 | tf_op jit(solution)/shard_map/ppermute | solution.py:523
  143.4 11.0 %collective-permute-start.35 = (f32[128,512]{1,0:T(8,128)S(1)}, f32[128,512]{1,0:T(8,128)S(1)}, u32[]{:S(2)}, u32[]{:S(2)}) collective-permute-start(f32[128,512]{1,0:T(8,128)S(1)} %shard_map.198.refs_7_.refs_3_), channel_id=1, source_target_pairs={{0,2},{2,0},{4,6},{6,4},{1,3},{3,1},{5,7},{7,5},{8,10},{10,8},{12,... | collective-permute-start | bytes 786440 | tf_op jit(solution)/shard_map/ppermute | solution.py:520
  147.9 11.4 %collective-permute-start.34 = (f32[128,512]{1,0:T(8,128)S(1)}, f32[128,512]{1,0:T(8,128)S(1)}, u32[]{:S(2)}, u32[]{:S(2)}) collective-permute-start(f32[128,512]{1,0:T(8,128)S(1)} %shard_map.201.refs_7_.refs_3_), channel_id=1, source_target_pairs={{0,2},{2,0},{4,6},{6,4},{1,3},{3,1},{5,7},{7,5},{8,10},{10,8},{12,... | collective-permute-start | bytes 786440 | tf_op jit(solution)/shard_map/ppermute | solution.py:520
  151.6 10.5 %collective-permute-start.33 = (f32[128,512]{1,0:T(8,128)S(1)}, f32[128,512]{1,0:T(8,128)S(1)}, u32[]{:S(2)}, u32[]{:S(2)}) collective-permute-start(f32[128,512]{1,0:T(8,128)S(1)} %shard_map.203.refs_7_.refs_3_), channel_id=1, source_target_pairs={{0,2},{2,0},{4,6},{6,4},{1,3},{3,1},{5,7},{7,5},{8,10},{10,8},{12,... | collective-permute-start | bytes 786440 | tf_op jit(solution)/shard_map/ppermute | solution.py:520
  176.7 9.6 %collective-permute-start.41 = (f32[136,512]{1,0:T(8,128)S(1)}, f32[136,512]{1,0:T(8,128)S(1)}, u32[]{:S(2)}, u32[]{:S(2)}) collective-permute-start(f32[136,512]{1,0:T(8,128)S(1)} %shard_map.209.refs_3_.refs_0_), channel_id=1, source_target_pairs={{0,2},{2,0},{4,6},{6,4},{1,3},{3,1},{5,7},{7,5},{8,10},{10,8},{12,... | collective-permute-start | bytes 835592 | tf_op jit(solution)/shard_map/ppermute | solution.py:520
  179.9 12.0 %collective-permute-start.43 = (f32[128,512]{1,0:T(8,128)S(1)}, f32[128,512]{1,0:T(8,128)S(1)}, u32[]{:S(2)}, u32[]{:S(2)}) collective-permute-start(f32[128,512]{1,0:T(8,128)S(1)} %shard_map.214.refs_2_.refs_0_), channel_id=1, source_target_pairs={{0,2},{2,0},{4,6},{6,4},{1,3},{3,1},{5,7},{7,5},{8,10},{10,8},{12,... | collective-permute-start | bytes 786440 | tf_op jit(solution)/shard_map/ppermute | solution.py:520
  187.0 10.5 %collective-permute-start.40 = (f32[128,512]{1,0:T(8,128)S(1)}, f32[128,512]{1,0:T(8,128)S(1)}, u32[]{:S(2)}, u32[]{:S(2)}) collective-permute-start(f32[128,512]{1,0:T(8,128)S(1)} %shard_map.210.refs_3_.refs_0_), channel_id=1, source_target_pairs={{0,2},{2,0},{4,6},{6,4},{1,3},{3,1},{5,7},{7,5},{8,10},{10,8},{12,... | collective-permute-start | bytes 786440 | tf_op jit(solution)/shard_map/ppermute | solution.py:520
  192.6 11.4 %collective-permute-start.45 = (f32[136,512]{1,0:T(8,128)S(1)}, f32[136,512]{1,0:T(8,128)S(1)}, u32[]{:S(2)}, u32[]{:S(2)}) collective-permute-start(f32[136,512]{1,0:T(8,128)S(1)} %get-tuple-element.169.refs_2_), channel_id=1, source_target_pairs={{0,2},{2,0},{4,6},{6,4},{1,3},{3,1},{5,7},{7,5},{8,10},{10,8},{12,... | collective-permute-start | bytes 835592 | tf_op jit(solution)/shard_map/ppermute | solution.py:520
  198.2 12.2 %collective-permute-start.48 = (f32[128,512]{1,0:T(8,128)S(1)}, f32[128,512]{1,0:T(8,128)S(1)}, u32[]{:S(2)}, u32[]{:S(2)}) collective-permute-start(f32[128,512]{1,0:T(8,128)S(1)} %get-tuple-element.170.refs_2_), channel_id=1, source_target_pairs={{0,2},{2,0},{4,6},{6,4},{1,3},{3,1},{5,7},{7,5},{8,10},{10,8},{12,... | collective-permute-start | bytes 786440 | tf_op jit(solution)/shard_map/ppermute | solution.py:520
  204.9 9.5 %collective-permute-start.47 = (f32[128,512]{1,0:T(8,128)S(1)}, f32[128,512]{1,0:T(8,128)S(1)}, u32[]{:S(2)}, u32[]{:S(2)}) collective-permute-start(f32[128,512]{1,0:T(8,128)S(1)} %get-tuple-element.171.refs_5_), channel_id=1, source_target_pairs={{0,2},{2,0},{4,6},{6,4},{1,3},{3,1},{5,7},{7,5},{8,10},{10,8},{12,... | collective-permute-start | bytes 786440 | tf_op jit(solution)/shard_map/ppermute | solution.py:520
  210.5 9.0 %collective-permute-start.51 = (f32[128,512]{1,0:T(8,128)S(1)}, f32[128,512]{1,0:T(8,128)S(1)}, u32[]{:S(2)}, u32[]{:S(2)}) collective-permute-start(f32[128,512]{1,0:T(8,128)S(1)} %shard_map.223.refs_2_.refs_0_), channel_id=1, source_target_pairs={{0,0},{2,4},{4,2},{6,6},{1,1},{3,5},{5,3},{7,7},{8,8},{10,12},{12,... | collective-permute-start | bytes 786440 | tf_op jit(solution)/shard_map/ppermute | solution.py:523
  214.4 8.8 %collective-permute-start.50 = (f32[128,512]{1,0:T(8,128)S(1)}, f32[128,512]{1,0:T(8,128)S(1)}, u32[]{:S(2)}, u32[]{:S(2)}) collective-permute-start(f32[128,512]{1,0:T(8,128)S(1)} %shard_map.226.refs_2_.refs_0_), channel_id=1, source_target_pairs={{0,0},{2,4},{4,2},{6,6},{1,1},{3,5},{5,3},{7,7},{8,8},{10,12},{12,... | collective-permute-start | bytes 786440 | tf_op jit(solution)/shard_map/ppermute | solution.py:523
  215.1 11.0 %collective-permute-start.54 = (f32[128,512]{1,0:T(8,128)S(1)}, f32[128,512]{1,0:T(8,128)S(1)}, u32[]{:S(2)}, u32[]{:S(2)}) collective-permute-start(f32[128,512]{1,0:T(8,128)S(1)} %shard_map.224.refs_7_.refs_3_), channel_id=1, source_target_pairs={{0,2},{2,0},{4,6},{6,4},{1,3},{3,1},{5,7},{7,5},{8,10},{10,8},{12,... | collective-permute-start | bytes 786440 | tf_op jit(solution)/shard_map/ppermute | solution.py:520
  219.5 11.4 %collective-permute-start.53 = (f32[128,512]{1,0:T(8,128)S(1)}, f32[128,512]{1,0:T(8,128)S(1)}, u32[]{:S(2)}, u32[]{:S(2)}) collective-permute-start(f32[128,512]{1,0:T(8,128)S(1)} %shard_map.227.refs_7_.refs_3_), channel_id=1, source_target_pairs={{0,2},{2,0},{4,6},{6,4},{1,3},{3,1},{5,7},{7,5},{8,10},{10,8},{12,... | collective-permute-start | bytes 786440 | tf_op jit(solution)/shard_map/ppermute | solution.py:520
  223.3 10.5 %collective-permute-start.52 = (f32[128,512]{1,0:T(8,128)S(1)}, f32[128,512]{1,0:T(8,128)S(1)}, u32[]{:S(2)}, u32[]{:S(2)}) collective-permute-start(f32[128,512]{1,0:T(8,128)S(1)} %shard_map.229.refs_7_.refs_3_), channel_id=1, source_target_pairs={{0,2},{2,0},{4,6},{6,4},{1,3},{3,1},{5,7},{7,5},{8,10},{10,8},{12,... | collective-permute-start | bytes 786440 | tf_op jit(solution)/shard_map/ppermute | solution.py:520
  248.4 9.6 %collective-permute-start.60 = (f32[136,512]{1,0:T(8,128)S(1)}, f32[136,512]{1,0:T(8,128)S(1)}, u32[]{:S(2)}, u32[]{:S(2)}) collective-permute-start(f32[136,512]{1,0:T(8,128)S(1)} %shard_map.235.refs_3_.refs_0_), channel_id=1, source_target_pairs={{0,2},{2,0},{4,6},{6,4},{1,3},{3,1},{5,7},{7,5},{8,10},{10,8},{12,... | collective-permute-start | bytes 835592 | tf_op jit(solution)/shard_map/ppermute | solution.py:520
  251.7 12.0 %collective-permute-start.62 = (f32[128,512]{1,0:T(8,128)S(1)}, f32[128,512]{1,0:T(8,128)S(1)}, u32[]{:S(2)}, u32[]{:S(2)}) collective-permute-start(f32[128,512]{1,0:T(8,128)S(1)} %shard_map.240.refs_2_.refs_0_), channel_id=1, source_target_pairs={{0,2},{2,0},{4,6},{6,4},{1,3},{3,1},{5,7},{7,5},{8,10},{10,8},{12,... | collective-permute-start | bytes 786440 | tf_op jit(solution)/shard_map/ppermute | solution.py:520
  258.7 10.5 %collective-permute-start.59 = (f32[128,512]{1,0:T(8,128)S(1)}, f32[128,512]{1,0:T(8,128)S(1)}, u32[]{:S(2)}, u32[]{:S(2)}) collective-permute-start(f32[128,512]{1,0:T(8,128)S(1)} %shard_map.236.refs_3_.refs_0_), channel_id=1, source_target_pairs={{0,2},{2,0},{4,6},{6,4},{1,3},{3,1},{5,7},{7,5},{8,10},{10,8},{12,... | collective-permute-start | bytes 786440 | tf_op jit(solution)/shard_map/ppermute | solution.py:520
  264.4 11.4 %collective-permute-start.64 = (f32[136,512]{1,0:T(8,128)S(1)}, f32[136,512]{1,0:T(8,128)S(1)}, u32[]{:S(2)}, u32[]{:S(2)}) collective-permute-start(f32[136,512]{1,0:T(8,128)S(1)} %get-tuple-element.194.refs_2_), channel_id=1, source_target_pairs={{0,2},{2,0},{4,6},{6,4},{1,3},{3,1},{5,7},{7,5},{8,10},{10,8},{12,... | collective-permute-start | bytes 835592 | tf_op jit(solution)/shard_map/ppermute | solution.py:520
  269.3 7.3 %collective-permute-start.63 = (f32[128,512]{1,0:T(8,128)S(1)}, f32[128,512]{1,0:T(8,128)S(1)}, u32[]{:S(2)}, u32[]{:S(2)}) collective-permute-start(f32[128,512]{1,0:T(8,128)S(1)} %shard_map.244.refs_4_.refs_1_), channel_id=1, source_target_pairs={{0,0},{2,4},{4,2},{6,6},{1,1},{3,5},{5,3},{7,7},{8,8},{10,12},{12,... | collective-permute-start | bytes 786440 | tf_op jit(solution)/shard_map/ppermute | solution.py:523
  270.0 12.2 %collective-permute-start.67 = (f32[128,512]{1,0:T(8,128)S(1)}, f32[128,512]{1,0:T(8,128)S(1)}, u32[]{:S(2)}, u32[]{:S(2)}) collective-permute-start(f32[128,512]{1,0:T(8,128)S(1)} %get-tuple-element.195.refs_2_), channel_id=1, source_target_pairs={{0,2},{2,0},{4,6},{6,4},{1,3},{3,1},{5,7},{7,5},{8,10},{10,8},{12,... | collective-permute-start | bytes 786440 | tf_op jit(solution)/shard_map/ppermute | solution.py:520
  276.6 9.5 %collective-permute-start.66 = (f32[128,512]{1,0:T(8,128)S(1)}, f32[128,512]{1,0:T(8,128)S(1)}, u32[]{:S(2)}, u32[]{:S(2)}) collective-permute-start(f32[128,512]{1,0:T(8,128)S(1)} %get-tuple-element.196.refs_5_), channel_id=1, source_target_pairs={{0,2},{2,0},{4,6},{6,4},{1,3},{3,1},{5,7},{7,5},{8,10},{10,8},{12,... | collective-permute-start | bytes 786440 | tf_op jit(solution)/shard_map/ppermute | solution.py:520
  282.3 9.0 %collective-permute-start.70 = (f32[128,512]{1,0:T(8,128)S(1)}, f32[128,512]{1,0:T(8,128)S(1)}, u32[]{:S(2)}, u32[]{:S(2)}) collective-permute-start(f32[128,512]{1,0:T(8,128)S(1)} %shard_map.249.refs_2_.refs_0_), channel_id=1, source_target_pairs={{0,0},{2,4},{4,2},{6,6},{1,1},{3,5},{5,3},{7,7},{8,8},{10,12},{12,... | collective-permute-start | bytes 786440 | tf_op jit(solution)/shard_map/ppermute | solution.py:523
  286.2 8.8 %collective-permute-start.69 = (f32[128,512]{1,0:T(8,128)S(1)}, f32[128,512]{1,0:T(8,128)S(1)}, u32[]{:S(2)}, u32[]{:S(2)}) collective-permute-start(f32[128,512]{1,0:T(8,128)S(1)} %shard_map.252.refs_2_.refs_0_), channel_id=1, source_target_pairs={{0,0},{2,4},{4,2},{6,6},{1,1},{3,5},{5,3},{7,7},{8,8},{10,12},{12,... | collective-permute-start | bytes 786440 | tf_op jit(solution)/shard_map/ppermute | solution.py:523
  286.9 11.0 %collective-permute-start.73 = (f32[128,512]{1,0:T(8,128)S(1)}, f32[128,512]{1,0:T(8,128)S(1)}, u32[]{:S(2)}, u32[]{:S(2)}) collective-permute-start(f32[128,512]{1,0:T(8,128)S(1)} %shard_map.250.refs_7_.refs_3_), channel_id=1, source_target_pairs={{0,2},{2,0},{4,6},{6,4},{1,3},{3,1},{5,7},{7,5},{8,10},{10,8},{12,... | collective-permute-start | bytes 786440 | tf_op jit(solution)/shard_map/ppermute | solution.py:520
  291.3 11.4 %collective-permute-start.72 = (f32[128,512]{1,0:T(8,128)S(1)}, f32[128,512]{1,0:T(8,128)S(1)}, u32[]{:S(2)}, u32[]{:S(2)}) collective-permute-start(f32[128,512]{1,0:T(8,128)S(1)} %shard_map.253.refs_7_.refs_3_), channel_id=1, source_target_pairs={{0,2},{2,0},{4,6},{6,4},{1,3},{3,1},{5,7},{7,5},{8,10},{10,8},{12,... | collective-permute-start | bytes 786440 | tf_op jit(solution)/shard_map/ppermute | solution.py:520
  295.1 10.5 %collective-permute-start.71 = (f32[128,512]{1,0:T(8,128)S(1)}, f32[128,512]{1,0:T(8,128)S(1)}, u32[]{:S(2)}, u32[]{:S(2)}) collective-permute-start(f32[128,512]{1,0:T(8,128)S(1)} %shard_map.255.refs_7_.refs_3_), channel_id=1, source_target_pairs={{0,2},{2,0},{4,6},{6,4},{1,3},{3,1},{5,7},{7,5},{8,10},{10,8},{12,... | collective-permute-start | bytes 786440 | tf_op jit(solution)/shard_map/ppermute | solution.py:520
  (46 other events, 189.0 us)
